TPU v7x, 32 devices: a whole 2x2x4 slice. The times are simulated.
32 devices in a mesh: depth: 2 (over y), row: 4 (over x, core), col: 4 (over z).
Axes of the slice: x: 2, y: 2, z: 4, core: 2. Of those that a mesh axis runs over, the one named last changes fastest.
Arguments:
- state: float32 [4, 32, 64, 512], P(None, 'depth', 'row', 'col'), may hold values from 0 to 1
- velocity: float32 [3, 32, 64, 512], P(None, 'depth', 'row', 'col'), may hold values from -3 to 3
- view_order: int32 [4, 4], P('row', 'col'), may hold values from 0 to 1
- tf_table: int32 [4, 256], replicated, may hold values from 0 to 255
Outputs:
- new_state: float32 [4, 32, 64, 512], P(None, 'depth', 'row', 'col')
- image: float32 [4, 256, 256], P(None, 'row', 'col')
Inputs may be any that keep to these rules, and one draw needn't show every extreme that they name: `view_order`: 0 puts the lowest depth indices in front, 1 the highest. `tf_table`: levels in units of 1/255.
All inputs are finite; a program needn't handle non-finite values.
Results may differ from a plain program's by a relative error of at most 0.0003.
Values sent between devices are 32-bit elements; how exact they have to be, the bound alone decides.
No kernel may reach another device: no remote copies, remote signals or barrier semaphores. Data moves between devices by JAX's collectives and lax.ppermute only.
A program may use at most 128 MiB of HBM per device.

v0:
```python
import jax
import jax.numpy as jnp
import numpy as np
from jax import lax
from jax.sharding import PartitionSpec as P

PIX_R = 64
PIX_C = 64


FIRST_COEF = (0.8, -0.2, 4.0 / 105.0, -1.0 / 280.0)
SECOND_COEF = (1.6, -0.2, 8.0 / 315.0, -1.0 / 560.0)
CENTER_COEF = -205.0 / 72.0
DIFFUSIVITY = (0.05, 0.04, 0.03, 0.08)
TIME_STEP = 0.2
RATE_CONST = 2.0
IGNITION_SLOPE = 8.0
IGNITION_TEMP = 0.5
OXIDIZER_RATIO = 1.5
HEAT_RELEASE = 0.8
SHEAR_CELLS = 2.0
OPACITY_TOTAL = 6.0


def extended(block, sides, width):
    for axis, dim in sides:
        count = lax.axis_size(axis)
        forward = [(i, i + 1) for i in range(count - 1)]
        forward.append((count - 1, 0))
        backward = [(target, source) for source, target in forward]
        low = lax.ppermute(
            lax.slice_in_dim(block, block.shape[dim] - width, None, axis=dim), axis, forward
        )
        high = lax.ppermute(lax.slice_in_dim(block, 0, width, axis=dim), axis, backward)
        block = jnp.concatenate([low, block, high], axis=dim)
    return block


def partner(value, axis, distance):
    mask = 2**distance
    pairs = [(source, source ^ mask) for source in range(lax.axis_size(axis))]
    return lax.ppermute(value, axis, pairs)


def source_terms(centre):
    rate = (
        RATE_CONST
        * centre[0]
        * centre[1]
        * jax.nn.sigmoid(IGNITION_SLOPE * (centre[3] - IGNITION_TEMP))
    )
    return jnp.stack(
        [-rate, -OXIDIZER_RATIO * rate, (1.0 + OXIDIZER_RATIO) * rate, HEAT_RELEASE * rate]
    )


def combine_terms(centre, gradients, laplace, velocity):
    advect = (
        velocity[0][None] * gradients[0]
        + velocity[1][None] * gradients[1]
        + velocity[2][None] * gradients[2]
    )
    diffusion = jnp.stack(
        [DIFFUSIVITY[field_index] * laplace[field_index] for field_index in range(4)]
    )
    return diffusion - advect + source_terms(centre)


def tendency(padded, velocity):
    depth_cells = padded.shape[1] - 8
    row_cells = padded.shape[2] - 8
    column_cells = padded.shape[3] - 8

    def window(shifts):
        begin = (0, 4 + shifts[0], 4 + shifts[1], 4 + shifts[2])
        finish = (
            padded.shape[0],
            begin[1] + depth_cells,
            begin[2] + row_cells,
            begin[3] + column_cells,
        )
        return lax.slice(padded, begin, finish)

    centre = window((0, 0, 0))
    laplace = 3.0 * CENTER_COEF * centre
    gradients = []
    for spatial in range(3):
        gradient = jnp.zeros_like(centre)
        for offset in range(4):
            ahead_shift = tuple(
                (offset + 1 if dimension == spatial else 0 for dimension in range(3))
            )
            behind_shift = tuple(
                (-(offset + 1) if dimension == spatial else 0 for dimension in range(3))
            )
            forward = window(ahead_shift)
            backward = window(behind_shift)
            gradient = gradient + FIRST_COEF[offset] * (forward - backward)
            laplace = laplace + SECOND_COEF[offset] * (forward + backward)
        gradients.append(gradient)
    return combine_terms(centre, gradients, laplace, velocity)


def section_padding(fields):
    return extended(fields, (("depth", 1), ("row", 2), ("col", 3)), 4)


def row_matrix(first_slice, slice_count, slice_total, cell_count, pixels):
    stride = cell_count / pixels
    spread = max(1.0, stride)
    centres = (jnp.arange(pixels, dtype=jnp.float32) + 0.5) * stride - 0.5
    global_slices = (first_slice + jnp.arange(slice_count, dtype=jnp.int32)).astype(jnp.float32)
    shifts = SHEAR_CELLS * ((global_slices + 0.5) / slice_total - 0.5)
    places = jnp.clip(centres[None, :] + shifts[:, None], 0.0, cell_count - 1.0)
    cells_at = jnp.arange(cell_count, dtype=jnp.float32)
    return (
        jnp.maximum(0.0, 1.0 - jnp.abs(places[:, :, None] - cells_at[None, None, :]) / spread)
        / spread
    )


def column_matrix(cell_count, pixels):
    stride = cell_count / pixels
    spread = max(1.0, stride)
    centres = jnp.clip(
        (jnp.arange(pixels, dtype=jnp.float32) + 0.5) * stride - 0.5, 0.0, cell_count - 1.0
    )
    cells_at = jnp.arange(cell_count, dtype=jnp.float32)
    return jnp.maximum(0.0, 1.0 - jnp.abs(centres[None, :] - cells_at[:, None]) / spread) / spread


def shade(values, table_values, slice_total):
    levels = table_values.shape[1]
    level = jnp.clip(values, 0.0, 1.0) * (levels - 1.0)
    marks = jnp.arange(levels, dtype=jnp.float32)
    weights = jnp.maximum(0.0, 1.0 - jnp.abs(level[None, :] - marks[:, None]))
    raw_colour = jnp.dot(
        table_values, weights, preferred_element_type=jnp.float32, precision=lax.Precision.HIGHEST
    ) * (1.0 / 255.0)
    opacity = OPACITY_TOTAL / slice_total * raw_colour[3]
    return jnp.concatenate([opacity[None, :] * raw_colour[:3], opacity[None, :]], 0)


def march_slices(sampled, table_values, order_flag, slice_total):
    slice_count = sampled.shape[0]

    def advance(running, position):
        accumulated, transmit = running
        chosen = jnp.where(order_flag == 0, position, slice_count - 1 - position)
        values = lax.dynamic_index_in_dim(sampled, chosen, 0, keepdims=False)
        colour = shade(values, table_values, slice_total)
        return ((accumulated + transmit[None, :] * colour, transmit * (1.0 - colour[3])), None)

    start = (
        jnp.zeros((4, sampled.shape[1]), jnp.float32),
        jnp.ones((sampled.shape[1],), jnp.float32),
    )
    finished, unused = lax.scan(advance, start, jnp.arange(slice_count, dtype=jnp.int32))
    return finished[0]


def composite_over(front_part, back_part):
    return front_part + (1.0 - front_part[3:4]) * back_part


def reversed_bits(count, bit_total):
    result = []
    for position in range(count):
        flipped = 0
        for bit_number in range(bit_total):
            if position >> bit_number & 1:
                flipped = flipped | 1 << bit_total - 1 - bit_number
        result.append(flipped)
    return np.array(result, dtype=np.int32)


def local(state, velocity, view_order, tf_table):
    first_rate = tendency(section_padding(state), velocity)
    middle = state + TIME_STEP * first_rate
    second_rate = tendency(section_padding(middle), velocity)
    new_state = state + 0.5 * TIME_STEP * (first_rate + second_rate)
    slice_count = state.shape[1]
    depth_index = lax.axis_index("depth")
    depth_count = lax.axis_size("depth")
    bit_total = depth_count.bit_length() - 1
    slice_total = slice_count * depth_count
    order_flag = view_order[0, 0]
    row_weights = row_matrix(
        depth_index * slice_count, slice_count, slice_total, state.shape[2], PIX_R
    )
    column_weights = column_matrix(state.shape[3], PIX_C)
    partial_rows = jnp.einsum(
        "dpr,drc->dpc", row_weights, new_state[3], precision=lax.Precision.HIGHEST
    )
    sampled = jnp.einsum(
        "dpc,cq->dpq", partial_rows, column_weights, precision=lax.Precision.HIGHEST
    )
    sampled = sampled.reshape(slice_count, PIX_R * PIX_C)
    table_values = tf_table.astype(jnp.float32)
    brick_tile = march_slices(sampled, table_values, order_flag, slice_total)
    piece_order = np.arange(depth_count, dtype=np.int32)
    portion = brick_tile
    for bit_number in range(bit_total):
        half_width = portion.shape[1] // 2
        lower_half = portion[:, :half_width]
        upper_half = portion[:, half_width:]
        own_bit = depth_index // 2**bit_number % 2
        kept_half = jnp.where(own_bit == 0, lower_half, upper_half)
        sent_half = jnp.where(own_bit == 0, upper_half, lower_half)
        received = partner(sent_half, "depth", bit_number)
        in_front = own_bit == order_flag
        portion = jnp.where(
            in_front, composite_over(kept_half, received), composite_over(received, kept_half)
        )
    piece_order = reversed_bits(depth_count, bit_total)
    whole_tile = lax.all_gather(portion, "depth", axis=1, tiled=True)
    piece_width = portion.shape[1]
    pieces = whole_tile.reshape(4, depth_count, piece_width)
    placed = pieces[:, np.argsort(piece_order), :]
    return (new_state, placed.reshape(4, PIX_R, PIX_C))


def solution(mesh):
    in_specs = (
        P(None, "depth", "row", "col"),
        P(None, "depth", "row", "col"),
        P("row", "col"),
        P(),
    )
    out_specs = (P(None, "depth", "row", "col"), P(None, "row", "col"))
    return jax.shard_map(local, mesh=mesh, in_specs=in_specs, out_specs=out_specs, check_vma=False)
```

profile of v0, /device:TPU:0, one launch (start us, length us, event | category | flops | bytes accessed | tf_op | source)
XLA Modules:
  0.0 187.5 jit_solution(8019899837008678539)
XLA Ops:
  1.7 3.0 %collective-permute-start.1 = (f32[4,4,16,128]{3,2,1,0:T(8,128)S(1)}, f32[4,4,16,128]{3,2,1,0:T(8,128)S(1)}, u32[]{:S(2)}, u32[]{:S(2)}) collective-permute-start(f32[4,4,16,128]{3,2,1,0:T(8,128)S(1)} %get-tuple-element.158), channel_id=1, source_target_pairs={{0,16},{16,0},{1,17},{17,1},{2,18},{18,2},{3,19},{19,3},{4,20},{20... | collective-permute-start | bytes 393224 | tf_op jit(solution)/shard_map/ppermute | solution.py:31
  12.4 3.5 %collective-permute-done.2 = f32[4,24,4,128]{3,2,1,0:T(4,128)S(1)} collective-permute-done((f32[4,24,4,128]{3,2,1,0:T(4,128)S(1)}, f32[4,24,4,128]{3,2,1,0:T(4,128)S(1)}, u32[]{:S(2)}, u32[]{:S(2)}) %collective-permute-start.2) | collective-permute-done | bytes 196640 | tf_op jit(solution)/shard_map/ppermute | solution.py:34
  15.8 2.8 %collective-permute-done.3 = f32[4,24,4,128]{3,2,1,0:T(4,128)S(1)} collective-permute-done((f32[4,24,4,128]{3,2,1,0:T(4,128)S(1)}, f32[4,24,4,128]{3,2,1,0:T(4,128)S(1)}, u32[]{:S(2)}, u32[]{:S(2)}) %collective-permute-start.3) | collective-permute-done | bytes 196640 | tf_op jit(solution)/shard_map/ppermute | solution.py:31
  22.9 3.7 %collective-permute-start.4 = (f32[4,24,24,4]{2,1,3,0:T(8,128)S(1)}, f32[4,24,24,4]{2,1,3,0:T(8,128)}, u32[]{:S(2)}, u32[]{:S(2)}) collective-permute-start(f32[4,24,24,4]{2,1,3,0:T(8,128)S(1)} %copy.9), channel_id=1, source_target_pairs={{1,0},{2,1},{3,2},{0,3},{5,4},{6,5},{7,6},{4,7},{9,8},{10,9},{11,1... | collective-permute-start | bytes 110600 | tf_op jit(solution)/shard_map/ppermute | solution.py:34
  33.4 3.7 %collective-permute-done.5 = f32[4,24,24,4]{2,1,3,0:T(8,128)S(1)} collective-permute-done((f32[4,24,24,4]{2,1,3,0:T(8,128)}, f32[4,24,24,4]{2,1,3,0:T(8,128)S(1)}, u32[]{:S(2)}, u32[]{:S(2)}) %collective-permute-start.5) | collective-permute-done | bytes 36896 | tf_op jit(solution)/shard_map/ppermute | solution.py:31
  38.9 8.4 %multiply_add_fusion.2 = f32[4,16,16,128]{3,2,1,0:T(8,128)S(1)} fusion(f32[4,16,16,128]{3,2,1,0:T(8,128)S(1)} %copy-done, f32[4,20,16,128]{3,2,1,0:T(8,128)S(1)} %get-tuple-element.156, f32[4,20,16,128]{3,2,1,0:T(8,128)S(1)} %get-tuple-element.165, f32[4,24,4,128]{3,2,1,0:T(4,128)} %copy-done.14, f32[4,24,16,128]{3,2,1,0:T(8,128)} %copy-done.4, ...), kind=kLoop, calls=%fused_computation.101 | loop fusion | flops 9043968 | bytes 6496256 | tf_op jit(solution)/shard_map/add | solution.py:99
  48.5 4.3 %multiply_add_fusion.1 = (f32[4,16,16,128]{3,2,1,0:T(8,128)S(1)}, f32[4,16,16,128]{3,2,1,0:T(8,128)}) fusion(f32[4,16,16,128]{3,2,1,0:T(8,128)S(1)} %copy-done, f32[1,16,16,128]{3,2,1,0:T(8,128)S(1)} %copy-done.29, f32[1,16,16,128]{3,2,1,0:T(8,128)S(1)} %copy-done.28, f32[1,16,16,128]{3,2,1,0:T(8,128)S(1)} %copy-done.27, ...), kind=kLoop, calls=%fused_computation.100 | loop fusion | flops 10485760 | bytes 8462336 | tf_op jit(solution)/shard_map/add | solution.py:179
  55.6 3.7 %collective-permute-done.6 = f32[4,4,16,128]{3,2,1,0:T(8,128)S(1)} collective-permute-done((f32[4,4,16,128]{3,2,1,0:T(8,128)S(1)}, f32[4,4,16,128]{3,2,1,0:T(8,128)S(1)}, u32[]{:S(2)}, u32[]{:S(2)}) %collective-permute-start.6) | collective-permute-done | bytes 131104 | tf_op jit(solution)/shard_map/ppermute | solution.py:34
  62.2 3.9 %collective-permute-done.8 = f32[4,24,4,128]{3,2,1,0:T(4,128)S(1)} collective-permute-done((f32[4,24,4,128]{3,2,1,0:T(4,128)S(1)}, f32[4,24,4,128]{3,2,1,0:T(4,128)S(1)}, u32[]{:S(2)}, u32[]{:S(2)}) %collective-permute-start.8) | collective-permute-done | bytes 196640 | tf_op jit(solution)/shard_map/ppermute | solution.py:34
  69.7 3.3 %collective-permute-start.10 = (f32[4,24,24,4]{2,1,3,0:T(8,128)}, f32[4,24,24,4]{2,1,3,0:T(8,128)}, u32[]{:S(2)}, u32[]{:S(2)}) collective-permute-start(f32[4,24,24,4]{2,1,3,0:T(8,128)} %copy.13), channel_id=1, source_target_pairs={{1,0},{2,1},{3,2},{0,3},{5,4},{6,5},{7,6},{4,7},{9,8},{10,9},{11,1... | collective-permute-start | bytes 110600 | tf_op jit(solution)/shard_map/ppermute | solution.py:34
  75.7 2.9 %collective-permute-done.10 = f32[4,24,24,4]{2,1,3,0:T(8,128)} collective-permute-done((f32[4,24,24,4]{2,1,3,0:T(8,128)}, f32[4,24,24,4]{2,1,3,0:T(8,128)}, u32[]{:S(2)}, u32[]{:S(2)}) %collective-permute-start.10) | collective-permute-done | bytes 36896 | tf_op jit(solution)/shard_map/ppermute | solution.py:34
  78.6 2.6 %copy.14 = f32[4,24,24,4]{3,2,1,0:T(8,128)} copy(f32[4,24,24,4]{2,1,3,0:T(8,128)} %collective-permute-done.10) | data formatting | bytes 73728 | tf_op jit(solution)/shard_map/ppermute | solution.py:34
  85.6 5.9 %multiply_add_fusion = f32[4,16,16,128]{3,2,1,0:T(8,128)S(1)} fusion(f32[4,16,16,128]{3,2,1,0:T(8,128)S(1)} %get-tuple-element.128, f32[4,24,20,128]{3,2,1,0:T(8,128)S(1)} %get-tuple-element.139, f32[4,24,20,128]{3,2,1,0:T(8,128)S(1)} %get-tuple-element.138, f32[4,4,16,128]{3,2,1,0:T(8,128)S(1)} %collective-permute-done.6, f32[4,4,16,128]{3,2,1,0:T(8,128)} %copy-done.6, ...), kind=kLoop, calls=%fused_computation.99 | loop fusion | flops 11141120 | bytes 5971968 | tf_op jit(solution)/shard_map/add | solution.py:99
  92.7 3.6 %fusion.28 = f32[4,16,16,128]{3,2,1,0:T(8,128)S(1)} fusion(f32[4,16,16,128]{3,2,1,0:T(8,128)S(1)} %copy-done, f32[4,16,16,128]{3,2,1,0:T(8,128)S(1)} %copy-done.13, f32[1,16,16,128]{3,2,1,0:T(8,128)S(1)} %get-tuple-element.145, f32[1,16,16,128]{3,2,1,0:T(8,128)S(1)} %get-tuple-element.146, f32[1,16,16,128]{3,2,1,0:T(8,128)S(1)} %get-tuple-element.147, ...), kind=kLoop, calls=%fused_computation.98 | loop fusion | flops 12713984 | bytes 8462336 | tf_op jit(solution)/shard_map/add | solution.py:181
  99.0 78.2 %while.15 = (s32[]{:T(128)}, f32[4,4096]{1,0:T(4,128)S(1)}, f32[4096]{0:T(1024)S(1)}, s32[16]{0:T(128)S(1)}, pred[]{:T(512)}, /*index=5*/f32[16,4096]{1,0:T(8,12...) while((s32[]{:T(128)}, f32[4,4096]{1,0:T(4,128)S(1)}, ...), condition=%wide.region_1.2_spmd.clone, body=%wide.region_0.1_spmd.clone.sunk | while | flops 54644744 | bytes 561347 | solution.py:158
  101.0 2.8 %fusion.81 = f32[4,4096]{1,0:T(4,128)S(1)} fusion(f32[4,256]{1,0:T(4,128)S(1)} %get-tuple-element.253, f32[4096]{0:T(1024)S(1)} %bitcast.41), kind=kOutput, calls=%fused_computation.2.clone.1 | convolution fusion | flops 54542336 | bytes 86016 | tf_op jit(solution)/shard_map/while/body/eval_jaxpr/dot_general | solution.py:137
  105.9 2.8 %fusion.81 = f32[4,4096]{1,0:T(4,128)S(1)} fusion(f32[4,256]{1,0:T(4,128)S(1)} %get-tuple-element.253, f32[4096]{0:T(1024)S(1)} %bitcast.41), kind=kOutput, calls=%fused_computation.2.clone.1 | convolution fusion | flops 54542336 | bytes 86016 | tf_op jit(solution)/shard_map/while/body/eval_jaxpr/dot_general | solution.py:137
  110.8 2.8 %fusion.81 = f32[4,4096]{1,0:T(4,128)S(1)} fusion(f32[4,256]{1,0:T(4,128)S(1)} %get-tuple-element.253, f32[4096]{0:T(1024)S(1)} %bitcast.41), kind=kOutput, calls=%fused_computation.2.clone.1 | convolution fusion | flops 54542336 | bytes 86016 | tf_op jit(solution)/shard_map/while/body/eval_jaxpr/dot_general | solution.py:137
  115.6 2.8 %fusion.81 = f32[4,4096]{1,0:T(4,128)S(1)} fusion(f32[4,256]{1,0:T(4,128)S(1)} %get-tuple-element.253, f32[4096]{0:T(1024)S(1)} %bitcast.41), kind=kOutput, calls=%fused_computation.2.clone.1 | convolution fusion | flops 54542336 | bytes 86016 | tf_op jit(solution)/shard_map/while/body/eval_jaxpr/dot_general | solution.py:137
  120.5 2.8 %fusion.81 = f32[4,4096]{1,0:T(4,128)S(1)} fusion(f32[4,256]{1,0:T(4,128)S(1)} %get-tuple-element.253, f32[4096]{0:T(1024)S(1)} %bitcast.41), kind=kOutput, calls=%fused_computation.2.clone.1 | convolution fusion | flops 54542336 | bytes 86016 | tf_op jit(solution)/shard_map/while/body/eval_jaxpr/dot_general | solution.py:137
  125.4 2.8 %fusion.81 = f32[4,4096]{1,0:T(4,128)S(1)} fusion(f32[4,256]{1,0:T(4,128)S(1)} %get-tuple-element.253, f32[4096]{0:T(1024)S(1)} %bitcast.41), kind=kOutput, calls=%fused_computation.2.clone.1 | convolution fusion | flops 54542336 | bytes 86016 | tf_op jit(solution)/shard_map/while/body/eval_jaxpr/dot_general | solution.py:137
  130.3 2.8 %fusion.81 = f32[4,4096]{1,0:T(4,128)S(1)} fusion(f32[4,256]{1,0:T(4,128)S(1)} %get-tuple-element.253, f32[4096]{0:T(1024)S(1)} %bitcast.41), kind=kOutput, calls=%fused_computation.2.clone.1 | convolution fusion | flops 54542336 | bytes 86016 | tf_op jit(solution)/shard_map/while/body/eval_jaxpr/dot_general | solution.py:137
  135.2 2.8 %fusion.81 = f32[4,4096]{1,0:T(4,128)S(1)} fusion(f32[4,256]{1,0:T(4,128)S(1)} %get-tuple-element.253, f32[4096]{0:T(1024)S(1)} %bitcast.41), kind=kOutput, calls=%fused_computation.2.clone.1 | convolution fusion | flops 54542336 | bytes 86016 | tf_op jit(solution)/shard_map/while/body/eval_jaxpr/dot_general | solution.py:137
  140.1 2.8 %fusion.81 = f32[4,4096]{1,0:T(4,128)S(1)} fusion(f32[4,256]{1,0:T(4,128)S(1)} %get-tuple-element.253, f32[4096]{0:T(1024)S(1)} %bitcast.41), kind=kOutput, calls=%fused_computation.2.clone.1 | convolution fusion | flops 54542336 | bytes 86016 | tf_op jit(solution)/shard_map/while/body/eval_jaxpr/dot_general | solution.py:137
  145.0 2.8 %fusion.81 = f32[4,4096]{1,0:T(4,128)S(1)} fusion(f32[4,256]{1,0:T(4,128)S(1)} %get-tuple-element.253, f32[4096]{0:T(1024)S(1)} %bitcast.41), kind=kOutput, calls=%fused_computation.2.clone.1 | convolution fusion | flops 54542336 | bytes 86016 | tf_op jit(solution)/shard_map/while/body/eval_jaxpr/dot_general | solution.py:137
  149.9 2.8 %fusion.81 = f32[4,4096]{1,0:T(4,128)S(1)} fusion(f32[4,256]{1,0:T(4,128)S(1)} %get-tuple-element.253, f32[4096]{0:T(1024)S(1)} %bitcast.41), kind=kOutput, calls=%fused_computation.2.clone.1 | convolution fusion | flops 54542336 | bytes 86016 | tf_op jit(solution)/shard_map/while/body/eval_jaxpr/dot_general | solution.py:137
  154.7 2.8 %fusion.81 = f32[4,4096]{1,0:T(4,128)S(1)} fusion(f32[4,256]{1,0:T(4,128)S(1)} %get-tuple-element.253, f32[4096]{0:T(1024)S(1)} %bitcast.41), kind=kOutput, calls=%fused_computation.2.clone.1 | convolution fusion | flops 54542336 | bytes 86016 | tf_op jit(solution)/shard_map/while/body/eval_jaxpr/dot_general | solution.py:137
  159.6 2.8 %fusion.81 = f32[4,4096]{1,0:T(4,128)S(1)} fusion(f32[4,256]{1,0:T(4,128)S(1)} %get-tuple-element.253, f32[4096]{0:T(1024)S(1)} %bitcast.41), kind=kOutput, calls=%fused_computation.2.clone.1 | convolution fusion | flops 54542336 | bytes 86016 | tf_op jit(solution)/shard_map/while/body/eval_jaxpr/dot_general | solution.py:137
  164.5 2.8 %fusion.81 = f32[4,4096]{1,0:T(4,128)S(1)} fusion(f32[4,256]{1,0:T(4,128)S(1)} %get-tuple-element.253, f32[4096]{0:T(1024)S(1)} %bitcast.41), kind=kOutput, calls=%fused_computation.2.clone.1 | convolution fusion | flops 54542336 | bytes 86016 | tf_op jit(solution)/shard_map/while/body/eval_jaxpr/dot_general | solution.py:137
  169.4 2.8 %fusion.81 = f32[4,4096]{1,0:T(4,128)S(1)} fusion(f32[4,256]{1,0:T(4,128)S(1)} %get-tuple-element.253, f32[4096]{0:T(1024)S(1)} %bitcast.41), kind=kOutput, calls=%fused_computation.2.clone.1 | convolution fusion | flops 54542336 | bytes 86016 | tf_op jit(solution)/shard_map/while/body/eval_jaxpr/dot_general | solution.py:137
  174.3 2.8 %fusion.81 = f32[4,4096]{1,0:T(4,128)S(1)} fusion(f32[4,256]{1,0:T(4,128)S(1)} %get-tuple-element.253, f32[4096]{0:T(1024)S(1)} %bitcast.41), kind=kOutput, calls=%fused_computation.2.clone.1 | convolution fusion | flops 54542336 | bytes 86016 | tf_op jit(solution)/shard_map/while/body/eval_jaxpr/dot_general | solution.py:137
  181.3 4.6 %all_gather.3 = f32[4,4096]{1,0:T(4,128)S(1)} all-gather(f32[4,2048]{1,0:T(4,128)S(1)} %add_select_fusion), channel_id=1, replica_groups=mesh['depth'=2,'row'=4,'col'=4] {'depth'}, dimensions={1}, use_global_device_ids=true | all-gather | bytes 98304 | tf_op jit(solution)/shard_map/all_gather | solution.py:216
  (235 shorter events, 59.6 us)
Async XLA Ops:
  0.6 6.7 %copy-start.33 = (f32[3,16,16,128]{3,2,1,0:T(8,128)S(1)}, f32[3,16,16,128]{3,2,1,0:T(8,128)}, u32[]{:S(2)}) copy-start(f32[3,16,16,128]{3,2,1,0:T(8,128)} %param.9) | copy-start | bytes 1179652
  1.7 7.4 %collective-permute-start.1 = (f32[4,4,16,128]{3,2,1,0:T(8,128)S(1)}, f32[4,4,16,128]{3,2,1,0:T(8,128)S(1)}, u32[]{:S(2)}, u32[]{:S(2)}) collective-permute-start(f32[4,4,16,128]{3,2,1,0:T(8,128)S(1)} %get-tuple-element.158), channel_id=1, source_target_pairs={{0,16},{16,0},{1,17},{17,1},{2,18},{18,2},{3,19},{19,3},{4,20},{20... | collective-permute-start | bytes 393224 | tf_op jit(solution)/shard_map/ppermute | solution.py:31
  4.7 6.3 %collective-permute-start = (f32[4,4,16,128]{3,2,1,0:T(8,128)S(1)}, f32[4,4,16,128]{3,2,1,0:T(8,128)S(1)}, u32[]{:S(2)}, u32[]{:S(2)}) collective-permute-start(f32[4,4,16,128]{3,2,1,0:T(8,128)S(1)} %get-tuple-element.157), channel_id=1, source_target_pairs={{16,0},{0,16},{17,1},{1,17},{18,2},{2,18},{19,3},{3,19},{20,4},{4,... | collective-permute-start | bytes 393224 | tf_op jit(solution)/shard_map/ppermute | solution.py:34
  11.0 7.6 %copy-start.4 = (f32[4,24,16,128]{3,2,1,0:T(8,128)}, f32[4,24,16,128]{3,2,1,0:T(8,128)S(1)}, u32[]{:S(2)}) copy-start(f32[4,24,16,128]{3,2,1,0:T(8,128)S(1)} %get-tuple-element.166) | copy-start | bytes 2359300
  11.1 4.7 %collective-permute-start.2 = (f32[4,24,4,128]{3,2,1,0:T(4,128)S(1)}, f32[4,24,4,128]{3,2,1,0:T(4,128)S(1)}, u32[]{:S(2)}, u32[]{:S(2)}) collective-permute-start(f32[4,24,4,128]{3,2,1,0:T(4,128)S(1)} %get-tuple-element.143), channel_id=1, source_target_pairs={{4,0},{8,4},{12,8},{0,12},{5,1},{9,5},{13,9},{1,13},{6,2},{10,6},{... | collective-permute-start | bytes 589832 | tf_op jit(solution)/shard_map/ppermute | solution.py:34
  11.5 7.2 %collective-permute-start.3 = (f32[4,24,4,128]{3,2,1,0:T(4,128)S(1)}, f32[4,24,4,128]{3,2,1,0:T(4,128)S(1)}, u32[]{:S(2)}, u32[]{:S(2)}) collective-permute-start(f32[4,24,4,128]{3,2,1,0:T(4,128)S(1)} %get-tuple-element.142), channel_id=1, source_target_pairs={{0,4},{4,8},{8,12},{12,0},{1,5},{5,9},{9,13},{13,1},{2,6},{6,10},{... | collective-permute-start | bytes 589832 | tf_op jit(solution)/shard_map/ppermute | solution.py:31
  21.0 8.1 %copy-start.35 = (s32[4,256]{1,0:T(4,128)S(1)}, s32[4,256]{1,0:T(4,128)}, u32[]{:S(2)}) copy-start(s32[4,256]{1,0:T(4,128)} %param.11) | copy-start | bytes 12292
  22.9 9.0 %collective-permute-start.4 = (f32[4,24,24,4]{2,1,3,0:T(8,128)S(1)}, f32[4,24,24,4]{2,1,3,0:T(8,128)}, u32[]{:S(2)}, u32[]{:S(2)}) collective-permute-start(f32[4,24,24,4]{2,1,3,0:T(8,128)S(1)} %copy.9), channel_id=1, source_target_pairs={{1,0},{2,1},{3,2},{0,3},{5,4},{6,5},{7,6},{4,7},{9,8},{10,9},{11,1... | collective-permute-start | bytes 110600 | tf_op jit(solution)/shard_map/ppermute | solution.py:34
  27.9 9.3 %collective-permute-start.5 = (f32[4,24,24,4]{2,1,3,0:T(8,128)}, f32[4,24,24,4]{2,1,3,0:T(8,128)S(1)}, u32[]{:S(2)}, u32[]{:S(2)}) collective-permute-start(f32[4,24,24,4]{2,1,3,0:T(8,128)} %copy.11), channel_id=1, source_target_pairs={{0,1},{1,2},{2,3},{3,0},{4,5},{5,6},{6,7},{7,4},{8,9},{9,10},{10,1... | collective-permute-start | bytes 110600 | tf_op jit(solution)/shard_map/ppermute | solution.py:31
  38.8 8.6 %copy-start.1 = (f32[4,24,24,4]{3,2,1,0:T(8,128)S(1)}, f32[4,24,24,4]{3,2,1,0:T(8,128)}, u32[]{:S(2)}) copy-start(f32[4,24,24,4]{3,2,1,0:T(8,128)} %copy.12) | copy-start | bytes 110596
  38.8 8.6 %copy-start.17 = (f32[4,24,4,128]{3,2,1,0:T(4,128)S(1)}, f32[4,24,4,128]{3,2,1,0:T(4,128)}, u32[]{:S(2)}) copy-start(f32[4,24,4,128]{3,2,1,0:T(4,128)} %copy-done.16) | copy-start | bytes 589828
  38.8 8.6 %copy-start.18 = (f32[16,16,128]{2,1,0:T(8,128)S(1)}, f32[16,16,128]{2,1,0:T(8,128)}, u32[]{:S(2)}) copy-start(f32[16,16,128]{2,1,0:T(8,128)} %get-tuple-element.159) | copy-start | bytes 393220
  38.8 8.6 %copy-start.20 = (f32[16,16,128]{2,1,0:T(8,128)S(1)}, f32[16,16,128]{2,1,0:T(8,128)}, u32[]{:S(2)}) copy-start(f32[16,16,128]{2,1,0:T(8,128)} %get-tuple-element.160) | copy-start | bytes 393220
  38.8 8.6 %copy-start.22 = (f32[16,16,128]{2,1,0:T(8,128)S(1)}, f32[16,16,128]{2,1,0:T(8,128)}, u32[]{:S(2)}) copy-start(f32[16,16,128]{2,1,0:T(8,128)} %get-tuple-element.161) | copy-start | bytes 393220
  38.9 8.6 %copy-start.25 = (f32[1,16,16,128]{3,2,1,0:T(8,128)S(1)}, f32[1,16,16,128]{3,2,1,0:T(8,128)}, u32[]{:S(2)}) copy-start(f32[1,16,16,128]{3,2,1,0:T(8,128)} %get-tuple-element.130) | copy-start | bytes 393220
  38.9 8.6 %copy-start.27 = (f32[1,16,16,128]{3,2,1,0:T(8,128)S(1)}, f32[1,16,16,128]{3,2,1,0:T(8,128)}, u32[]{:S(2)}) copy-start(f32[1,16,16,128]{3,2,1,0:T(8,128)} %get-tuple-element.169) | copy-start | bytes 393220
  38.9 8.6 %copy-start.28 = (f32[1,16,16,128]{3,2,1,0:T(8,128)S(1)}, f32[1,16,16,128]{3,2,1,0:T(8,128)}, u32[]{:S(2)}) copy-start(f32[1,16,16,128]{3,2,1,0:T(8,128)} %get-tuple-element.170) | copy-start | bytes 393220
  38.9 8.6 %copy-start.29 = (f32[1,16,16,128]{3,2,1,0:T(8,128)S(1)}, f32[1,16,16,128]{3,2,1,0:T(8,128)}, u32[]{:S(2)}) copy-start(f32[1,16,16,128]{3,2,1,0:T(8,128)} %get-tuple-element.171) | copy-start | bytes 393220
  52.8 6.5 %collective-permute-start.6 = (f32[4,4,16,128]{3,2,1,0:T(8,128)S(1)}, f32[4,4,16,128]{3,2,1,0:T(8,128)S(1)}, u32[]{:S(2)}, u32[]{:S(2)}) collective-permute-start(f32[4,4,16,128]{3,2,1,0:T(8,128)S(1)} %get-tuple-element.149), channel_id=1, source_target_pairs={{16,0},{0,16},{17,1},{1,17},{18,2},{2,18},{19,3},{3,19},{20,4},{4,... | collective-permute-start | bytes 393224 | tf_op jit(solution)/shard_map/ppermute | solution.py:34
  54.4 6.4 %collective-permute-start.7 = (f32[4,4,16,128]{3,2,1,0:T(8,128)S(1)}, f32[4,4,16,128]{3,2,1,0:T(8,128)S(1)}, u32[]{:S(2)}, u32[]{:S(2)}) collective-permute-start(f32[4,4,16,128]{3,2,1,0:T(8,128)S(1)} %get-tuple-element.148), channel_id=1, source_target_pairs={{0,16},{16,0},{1,17},{17,1},{2,18},{18,2},{3,19},{19,3},{4,20},{20... | collective-permute-start | bytes 393224 | tf_op jit(solution)/shard_map/ppermute | solution.py:31
  60.8 6.3 %copy-start.6 = (f32[4,4,16,128]{3,2,1,0:T(8,128)}, f32[4,4,16,128]{3,2,1,0:T(8,128)S(1)}, u32[]{:S(2)}) copy-start(f32[4,4,16,128]{3,2,1,0:T(8,128)S(1)} %collective-permute-done.7) | copy-start | bytes 393220
  60.9 5.2 %collective-permute-start.8 = (f32[4,24,4,128]{3,2,1,0:T(4,128)S(1)}, f32[4,24,4,128]{3,2,1,0:T(4,128)S(1)}, u32[]{:S(2)}, u32[]{:S(2)}) collective-permute-start(f32[4,24,4,128]{3,2,1,0:T(4,128)S(1)} %get-tuple-element.140), channel_id=1, source_target_pairs={{4,0},{8,4},{12,8},{0,12},{5,1},{9,5},{13,9},{1,13},{6,2},{10,6},{... | collective-permute-start | bytes 589832 | tf_op jit(solution)/shard_map/ppermute | solution.py:34
  61.0 6.2 %collective-permute-start.9 = (f32[4,24,4,128]{3,2,1,0:T(4,128)S(1)}, f32[4,24,4,128]{3,2,1,0:T(4,128)S(1)}, u32[]{:S(2)}, u32[]{:S(2)}) collective-permute-start(f32[4,24,4,128]{3,2,1,0:T(4,128)S(1)} %get-tuple-element.141), channel_id=1, source_target_pairs={{0,4},{4,8},{8,12},{12,0},{1,5},{5,9},{9,13},{13,1},{2,6},{6,10},{... | collective-permute-start | bytes 589832 | tf_op jit(solution)/shard_map/ppermute | solution.py:31
  69.7 8.9 %collective-permute-start.10 = (f32[4,24,24,4]{2,1,3,0:T(8,128)}, f32[4,24,24,4]{2,1,3,0:T(8,128)}, u32[]{:S(2)}, u32[]{:S(2)}) collective-permute-start(f32[4,24,24,4]{2,1,3,0:T(8,128)} %copy.13), channel_id=1, source_target_pairs={{1,0},{2,1},{3,2},{0,3},{5,4},{6,5},{7,6},{4,7},{9,8},{10,9},{11,1... | collective-permute-start | bytes 110600 | tf_op jit(solution)/shard_map/ppermute | solution.py:34
  74.3 8.6 %collective-permute-start.11 = (f32[4,24,24,4]{2,1,3,0:T(8,128)}, f32[4,24,24,4]{2,1,3,0:T(8,128)}, u32[]{:S(2)}, u32[]{:S(2)}) collective-permute-start(f32[4,24,24,4]{2,1,3,0:T(8,128)} %copy.15), channel_id=1, source_target_pairs={{0,1},{1,2},{2,3},{3,0},{4,5},{5,6},{6,7},{7,4},{8,9},{9,10},{10,1... | collective-permute-start | bytes 110600 | tf_op jit(solution)/shard_map/ppermute | solution.py:31
  85.5 6.1 %copy-start.21 = (f32[16,16,128]{2,1,0:T(8,128)S(1)}, f32[16,16,128]{2,1,0:T(8,128)}, u32[]{:S(2)}) copy-start(f32[16,16,128]{2,1,0:T(8,128)} %get-tuple-element.160) | copy-start | bytes 393220
  85.5 6.1 %copy-start.23 = (f32[16,16,128]{2,1,0:T(8,128)S(1)}, f32[16,16,128]{2,1,0:T(8,128)}, u32[]{:S(2)}) copy-start(f32[16,16,128]{2,1,0:T(8,128)} %get-tuple-element.161) | copy-start | bytes 393220
  85.5 6.1 %copy-start.26 = (f32[1,16,16,128]{3,2,1,0:T(8,128)S(1)}, f32[1,16,16,128]{3,2,1,0:T(8,128)}, u32[]{:S(2)}) copy-start(f32[1,16,16,128]{3,2,1,0:T(8,128)} %get-tuple-element.126) | copy-start | bytes 393220
  85.5 6.1 %copy-start.30 = (f32[1,16,16,128]{3,2,1,0:T(8,128)S(1)}, f32[1,16,16,128]{3,2,1,0:T(8,128)}, u32[]{:S(2)}) copy-start(f32[1,16,16,128]{3,2,1,0:T(8,128)} %get-tuple-element.162) | copy-start | bytes 393220
  85.5 6.1 %copy-start.31 = (f32[1,16,16,128]{3,2,1,0:T(8,128)S(1)}, f32[1,16,16,128]{3,2,1,0:T(8,128)}, u32[]{:S(2)}) copy-start(f32[1,16,16,128]{3,2,1,0:T(8,128)} %get-tuple-element.163) | copy-start | bytes 393220
  85.6 6.1 %copy-start.32 = (f32[1,16,16,128]{3,2,1,0:T(8,128)S(1)}, f32[1,16,16,128]{3,2,1,0:T(8,128)}, u32[]{:S(2)}) copy-start(f32[1,16,16,128]{3,2,1,0:T(8,128)} %get-tuple-element.164) | copy-start | bytes 393220
  177.3 4.0 %collective-permute-start.12 = (f32[4,2048]{1,0:T(4,128)S(1)}, f32[4,2048]{1,0:T(4,128)S(1)}, u32[]{:S(2)}, u32[]{:S(2)}) collective-permute-start(f32[4,2048]{1,0:T(4,128)S(1)} %get-tuple-element.173), channel_id=1, source_target_pairs={{0,16},{16,0},{1,17},{17,1},{2,18},{18,2},{3,19},{19,3},{4,20},{20... | collective-permute-start | bytes 98312 | tf_op jit(solution)/shard_map/ppermute | solution.py:42
  (19 other events, 53.9 us)
where the time goes:
time: 188 us; the launch traced here: 187 us
  matrix products  46.3 us (25%)
  local copies, waits for them, and re-layouts  33.6 us (18%)
  other arithmetic  33.4 us (18%)
  waiting for transfers between devices  31.4 us (17%)
  loops' own time  21.5 us (11%)
  starting transfers between devices  14.8 us (8%)
  blocking collectives  4.59 us (2%)
    dot_general x16, matrix products, shade(): jnp.dot(table_values, weights, preferred_element_type=jnp.float32, precis...  44.6 us
    another operation x1, loops' own time, march_slices(): lax.scan(advance, start, jnp.arange(slice_count, dtype=jnp.int32))  21.5 us
    ppermute x6, waiting for transfers between devices, extended(): lax.ppermute(lax.slice_in_dim(block, 0, width, axis=dim), axis, backward)  18 us
    add x2, other arithmetic, tendency(): laplace = laplace + SECOND_COEF[offset] * (forward + backward)  14.3 us
    ppermute x6, waiting for transfers between devices, extended(): lax.ppermute(lax.slice_in_dim(block, block.shape[dim] - width, None, axis...  11.1 us
    dynamic_slice x16, local copies, waits for them, and re-layouts, march_slices(): lax.scan(advance, start, jnp.arange(slice_count, dtype=jnp.int32))  9.38 us
    ppermute x6, starting transfers between devices, extended(): lax.ppermute(lax.slice_in_dim(block, 0, width, axis=dim), axis, backward)  8.99 us
    slice x4, local copies, waits for them, and re-layouts, extended(): lax.slice_in_dim(block, 0, width, axis=dim)  5.69 us
  transfers between devices with their start and end apart: 13, of which 13 were waited for; matrix products, arithmetic and copies ran while one was open for 8% of the time, Pallas kernels for 0%

commit v1 on v0

v1 whole, which is shorter than its diff:
```python
import functools

import jax
import jax.numpy as jnp
import numpy as np
from jax import lax
from jax.experimental import pallas as pl
from jax.experimental.pallas import tpu as pltpu
from jax.sharding import PartitionSpec as P

PIX_R = 64
PIX_C = 64
HALO = 4

FIRST_COEF = (0.8, -0.2, 4.0 / 105.0, -1.0 / 280.0)
SECOND_COEF = (1.6, -0.2, 8.0 / 315.0, -1.0 / 560.0)
CENTER_COEF = -205.0 / 72.0
FIRST_SCALE = 840
SECOND_SCALE = 5040
DIFFUSIVITY = (0.05, 0.04, 0.03, 0.08)
TIME_STEP = 0.2
RATE_CONST = 2.0
IGNITION_SLOPE = 8.0
IGNITION_TEMP = 0.5
OXIDIZER_RATIO = 1.5
HEAT_RELEASE = 0.8
SHEAR_CELLS = 2.0
OPACITY_TOTAL = 6.0
SOURCE_COEF = (-1.0, -OXIDIZER_RATIO, 1.0 + OXIDIZER_RATIO, HEAT_RELEASE)

VMEM_LIMIT = 24 * 1024 * 1024
F32 = jnp.float32
BF16 = jnp.bfloat16


def column_stencil(columns):
    band = np.zeros((columns + 2 * HALO, 2 * columns), np.float32)
    for column in range(columns):
        for k in range(HALO):
            first = round(FIRST_COEF[k] * FIRST_SCALE)
            second = round(SECOND_COEF[k] * SECOND_SCALE)
            ahead, behind = column + HALO + k + 1, column + HALO - k - 1
            band[ahead, column] += first
            band[behind, column] -= first
            band[ahead, columns + column] += second
            band[behind, columns + column] += second
    inner = band[HALO : HALO + columns]
    halo = np.concatenate([band[:HALO], band[HALO + columns :]], 0)
    return inner, halo


def stencil_weights(columns):
    inner, halo = column_stencil(columns)
    spread = np.tile(halo, (columns // (2 * HALO), 1))
    return np.concatenate([inner, inner], 0), np.concatenate([spread, spread], 0)


def column_matrix(cell_count, pixels):
    stride = cell_count / pixels
    spread = max(1.0, stride)
    centres = np.clip((np.arange(pixels) + 0.5) * stride - 0.5, 0.0, cell_count - 1.0)
    cells_at = np.arange(cell_count)
    return np.maximum(0.0, 1.0 - np.abs(centres[None, :] - cells_at[:, None]) / spread) / spread


def halves(value):
    upper = value.astype(BF16)
    return upper, (value - upper.astype(F32)).astype(BF16)


def by_field(field, values):
    result = jnp.float32(values[-1])
    for index in range(len(values) - 2, -1, -1):
        result = jnp.where(field == index, jnp.float32(values[index]), result)
    return result


def pack_field(source, field, depth_out, low_out, high_out, column_out):
    _, depth, rows, columns = source.shape
    half = depth // 2
    depth_out[field, 0:HALO] = source[field, depth - HALO : depth]
    depth_out[field, HALO : 2 * HALO] = source[field, 0:HALO]
    for d in range(half):
        low_out[field, d, 0:HALO] = source[field, d, 0:HALO]
        low_out[field, d, HALO : 2 * HALO] = source[field, d + half, 0:HALO]
        high_out[field, d, 0:HALO] = source[field, d, rows - HALO : rows]
        high_out[field, d, HALO : 2 * HALO] = source[field, d + half, rows - HALO : rows]
    lane = lax.broadcasted_iota(jnp.int32, (rows, columns), 1)
    packed = jnp.zeros((rows, columns), F32)
    for d in range(depth):
        turned = pltpu.roll(source[field, d], (2 * HALO * d + HALO) % columns, 1)
        packed = jnp.where(lane // (2 * HALO) == d, turned, packed)
    column_out[field] = packed


def pack_kernel(state, depth_out, low_out, high_out, column_out):
    def each(field, carry):
        pack_field(state, field, depth_out, low_out, high_out, column_out)
        return carry

    lax.fori_loop(0, state.shape[0], each, 0)


def reaction(fields, rate):
    rate[...] = (
        RATE_CONST
        * fields[0]
        * fields[1]
        / (1.0 + jnp.exp(-IGNITION_SLOPE * (fields[3] - IGNITION_TEMP)))
    )


def field_tendency(
    fields, field, velocity, halos, weights, rate, padded, across, write
):
    depth_halo, row_below, row_above, column_below, column_above = halos
    inner_weight, halo_weight = weights
    _, depth, rows, columns = fields.shape
    half = depth // 2
    start = 2 * HALO

    flat = fields[field].reshape(depth * rows, columns)
    upper, lower = halves(flat)
    total = jnp.dot(
        jnp.concatenate([upper, lower], 1), inner_weight[...], preferred_element_type=F32
    )
    lane = lax.broadcasted_iota(jnp.int32, (rows, columns), 1)
    edge = jnp.where(lane % (2 * HALO) < HALO, column_below[field], column_above[field])
    edge_upper, edge_lower = halves(edge)
    spread = []
    for d in range(depth):
        own = lane // (2 * HALO) == d
        zero = jnp.zeros((rows, columns), BF16)
        spread.append(
            jnp.concatenate(
                [jnp.where(own, edge_upper, zero), jnp.where(own, edge_lower, zero)], 1
            )
        )
    total = total + jnp.dot(
        jnp.concatenate(spread, 0), halo_weight[...], preferred_element_type=F32
    )
    across[...] = total

    for d in range(depth):
        padded[d, start : start + rows] = fields[field, d]
        part = slice(0, HALO) if d < half else slice(HALO, 2 * HALO)
        padded[d, start - HALO : start] = row_below[field, d % half, part]
        padded[d, start + rows : start + rows + HALO] = row_above[field, d % half, part]

    def layer(d):
        if d < 0:
            return depth_halo[field, d + HALO]
        if d >= depth:
            return depth_halo[field, d - depth + HALO]
        return fields[field, d]

    diffusivity = by_field(field, DIFFUSIVITY)
    source = by_field(field, SOURCE_COEF)
    for d in range(depth):
        centre = fields[field, d]
        laplace = 3.0 * CENTER_COEF * centre
        along_depth = jnp.zeros_like(centre)
        along_row = jnp.zeros_like(centre)
        for k in range(HALO):
            ahead, behind = layer(d + k + 1), layer(d - k - 1)
            up = padded[d, start + k + 1 : start + k + 1 + rows]
            down = padded[d, start - k - 1 : start - k - 1 + rows]
            along_depth = along_depth + FIRST_COEF[k] * (ahead - behind)
            along_row = along_row + FIRST_COEF[k] * (up - down)
            laplace = laplace + SECOND_COEF[k] * ((ahead + behind) + (up + down))
        here = pl.ds(d * rows, rows)
        along_column = across[here, 0:columns] * (1.0 / FIRST_SCALE)
        laplace = laplace + across[here, columns : 2 * columns] * (1.0 / SECOND_SCALE)
        advect = (
            velocity[0, d] * along_depth
            + velocity[1, d] * along_row
            + velocity[2, d] * along_column
        )
        write(d, diffusivity * laplace - advect + source * rate[d])


def first_kernel(
    state,
    velocity,
    depth_halo,
    row_below,
    row_above,
    column_below,
    column_above,
    inner_weight,
    halo_weight,
    middle,
    depth_out,
    low_out,
    high_out,
    column_out,
    rate,
    padded,
    across,
):
    reaction(state, rate)
    halos = (depth_halo, row_below, row_above, column_below, column_above)

    def each(field, carry):
        def write(d, value):
            middle[field, d] = state[field, d] + TIME_STEP * value

        field_tendency(
            state, field, velocity, halos, (inner_weight, halo_weight), rate, padded, across, write
        )
        pack_field(middle, field, depth_out, low_out, high_out, column_out)
        return carry

    lax.fori_loop(0, state.shape[0], each, 0)


def sample_slices(temperature, column_weight, first_slice, slice_total, samples):
    depth, rows, columns = temperature.shape
    half = depth // 2
    upper, lower = halves(temperature[...].reshape(depth * rows, columns))
    wide = jnp.dot(
        jnp.concatenate([upper, lower], 1), column_weight[...], preferred_element_type=F32
    )
    lane = lax.broadcasted_iota(jnp.int32, (rows, 2 * PIX_C), 1)
    stride = rows / PIX_R
    reach = max(1.0, stride)
    shape = (PIX_R, 4 * rows)
    pixel = lax.broadcasted_iota(jnp.int32, shape, 0).astype(F32)
    place = lax.broadcasted_iota(jnp.int32, shape, 1)
    cell = (place % rows).astype(F32)
    later = (place // rows % 2) * half
    for i in range(half):
        level = (first_slice + i + later).astype(F32)
        shift = SHEAR_CELLS * ((level + 0.5) / slice_total - 0.5)
        at = jnp.clip((pixel + 0.5) * stride - 0.5 + shift, 0.0, rows - 1.0)
        weight = jnp.maximum(0.0, 1.0 - jnp.abs(at - cell) / reach) / reach
        left = jnp.where(lane < PIX_C, wide[i * rows : (i + 1) * rows], 0.0)
        right = jnp.where(
            lane < PIX_C, 0.0, wide[(i + half) * rows : (i + half + 1) * rows]
        )
        both = jnp.concatenate([left, right], 0)
        both_upper, both_lower = halves(both)
        samples[i] = jnp.dot(
            weight.astype(BF16),
            jnp.concatenate([both_upper, both_lower], 0),
            preferred_element_type=F32,
        )


def look_up(tables, index, shape):
    lanes = tables[0].shape[1]
    inside = index % lanes
    result = None
    for part, table in enumerate(tables):
        found = jnp.take_along_axis(
            jnp.broadcast_to(table, shape), inside, axis=1, mode="promise_in_bounds"
        )
        result = found if part == 0 else jnp.where(index >= part * lanes, found, result)
    return result


def march(samples, table, flag, slice_total, share):
    half, pixel_rows, lanes = samples.shape
    levels = table.shape[1]
    packed = table[0:1] + table[1:2] * 256 + table[2:3] * 65536 + table[3:4] * 16777216
    following = jnp.concatenate([packed[:, 1:], packed[:, levels - 1 :]], 1)
    below_tables = [packed[:, i : i + lanes] for i in range(0, levels, lanes)]
    above_tables = [following[:, i : i + lanes] for i in range(0, levels, lanes)]
    shape = (pixel_rows // 2, lanes)
    lane = lax.broadcasted_iota(jnp.int32, shape, 1)
    in_front = (lane < PIX_C) == (flag == 0)
    parts = []
    for part in range(2):
        rows_here = pl.ds(part * shape[0], shape[0])

        def advance(position, running):
            chosen = jnp.where(flag == 0, half - 1 - position, position)
            values = samples[chosen, rows_here]
            level = jnp.clip(values, 0.0, 1.0) * (levels - 1.0)
            lower = jnp.minimum(level.astype(jnp.int32), levels - 2)
            fraction = level - lower.astype(F32)
            below = look_up(below_tables, lower, shape)
            above = look_up(above_tables, lower, shape)
            raw = []
            for channel in range(4):
                low = (lax.shift_right_logical(below, 8 * channel) & 255).astype(F32)
                high = (lax.shift_right_logical(above, 8 * channel) & 255).astype(F32)
                raw.append(low + fraction * (high - low))
            alpha = raw[3] * (OPACITY_TOTAL / slice_total / 255.0)
            scaled = alpha * (1.0 / 255.0)
            through = 1.0 - alpha
            return tuple(
                [scaled * raw[c] + through * running[c] for c in range(3)]
                + [alpha + through * running[3]]
            )

        zero = jnp.zeros(shape, F32)
        parts.append(lax.fori_loop(0, half, advance, (zero, zero, zero, zero)))
    for channel in range(4):
        merged = []
        for part in range(2):
            own, own_alpha = parts[part][channel], parts[part][3]
            other, other_alpha = pltpu.roll(own, PIX_C, 1), pltpu.roll(own_alpha, PIX_C, 1)
            merged.append(
                jnp.where(
                    in_front, own + (1.0 - own_alpha) * other, other + (1.0 - other_alpha) * own
                )
            )
        share[channel] = jnp.where(lane < PIX_C, merged[0], merged[1])


def second_kernel(
    slice_total,
    order,
    place,
    middle,
    state,
    velocity,
    depth_halo,
    row_below,
    row_above,
    column_below,
    column_above,
    inner_weight,
    halo_weight,
    column_weight,
    table,
    new_state,
    share,
    rate,
    padded,
    across,
    samples,
):
    reaction(middle, rate)
    halos = (depth_halo, row_below, row_above, column_below, column_above)

    def each(field, carry):
        def write(d, value):
            new_state[field, d] = 0.5 * (state[field, d] + middle[field, d]) + (
                0.5 * TIME_STEP
            ) * value

        field_tendency(
            middle, field, velocity, halos, (inner_weight, halo_weight), rate, padded, across, write
        )
        return carry

    lax.fori_loop(0, state.shape[0], each, 0)
    depth = state.shape[1]
    sample_slices(new_state.at[3], column_weight, place[0] * depth, slice_total, samples)
    march(samples, table, order[0, 0], slice_total, share)


def merge_kernel(last, order, bit, own, received, out):
    front = order[0, 0] == bit[0]
    shape = own.shape[1:]
    own_alpha, received_alpha = own[3], received[3]
    for channel in range(4):
        one, two = own[channel], received[channel]
        front_value = one + (1.0 - own_alpha) * two
        back_value = two + (1.0 - received_alpha) * one
        value = jnp.where(front, front_value, back_value)
        if last:
            out[channel, 0 : shape[0]] = value[:, 0:PIX_C]
            out[channel, shape[0] : 2 * shape[0]] = pltpu.roll(value, PIX_C, 1)[:, 0:PIX_C]
        else:
            out[channel] = value


def shift(value, axis, step):
    count = lax.axis_size(axis)
    return lax.ppermute(value, axis, [(i, (i + step) % count) for i in range(count)])


def exchange(depth_faces, low_rows, high_rows, columns):
    if lax.axis_size("depth") == 2:
        depth_halo = shift(depth_faces, "depth", 1)
    else:
        depth_halo = jnp.concatenate(
            [
                shift(depth_faces[:, :HALO], "depth", 1),
                shift(depth_faces[:, HALO:], "depth", -1),
            ],
            1,
        )
    row_below = shift(high_rows, "row", 1)
    row_above = shift(low_rows, "row", -1)
    column_below = shift(columns, "col", 1)
    column_above = shift(columns, "col", -1)
    return depth_halo, row_below, row_above, column_below, column_above


def call(kernel, outs, scratch, specs, *args):
    vmem = pl.BlockSpec(memory_space=pltpu.VMEM)
    return pl.pallas_call(
        kernel,
        out_shape=outs,
        in_specs=specs + [vmem] * (len(args) - len(specs)),
        out_specs=jax.tree.map(lambda _: vmem, outs),
        scratch_shapes=scratch,
        compiler_params=pltpu.CompilerParams(vmem_limit_bytes=VMEM_LIMIT),
    )(*args)


def local(state, velocity, view_order, tf_table):
    fields, depth, rows, columns = state.shape
    depth_count = lax.axis_size("depth")
    smem = pl.BlockSpec(memory_space=pltpu.SMEM)

    def array(*shape):
        return jax.ShapeDtypeStruct(shape, F32)

    faces = (
        array(fields, 2 * HALO, rows, columns),
        array(fields, depth // 2, 2 * HALO, columns),
        array(fields, depth // 2, 2 * HALO, columns),
        array(fields, rows, columns),
    )
    inner, halo = stencil_weights(columns)
    inner_weight, halo_weight = jnp.asarray(inner, BF16), jnp.asarray(halo, BF16)
    narrow = column_matrix(columns, PIX_C)
    column_weight = jnp.asarray(np.tile(narrow, (2, 2)), BF16)
    work = [
        pltpu.VMEM((depth, rows, columns), F32),
        pltpu.VMEM((depth, rows + 4 * HALO, columns), F32),
        pltpu.VMEM((depth * rows, 2 * columns), F32),
    ]

    halos = exchange(*call(pack_kernel, faces, [], [], state))
    middle, *middle_faces = call(
        first_kernel,
        (array(*state.shape),) + faces,
        work,
        [],
        state,
        velocity,
        *halos,
        inner_weight,
        halo_weight,
    )
    halos = exchange(*middle_faces)
    depth_index = lax.axis_index("depth")
    new_state, share = call(
        functools.partial(second_kernel, depth * depth_count),
        (array(*state.shape), array(4, PIX_R // 2, 2 * PIX_C)),
        work + [pltpu.VMEM((depth // 2, PIX_R, 2 * PIX_C), F32)],
        [smem, smem],
        view_order,
        depth_index.reshape(1),
        middle,
        state,
        velocity,
        *halos,
        inner_weight,
        halo_weight,
        column_weight,
        tf_table,
    )
    bits = depth_count.bit_length() - 1
    for bit in range(bits):
        pairs = [(i, i ^ 2**bit) for i in range(depth_count)]
        received = lax.ppermute(share, "depth", pairs)
        last = bit == bits - 1
        share = call(
            functools.partial(merge_kernel, last),
            array(4, PIX_R, PIX_C) if last else array(*share.shape),
            [],
            [smem, smem],
            view_order,
            (depth_index // 2**bit % 2).reshape(1),
            share,
            received,
        )
    return new_state, share


def solution(mesh):
    in_specs = (
        P(None, "depth", "row", "col"),
        P(None, "depth", "row", "col"),
        P("row", "col"),
        P(),
    )
    out_specs = (P(None, "depth", "row", "col"), P(None, "row", "col"))
    return jax.shard_map(local, mesh=mesh, in_specs=in_specs, out_specs=out_specs, check_vma=False)
```

time: 188 us -> 33.7 us (0.18)
  matrix products: 46.3 us -> 0 us
  other arithmetic: 33.4 us -> 0 us
  local copies, waits for them, and re-layouts: 33.6 us -> 1.96 us
  waiting for transfers between devices: 31.4 us -> 6.09 us
  loops' own time: 21.5 us -> 0 us
  Pallas kernels: 0 us -> 7.82 us
  blocking collectives: 4.59 us -> 0 us
    dot_general x18 -> x0, matrix products: 46.3 us -> none  [the longest x16 44.6 us: shade(): jnp.dot(table_values, weights, preferred_element_type=jnp.float32, precis...]
    ppermute x13 -> x11, waiting for transfers between devices: 31.4 us -> 6.09 us  [the longest x10 3.3 us: shift(): lax.ppermute(value, axis, [(i, (i + step) % count) for i in range(count)])]
    add x20 -> x0, other arithmetic: 23.6 us -> none  [the longest x2 14.3 us: tendency(): laplace = laplace + SECOND_COEF[offset] * (forward + backward)]
    another operation x1 -> x0, loops' own time: 21.5 us -> none  [march_slices(): lax.scan(advance, start, jnp.arange(slice_count, dtype=jnp.int32))]
    dynamic_slice x16 -> x0, local copies, waits for them, and re-layouts: 9.38 us -> none  [march_slices(): lax.scan(advance, start, jnp.arange(slice_count, dtype=jnp.int32))]
    slice x9 -> x0, local copies, waits for them, and re-layouts: 8.79 us -> none  [the longest x4 5.69 us: extended(): lax.slice_in_dim(block, 0, width, axis=dim)]
    ppermute x4 -> x0, local copies, waits for them, and re-layouts: 8.42 us -> none  [the longest x2 4.27 us: extended(): lax.ppermute(lax.slice_in_dim(block, block.shape[dim] - width, None, axis...]
    pallas_call x0 -> x4, Pallas kernels: none -> 7.82 us  [call(): pl.pallas_call(kernel, out_shape=outs, in_specs=specs + [vmem] * (len(arg...]
  transfers between devices with their start and end apart: 13 -> 11, of which waited for: 13 -> 3; matrix products, arithmetic and copies ran while one was open for 8% -> 0% of each run, Pallas kernels for 0% -> 0%
where the time goes in v1:
time: 33.7 us; the launch traced here: 33.5 us
  starting transfers between devices  16.2 us (48%)
  Pallas kernels  7.82 us (23%)
  waiting for transfers between devices  6.09 us (18%)
  local copies, waits for them, and re-layouts  1.96 us (6%)
  between operations  1.4 us (4%)
    ppermute x10, starting transfers between devices, shift(): lax.ppermute(value, axis, [(i, (i + step) % count) for i in range(count)])  14.7 us
    pallas_call x4, Pallas kernels, call(): pl.pallas_call(kernel, out_shape=outs, in_specs=specs + [vmem] * (len(arg...  7.82 us
    ppermute x10, waiting for transfers between devices, shift(): lax.ppermute(value, axis, [(i, (i + step) % count) for i in range(count)])  3.3 us
    ppermute x1, waiting for transfers between devices, local(): received = lax.ppermute(share, 'depth', pairs)  2.79 us
    unnamed x16, local copies, waits for them, and re-layouts  1.96 us
    ppermute x1, starting transfers between devices, local(): received = lax.ppermute(share, 'depth', pairs)  1.48 us
  transfers between devices with their start and end apart: 11, of which 3 were waited for; matrix products, arithmetic and copies ran while one was open for 0% of the time, Pallas kernels for 0%

profile of v1, /device:TPU:0, one launch (start us, length us, event | category | flops | bytes accessed | tf_op | source)
XLA Modules:
  0.0 33.5 jit_solution(16482756364266363395)
XLA Ops:
  0.6 0.0 copy-start
  0.6 1.0 %copy-done = f32[4,16,16,128]{3,2,1,0:T(8,128)S(1)} copy-done((f32[4,16,16,128]{3,2,1,0:T(8,128)S(1)}, f32[4,16,16,128]{3,2,1,0:T(8,128)}, u32[]{:S(2)}) %copy-start) | copy-done | bytes 524312
  1.7 0.4 %shard_map.86 = (f32[4,8,16,128]{3,2,1,0:T(8,128)S(1)}, f32[4,8,8,128]{3,2,1,0:T(8,128)S(1)}, f32[4,8,8,128]{3,2,1,0:T(8,128)S(1)}, f32[4,16,128]{2,1,0:T(8,128)S(1)}) custom-call(f32[4,16,16,128]{3,2,1,0:T(8,128)S(1)} %copy-done), custom_call_target="tpu_custom_call" | custom-call | tf_op jit(solution)/shard_map/pallas_call | solution.py:396
  2.1 3.0 %collective-permute-start = (f32[4,8,16,128]{3,2,1,0:T(8,128)S(1)}, f32[4,8,16,128]{3,2,1,0:T(8,128)S(1)}, u32[]{:S(2)}, u32[]{:S(2)}) collective-permute-start(f32[4,8,16,128]{3,2,1,0:T(8,128)S(1)} %get-tuple-element.13), channel_id=1, source_target_pairs={{0,16},{16,0},{1,17},{17,1},{2,18},{18,2},{3,19},{19,3},{4,20},{20... | collective-permute-start | bytes 786440 | tf_op jit(solution)/shard_map/ppermute | solution.py:373
  5.1 0.0 collective-permute-start.1
  5.1 1.7 %collective-permute-start.2 = (f32[4,8,8,128]{3,2,1,0:T(8,128)S(1)}, f32[4,8,8,128]{3,2,1,0:T(8,128)S(1)}, u32[]{:S(2)}, u32[]{:S(2)}) collective-permute-start(f32[4,8,8,128]{3,2,1,0:T(8,128)S(1)} %get-tuple-element.15), channel_id=1, source_target_pairs={{0,12},{4,0},{8,4},{12,8},{1,13},{5,1},{9,5},{13,9},{2,14},{6,2},{... | collective-permute-start | bytes 393224 | tf_op jit(solution)/shard_map/ppermute | solution.py:373
  6.9 1.6 %collective-permute-start.3 = (f32[4,16,128]{2,1,0:T(8,128)S(1)}, f32[4,16,128]{2,1,0:T(8,128)S(1)}, u32[]{:S(2)}, u32[]{:S(2)}) collective-permute-start(f32[4,16,128]{2,1,0:T(8,128)S(1)} %get-tuple-element.16), channel_id=1, source_target_pairs={{0,1},{1,2},{2,3},{3,0},{4,5},{5,6},{6,7},{7,4},{8,9},{9,10},{10,1... | collective-permute-start | bytes 98312 | tf_op jit(solution)/shard_map/ppermute | solution.py:373
  8.5 2.2 %collective-permute-start.4 = (f32[4,16,128]{2,1,0:T(8,128)S(1)}, f32[4,16,128]{2,1,0:T(8,128)S(1)}, u32[]{:S(2)}, u32[]{:S(2)}) collective-permute-start(f32[4,16,128]{2,1,0:T(8,128)S(1)} %get-tuple-element.16), channel_id=1, source_target_pairs={{0,3},{1,0},{2,1},{3,2},{4,7},{5,4},{6,5},{7,6},{8,11},{9,8},{10,9... | collective-permute-start | bytes 98312 | tf_op jit(solution)/shard_map/ppermute | solution.py:373
  10.7 2.0 %collective-permute-done.3.column_below = f32[4,16,128]{2,1,0:T(8,128)S(1)} collective-permute-done((f32[4,16,128]{2,1,0:T(8,128)S(1)}, f32[4,16,128]{2,1,0:T(8,128)S(1)}, u32[]{:S(2)}, u32[]{:S(2)}) %collective-permute-start.3) | collective-permute-done | bytes 32800 | tf_op jit(solution)/shard_map/ppermute | solution.py:373
  12.7 0.0 collective-permute-done.4.column_above
  12.7 0.0 collective-permute-done.1.row_below
  12.7 0.0 collective-permute-done.2.row_above
  12.7 0.0 collective-permute-done.depth_halo
  12.7 0.0 copy-done.2
  12.8 0.0 copy-done.3
  12.8 0.0 copy-start.4
  12.8 0.9 %copy-done.4 = bf16[256,256]{1,0:T(8,128)(2,1)S(1)} copy-done((bf16[256,256]{1,0:T(8,128)(2,1)S(1)}, bf16[256,256]{1,0:T(8,128)(2,1)}, u32[]{:S(2)}) %copy-start.4) | copy-done | bytes 131096
  13.7 1.9 %shard_map.87 = (f32[4,16,16,128]{3,2,1,0:T(8,128)S(1)}, f32[4,8,16,128]{3,2,1,0:T(8,128)S(1)}, f32[4,8,8,128]{3,2,1,0:T(8,128)S(1)}, f32[4,8,8,128]{3,2,1,0:T(8,128)S(1)}, f32[4,16,128]{2,1,0:T(8,128)S(1)}) custom-call(f32[4,16,16,128]{3,2,1,0:T(8,128)S(1)} %copy-done, f32[3,16,16,128]{3,2,1,0:T(8,128)S(1)} %copy-done.2, ...), custom_call_target="tpu_custom_call" | custom-call | tf_op jit(solution)/shard_map/pallas_call | solution.py:396
  15.6 0.5 %collective-permute-start.5 = (f32[4,8,16,128]{3,2,1,0:T(8,128)S(1)}, f32[4,8,16,128]{3,2,1,0:T(8,128)S(1)}, u32[]{:S(2)}, u32[]{:S(2)}) collective-permute-start(f32[4,8,16,128]{3,2,1,0:T(8,128)S(1)} %get-tuple-element.18), channel_id=1, source_target_pairs={{0,16},{16,0},{1,17},{17,1},{2,18},{18,2},{3,19},{19,3},{4,20},{20... | collective-permute-start | bytes 786440 | tf_op jit(solution)/shard_map/ppermute | solution.py:373
  16.1 0.0 collective-permute-start.6
  16.1 1.7 %collective-permute-start.7 = (f32[4,8,8,128]{3,2,1,0:T(8,128)S(1)}, f32[4,8,8,128]{3,2,1,0:T(8,128)S(1)}, u32[]{:S(2)}, u32[]{:S(2)}) collective-permute-start(f32[4,8,8,128]{3,2,1,0:T(8,128)S(1)} %get-tuple-element.20), channel_id=1, source_target_pairs={{0,12},{4,0},{8,4},{12,8},{1,13},{5,1},{9,5},{13,9},{2,14},{6,2},{... | collective-permute-start | bytes 393224 | tf_op jit(solution)/shard_map/ppermute | solution.py:373
  17.9 1.5 %collective-permute-start.8 = (f32[4,16,128]{2,1,0:T(8,128)S(1)}, f32[4,16,128]{2,1,0:T(8,128)S(1)}, u32[]{:S(2)}, u32[]{:S(2)}) collective-permute-start(f32[4,16,128]{2,1,0:T(8,128)S(1)} %get-tuple-element.21), channel_id=1, source_target_pairs={{0,1},{1,2},{2,3},{3,0},{4,5},{5,6},{6,7},{7,4},{8,9},{9,10},{10,1... | collective-permute-start | bytes 98312 | tf_op jit(solution)/shard_map/ppermute | solution.py:373
  19.4 2.3 %collective-permute-start.9 = (f32[4,16,128]{2,1,0:T(8,128)S(1)}, f32[4,16,128]{2,1,0:T(8,128)S(1)}, u32[]{:S(2)}, u32[]{:S(2)}) collective-permute-start(f32[4,16,128]{2,1,0:T(8,128)S(1)} %get-tuple-element.21), channel_id=1, source_target_pairs={{0,3},{1,0},{2,1},{3,2},{4,7},{5,4},{6,5},{7,6},{8,11},{9,8},{10,9... | collective-permute-start | bytes 98312 | tf_op jit(solution)/shard_map/ppermute | solution.py:373
  22.4 1.3 %collective-permute-done.8.column_below = f32[4,16,128]{2,1,0:T(8,128)S(1)} collective-permute-done((f32[4,16,128]{2,1,0:T(8,128)S(1)}, f32[4,16,128]{2,1,0:T(8,128)S(1)}, u32[]{:S(2)}, u32[]{:S(2)}) %collective-permute-start.8) | collective-permute-done | bytes 32800 | tf_op jit(solution)/shard_map/ppermute | solution.py:373
  23.6 0.0 collective-permute-done.9.column_above
  23.6 0.0 collective-permute-done.6.row_below
  23.6 0.0 collective-permute-done.7.row_above
  23.6 0.0 collective-permute-done.5.depth_halo
  23.7 4.7 %shard_map.88 = (f32[4,16,16,128]{3,2,1,0:T(8,128)}, f32[4,32,128]{2,1,0:T(8,128)S(1)}) custom-call(s32[1,1]{1,0:T(1,128)S(6)} %copy.9.order, s32[1]{0:T(128)} %bitcast.place, f32[4,16,16,128]{3,2,1,0:T(8,128)S(1)} %get-tuple-element.17.middle, f32[4,16,16,128]{3,2,1,0:T(8,128)S(1)} %copy-done.1, f32[3,16,16,128]{3,2,1,0:T(8,128)S(1)} %copy-done.2, ...), custom_call_target="tpu_custom_call" | custom-call | tf_op jit(solution)/shard_map/pallas_call | solution.py:396
  28.4 1.5 %collective-permute-start.10 = (f32[4,32,128]{2,1,0:T(8,128)S(1)}, f32[4,32,128]{2,1,0:T(8,128)S(1)}, u32[]{:S(2)}, u32[]{:S(2)}) collective-permute-start(f32[4,32,128]{2,1,0:T(8,128)S(1)} %get-tuple-element.23.own), channel_id=1, source_target_pairs={{0,16},{16,0},{1,17},{17,1},{2,18},{18,2},{3,19},{19,3},{4,20},{20... | collective-permute-start | bytes 196616 | tf_op jit(solution)/shard_map/ppermute | solution.py:463
  29.9 2.8 %collective-permute-done.10.received = f32[4,32,128]{2,1,0:T(8,128)S(1)} collective-permute-done((f32[4,32,128]{2,1,0:T(8,128)S(1)}, f32[4,32,128]{2,1,0:T(8,128)S(1)}, u32[]{:S(2)}, u32[]{:S(2)}) %collective-permute-start.10) | collective-permute-done | bytes 65568 | tf_op jit(solution)/shard_map/ppermute | solution.py:463
  32.7 0.7 %shard_map.89 = f32[4,64,64]{2,1,0:T(8,128)} custom-call(s32[1,1]{1,0:T(1,128)S(6)} %copy.9.order, s32[1]{0:T(128)} %bitcast.1.bit, f32[4,32,128]{2,1,0:T(8,128)S(1)} %get-tuple-element.23.own, f32[4,32,128]{2,1,0:T(8,128)S(1)} %collective-permute-done.10.received), custom_call_target="tpu_custom_call" | custom-call | tf_op jit(solution)/shard_map/pallas_call | solution.py:396
  (10 shorter events, 0.0 us)
Async XLA Ops:
  0.6 1.0 %copy-start = (f32[4,16,16,128]{3,2,1,0:T(8,128)S(1)}, f32[4,16,16,128]{3,2,1,0:T(8,128)}, u32[]{:S(2)}) copy-start(f32[4,16,16,128]{3,2,1,0:T(8,128)} %state.5) | copy-start | bytes 1572868
  1.7 11.1 %copy-start.2 = (f32[3,16,16,128]{3,2,1,0:T(8,128)S(1)}, f32[3,16,16,128]{3,2,1,0:T(8,128)}, u32[]{:S(2)}) copy-start(f32[3,16,16,128]{3,2,1,0:T(8,128)} %velocity.3) | copy-start | bytes 1179652
  1.7 11.1 %copy-start.3 = (bf16[256,256]{1,0:T(8,128)(2,1)S(1)}, bf16[256,256]{1,0:T(8,128)(2,1)}, u32[]{:S(2)}) copy-start(bf16[256,256]{1,0:T(8,128)(2,1)} %constant.36.clone.inner_weight) | copy-start | bytes 393220
  2.1 10.6 %collective-permute-start = (f32[4,8,16,128]{3,2,1,0:T(8,128)S(1)}, f32[4,8,16,128]{3,2,1,0:T(8,128)S(1)}, u32[]{:S(2)}, u32[]{:S(2)}) collective-permute-start(f32[4,8,16,128]{3,2,1,0:T(8,128)S(1)} %get-tuple-element.13), channel_id=1, source_target_pairs={{0,16},{16,0},{1,17},{17,1},{2,18},{18,2},{3,19},{19,3},{4,20},{20... | collective-permute-start | bytes 786440 | tf_op jit(solution)/shard_map/ppermute | solution.py:373
  5.1 7.6 %collective-permute-start.1 = (f32[4,8,8,128]{3,2,1,0:T(8,128)S(1)}, f32[4,8,8,128]{3,2,1,0:T(8,128)S(1)}, u32[]{:S(2)}, u32[]{:S(2)}) collective-permute-start(f32[4,8,8,128]{3,2,1,0:T(8,128)S(1)} %get-tuple-element.14), channel_id=1, source_target_pairs={{0,4},{4,8},{8,12},{12,0},{1,5},{5,9},{9,13},{13,1},{2,6},{6,10},{... | collective-permute-start | bytes 393224 | tf_op jit(solution)/shard_map/ppermute | solution.py:373
  5.1 7.6 %collective-permute-start.2 = (f32[4,8,8,128]{3,2,1,0:T(8,128)S(1)}, f32[4,8,8,128]{3,2,1,0:T(8,128)S(1)}, u32[]{:S(2)}, u32[]{:S(2)}) collective-permute-start(f32[4,8,8,128]{3,2,1,0:T(8,128)S(1)} %get-tuple-element.15), channel_id=1, source_target_pairs={{0,12},{4,0},{8,4},{12,8},{1,13},{5,1},{9,5},{13,9},{2,14},{6,2},{... | collective-permute-start | bytes 393224 | tf_op jit(solution)/shard_map/ppermute | solution.py:373
  6.9 16.8 %copy-start.1 = (f32[4,16,16,128]{3,2,1,0:T(8,128)S(1)}, f32[4,16,16,128]{3,2,1,0:T(8,128)}, u32[]{:S(2)}) copy-start(f32[4,16,16,128]{3,2,1,0:T(8,128)} %state.5) | copy-start | bytes 1572868
  6.9 5.8 %collective-permute-start.3 = (f32[4,16,128]{2,1,0:T(8,128)S(1)}, f32[4,16,128]{2,1,0:T(8,128)S(1)}, u32[]{:S(2)}, u32[]{:S(2)}) collective-permute-start(f32[4,16,128]{2,1,0:T(8,128)S(1)} %get-tuple-element.16), channel_id=1, source_target_pairs={{0,1},{1,2},{2,3},{3,0},{4,5},{5,6},{6,7},{7,4},{8,9},{9,10},{10,1... | collective-permute-start | bytes 98312 | tf_op jit(solution)/shard_map/ppermute | solution.py:373
  8.5 4.3 %collective-permute-start.4 = (f32[4,16,128]{2,1,0:T(8,128)S(1)}, f32[4,16,128]{2,1,0:T(8,128)S(1)}, u32[]{:S(2)}, u32[]{:S(2)}) collective-permute-start(f32[4,16,128]{2,1,0:T(8,128)S(1)} %get-tuple-element.16), channel_id=1, source_target_pairs={{0,3},{1,0},{2,1},{3,2},{4,7},{5,4},{6,5},{7,6},{8,11},{9,8},{10,9... | collective-permute-start | bytes 98312 | tf_op jit(solution)/shard_map/ppermute | solution.py:373
  12.8 0.9 %copy-start.4 = (bf16[256,256]{1,0:T(8,128)(2,1)S(1)}, bf16[256,256]{1,0:T(8,128)(2,1)}, u32[]{:S(2)}) copy-start(bf16[256,256]{1,0:T(8,128)(2,1)} %constant.37.clone.halo_weight) | copy-start | bytes 393220
  13.7 10.0 %copy-start.5 = (bf16[256,256]{1,0:T(8,128)(2,1)S(1)}, bf16[256,256]{1,0:T(8,128)(2,1)}, u32[]{:S(2)}) copy-start(bf16[256,256]{1,0:T(8,128)(2,1)} %constant.37.clone.halo_weight) | copy-start | bytes 393220
  13.7 10.0 %copy-start.6 = (bf16[256,128]{1,0:T(8,128)(2,1)S(1)}, bf16[256,128]{1,0:T(8,128)(2,1)}, u32[]{:S(2)}) copy-start(bf16[256,128]{1,0:T(8,128)(2,1)} %constant.38.clone.column_weight) | copy-start | bytes 196612
  15.6 8.1 %collective-permute-start.5 = (f32[4,8,16,128]{3,2,1,0:T(8,128)S(1)}, f32[4,8,16,128]{3,2,1,0:T(8,128)S(1)}, u32[]{:S(2)}, u32[]{:S(2)}) collective-permute-start(f32[4,8,16,128]{3,2,1,0:T(8,128)S(1)} %get-tuple-element.18), channel_id=1, source_target_pairs={{0,16},{16,0},{1,17},{17,1},{2,18},{18,2},{3,19},{19,3},{4,20},{20... | collective-permute-start | bytes 786440 | tf_op jit(solution)/shard_map/ppermute | solution.py:373
  16.1 7.5 %collective-permute-start.6 = (f32[4,8,8,128]{3,2,1,0:T(8,128)S(1)}, f32[4,8,8,128]{3,2,1,0:T(8,128)S(1)}, u32[]{:S(2)}, u32[]{:S(2)}) collective-permute-start(f32[4,8,8,128]{3,2,1,0:T(8,128)S(1)} %get-tuple-element.19), channel_id=1, source_target_pairs={{0,4},{4,8},{8,12},{12,0},{1,5},{5,9},{9,13},{13,1},{2,6},{6,10},{... | collective-permute-start | bytes 393224 | tf_op jit(solution)/shard_map/ppermute | solution.py:373
  16.1 7.5 %collective-permute-start.7 = (f32[4,8,8,128]{3,2,1,0:T(8,128)S(1)}, f32[4,8,8,128]{3,2,1,0:T(8,128)S(1)}, u32[]{:S(2)}, u32[]{:S(2)}) collective-permute-start(f32[4,8,8,128]{3,2,1,0:T(8,128)S(1)} %get-tuple-element.20), channel_id=1, source_target_pairs={{0,12},{4,0},{8,4},{12,8},{1,13},{5,1},{9,5},{13,9},{2,14},{6,2},{... | collective-permute-start | bytes 393224 | tf_op jit(solution)/shard_map/ppermute | solution.py:373
  17.9 5.8 %collective-permute-start.8 = (f32[4,16,128]{2,1,0:T(8,128)S(1)}, f32[4,16,128]{2,1,0:T(8,128)S(1)}, u32[]{:S(2)}, u32[]{:S(2)}) collective-permute-start(f32[4,16,128]{2,1,0:T(8,128)S(1)} %get-tuple-element.21), channel_id=1, source_target_pairs={{0,1},{1,2},{2,3},{3,0},{4,5},{5,6},{6,7},{7,4},{8,9},{9,10},{10,1... | collective-permute-start | bytes 98312 | tf_op jit(solution)/shard_map/ppermute | solution.py:373
  19.4 4.3 %collective-permute-start.9 = (f32[4,16,128]{2,1,0:T(8,128)S(1)}, f32[4,16,128]{2,1,0:T(8,128)S(1)}, u32[]{:S(2)}, u32[]{:S(2)}) collective-permute-start(f32[4,16,128]{2,1,0:T(8,128)S(1)} %get-tuple-element.21), channel_id=1, source_target_pairs={{0,3},{1,0},{2,1},{3,2},{4,7},{5,4},{6,5},{7,6},{8,11},{9,8},{10,9... | collective-permute-start | bytes 98312 | tf_op jit(solution)/shard_map/ppermute | solution.py:373
  21.7 2.0 %copy-start.7 = (s32[4,256]{1,0:T(4,128)S(1)}, s32[4,256]{1,0:T(4,128)}, u32[]{:S(2)}) copy-start(s32[4,256]{1,0:T(4,128)} %table.1) | copy-start | bytes 12292
  28.4 4.3 %collective-permute-start.10 = (f32[4,32,128]{2,1,0:T(8,128)S(1)}, f32[4,32,128]{2,1,0:T(8,128)S(1)}, u32[]{:S(2)}, u32[]{:S(2)}) collective-permute-start(f32[4,32,128]{2,1,0:T(8,128)S(1)} %get-tuple-element.23.own), channel_id=1, source_target_pairs={{0,16},{16,0},{1,17},{17,1},{2,18},{18,2},{3,19},{19,3},{4,20},{20... | collective-permute-start | bytes 196616 | tf_op jit(solution)/shard_map/ppermute | solution.py:463

commit v2 on v1

v2 whole, which is shorter than its diff:
```python
import functools

import jax
import jax.numpy as jnp
from jax import lax
from jax.experimental import pallas as pl
from jax.experimental.pallas import tpu as pltpu
from jax.sharding import PartitionSpec as P

PIX_R = 64
PIX_C = 64
HALO = 4

FIRST_COEF = (0.8, -0.2, 4.0 / 105.0, -1.0 / 280.0)
SECOND_COEF = (1.6, -0.2, 8.0 / 315.0, -1.0 / 560.0)
CENTER_COEF = -205.0 / 72.0
FIRST_SCALE = 840
SECOND_SCALE = 5040
DIFFUSIVITY = (0.05, 0.04, 0.03, 0.08)
TIME_STEP = 0.2
RATE_CONST = 2.0
IGNITION_SLOPE = 8.0
IGNITION_TEMP = 0.5
OXIDIZER_RATIO = 1.5
HEAT_RELEASE = 0.8
SHEAR_CELLS = 2.0
OPACITY_TOTAL = 6.0
SOURCE_COEF = (-1.0, -OXIDIZER_RATIO, 1.0 + OXIDIZER_RATIO, HEAT_RELEASE)

VMEM_LIMIT = 24 * 1024 * 1024
F32 = jnp.float32
BF16 = jnp.bfloat16


def halves(value):
    upper = value.astype(BF16)
    return upper, (value - upper.astype(F32)).astype(BF16)


def by_field(field, values):
    result = jnp.float32(values[-1])
    for index in range(len(values) - 2, -1, -1):
        result = jnp.where(field == index, jnp.float32(values[index]), result)
    return result


def pack_field(source, field, depth_out, low_out, high_out, column_out):
    _, depth, rows, columns = source.shape
    half = depth // 2
    depth_out[field, 0:HALO] = source[field, depth - HALO : depth]
    depth_out[field, HALO : 2 * HALO] = source[field, 0:HALO]
    for d in range(half):
        low_out[field, d, 0:HALO] = source[field, d, 0:HALO]
        low_out[field, d, HALO : 2 * HALO] = source[field, d + half, 0:HALO]
        high_out[field, d, 0:HALO] = source[field, d, rows - HALO : rows]
        high_out[field, d, HALO : 2 * HALO] = source[field, d + half, rows - HALO : rows]
    lane = lax.broadcasted_iota(jnp.int32, (rows, columns), 1)
    packed = jnp.zeros((rows, columns), F32)
    for d in range(depth):
        turned = pltpu.roll(source[field, d], (2 * HALO * d + HALO) % columns, 1)
        packed = jnp.where(lane // (2 * HALO) == d, turned, packed)
    column_out[field] = packed


def pack_kernel(
    state_in, velocity_in, table_in, depth_out, low_out, high_out, column_out, state, velocity, table, sems
):
    copies = [
        pltpu.make_async_copy(source, target, sems.at[i])
        for i, (source, target) in enumerate(
            ((state_in, state), (velocity_in, velocity), (table_in, table))
        )
    ]
    for copy in copies:
        copy.start()
    copies[0].wait()

    def each(field, carry):
        pack_field(state, field, depth_out, low_out, high_out, column_out)
        return carry

    lax.fori_loop(0, state.shape[0], each, 0)
    for copy in copies[1:]:
        copy.wait()


def reaction(fields, rate):
    rate[...] = (
        RATE_CONST
        * fields[0]
        * fields[1]
        / (1.0 + jnp.exp(-IGNITION_SLOPE * (fields[3] - IGNITION_TEMP)))
    )


def band(cells, columns):
    lane = lax.broadcasted_iota(jnp.int32, cells.shape, 1)
    apart = cells - lane % columns
    distance = jnp.abs(apart)
    first = jnp.zeros(cells.shape, F32)
    second = jnp.zeros(cells.shape, F32)
    for k in range(HALO):
        near = distance == k + 1
        first = jnp.where(near, float(round(FIRST_COEF[k] * FIRST_SCALE)), first)
        second = jnp.where(near, float(round(SECOND_COEF[k] * SECOND_SCALE)), second)
    first = jnp.where(apart < 0, -first, first)
    return jnp.where(lane < columns, first, second).astype(BF16)


def interior_field(fields, field, velocity, inner_weight, rate, padded, across, write):
    _, depth, rows, columns = fields.shape
    start = 2 * HALO
    upper, lower = halves(fields[field].reshape(depth * rows, columns))
    across[...] = jnp.dot(
        jnp.concatenate([upper, lower], 1), inner_weight[...], preferred_element_type=F32
    )
    for d in range(depth):
        padded[d, start : start + rows] = fields[field, d]
    diffusivity = by_field(field, DIFFUSIVITY)
    source = by_field(field, SOURCE_COEF)
    for d in range(depth):
        centre = fields[field, d]
        laplace = 3.0 * CENTER_COEF * centre
        along_depth = jnp.zeros_like(centre)
        along_row = jnp.zeros_like(centre)
        for k in range(HALO):
            up = padded[d, start + k + 1 : start + k + 1 + rows]
            down = padded[d, start - k - 1 : start - k - 1 + rows]
            along_row = along_row + FIRST_COEF[k] * (up - down)
            both = up + down
            if d + k + 1 < depth:
                ahead = fields[field, d + k + 1]
                along_depth = along_depth + FIRST_COEF[k] * ahead
                both = both + ahead
            if d - k - 1 >= 0:
                behind = fields[field, d - k - 1]
                along_depth = along_depth - FIRST_COEF[k] * behind
                both = both + behind
            laplace = laplace + SECOND_COEF[k] * both
        here = pl.ds(d * rows, rows)
        along_column = across[here, 0:columns] * (1.0 / FIRST_SCALE)
        laplace = laplace + across[here, columns : 2 * columns] * (1.0 / SECOND_SCALE)
        advect = (
            velocity[0, d] * along_depth
            + velocity[1, d] * along_row
            + velocity[2, d] * along_column
        )
        write(d, diffusivity * laplace - advect + source * rate[d])


def halo_field(part, field, velocity, halos, halo_weight, below, above, across, scale, write):
    depth_halo, row_below, row_above, column_below, column_above = halos
    depth, rows, columns = velocity.shape[1:]
    half = depth // 2
    lane = lax.broadcasted_iota(jnp.int32, (rows, columns), 1)
    edge = jnp.where(lane % (2 * HALO) < HALO, column_below[field], column_above[field])
    edge_upper, edge_lower = halves(edge)
    spread = []
    for d in range(depth):
        own = lane // (2 * HALO) == d
        zero = jnp.zeros((rows, columns), BF16)
        spread.append(
            jnp.concatenate(
                [jnp.where(own, edge_upper, zero), jnp.where(own, edge_lower, zero)], 1
            )
        )
    across[...] = jnp.dot(
        jnp.concatenate(spread, 0), halo_weight[...], preferred_element_type=F32
    )
    for d in range(depth):
        piece = slice(0, HALO) if d < half else slice(HALO, 2 * HALO)
        below[d, HALO : 2 * HALO] = row_below[field, d % half, piece]
        above[d, 2 * HALO : 3 * HALO] = row_above[field, d % half, piece]
    diffusivity = by_field(field, DIFFUSIVITY)
    block = 2 * HALO
    for d in range(depth):
        value = []
        for first in range(0, rows, block):
            here = slice(first, first + block)
            along_column = across[pl.ds(d * rows + first, block), 0:columns] * (1.0 / FIRST_SCALE)
            laplace = across[pl.ds(d * rows + first, block), columns : 2 * columns] * (
                1.0 / SECOND_SCALE
            )
            advect = velocity[2, d, here] * along_column
            along_row = None
            for k in range(HALO):
                if first == 0:
                    down = below[d, block - k - 1 : 2 * block - k - 1]
                    term = -FIRST_COEF[k] * down
                    along_row = term if along_row is None else along_row + term
                    laplace = laplace + SECOND_COEF[k] * down
                if first + block == rows:
                    up = above[d, k + 1 : k + 1 + block]
                    term = FIRST_COEF[k] * up
                    along_row = term if along_row is None else along_row + term
                    laplace = laplace + SECOND_COEF[k] * up
            if along_row is not None:
                advect = advect + velocity[1, d, here] * along_row
            along_depth = None
            for k in range(HALO):
                if d - k - 1 < 0:
                    behind = depth_halo[field, d - k - 1 + HALO, here]
                    term = -FIRST_COEF[k] * behind
                    along_depth = term if along_depth is None else along_depth + term
                    laplace = laplace + SECOND_COEF[k] * behind
                if d + k + 1 >= depth:
                    ahead = depth_halo[field, d + k + 1 - depth + HALO, here]
                    term = FIRST_COEF[k] * ahead
                    along_depth = term if along_depth is None else along_depth + term
                    laplace = laplace + SECOND_COEF[k] * ahead
            if along_depth is not None:
                advect = advect + velocity[0, d, here] * along_depth
            write(d, here, part[field, d, here] + scale * (diffusivity * laplace - advect))


def first_interior(
    slice_total,
    state,
    velocity,
    table,
    columns_sent,
    part,
    inner_weight,
    halo_weight,
    row_weight,
    column_weight,
    packed_table,
    rate,
    padded,
    across,
):
    del columns_sent
    _, depth, rows, columns = state.shape
    shape = inner_weight.shape
    index = lax.broadcasted_iota(jnp.int32, shape, 0) % columns
    inner_weight[...] = band(index, columns)
    edge = index % (2 * HALO)
    halo_weight[...] = band(jnp.where(edge < HALO, edge, edge + columns) - HALO, columns)
    shape = column_weight.shape
    cell = (lax.broadcasted_iota(jnp.int32, shape, 0) % columns).astype(F32)
    pixel = (lax.broadcasted_iota(jnp.int32, shape, 1) % PIX_C).astype(F32)
    column_weight[...] = tent(pixel, cell, 0.0, columns, PIX_C).astype(BF16)
    half = depth // 2
    place = lax.axis_index("depth") * depth
    shape = (PIX_R, row_weight.shape[2])
    pixel = lax.broadcasted_iota(jnp.int32, shape, 0).astype(F32)
    lane = lax.broadcasted_iota(jnp.int32, shape, 1)
    cell = (lane % rows).astype(F32)
    later = (lane // rows % 2) * half
    for i in range(half):
        level = (place + i + later).astype(F32)
        shift = SHEAR_CELLS * ((level + 0.5) / slice_total - 0.5)
        row_weight[i] = tent(pixel, cell, shift, rows, PIX_R).astype(BF16)
    levels = table.shape[1]
    packed = table[0:1] + table[1:2] * 256 + table[2:3] * 65536 + table[3:4] * 16777216
    packed_table[0:1] = packed
    packed_table[1:2] = jnp.concatenate([packed[:, 1:], packed[:, levels - 1 :]], 1)
    padded[...] = jnp.zeros_like(padded)
    reaction(state, rate)

    def each(field, carry):
        def write(d, value):
            part[field, d] = state[field, d] + TIME_STEP * value

        interior_field(state, field, velocity, inner_weight, rate, padded, across, write)
        return carry

    lax.fori_loop(0, state.shape[0], each, 0)


def first_halo(
    part,
    velocity,
    depth_halo,
    row_below,
    row_above,
    column_below,
    column_above,
    halo_weight,
    middle,
    depth_out,
    low_out,
    high_out,
    column_out,
    below,
    above,
    across,
):
    halos = (depth_halo, row_below, row_above, column_below, column_above)
    below[...] = jnp.zeros_like(below)
    above[...] = jnp.zeros_like(above)

    def each(field, carry):
        def write(d, here, value):
            middle[field, d, here] = value

        halo_field(
            part, field, velocity, halos, halo_weight, below, above, across, TIME_STEP, write
        )
        pack_field(middle, field, depth_out, low_out, high_out, column_out)
        return carry

    lax.fori_loop(0, part.shape[0], each, 0)


def second_interior(
    middle, state, velocity, inner_weight, columns_sent, part, rate, padded, across
):
    del columns_sent
    padded[...] = jnp.zeros_like(padded)
    reaction(middle, rate)

    def each(field, carry):
        def write(d, value):
            part[field, d] = 0.5 * (state[field, d] + middle[field, d]) + (
                0.5 * TIME_STEP
            ) * value

        interior_field(middle, field, velocity, inner_weight, rate, padded, across, write)
        return carry

    lax.fori_loop(0, state.shape[0], each, 0)


def tent(pixel, cell, shift, cells, pixels):
    stride = cells / pixels
    reach = max(1.0, stride)
    at = jnp.clip((pixel + 0.5) * stride - 0.5 + shift, 0.0, cells - 1.0)
    return jnp.maximum(0.0, 1.0 - jnp.abs(at - cell) / reach) / reach


def sample_slices(temperature, column_weight, row_weight, samples):
    depth, rows, columns = temperature.shape
    half = depth // 2
    upper, lower = halves(temperature[...].reshape(depth * rows, columns))
    wide = jnp.dot(
        jnp.concatenate([upper, lower], 1), column_weight[...], preferred_element_type=F32
    )
    lane = lax.broadcasted_iota(jnp.int32, (rows, 2 * PIX_C), 1)
    for i in range(half):
        left = jnp.where(lane < PIX_C, wide[i * rows : (i + 1) * rows], 0.0)
        right = jnp.where(
            lane < PIX_C, 0.0, wide[(i + half) * rows : (i + half + 1) * rows]
        )
        both_upper, both_lower = halves(jnp.concatenate([left, right], 0))
        samples[i] = jnp.dot(
            row_weight[i],
            jnp.concatenate([both_upper, both_lower], 0),
            preferred_element_type=F32,
        )


def look_up(tables, index, shape):
    lanes = tables[0].shape[1]
    inside = index % lanes
    result = None
    for part, table in enumerate(tables):
        found = jnp.take_along_axis(
            jnp.broadcast_to(table, shape), inside, axis=1, mode="promise_in_bounds"
        )
        result = found if part == 0 else jnp.where(index >= part * lanes, found, result)
    return result


def march(samples, table, flag, slice_total, share):
    half, pixel_rows, lanes = samples.shape
    levels = table.shape[1]
    below_tables = [table[0:1, i : i + lanes] for i in range(0, levels, lanes)]
    above_tables = [table[1:2, i : i + lanes] for i in range(0, levels, lanes)]
    shape = (pixel_rows // 2, lanes)
    lane = lax.broadcasted_iota(jnp.int32, shape, 1)
    in_front = (lane < PIX_C) == (flag == 0)
    parts = []
    for part in range(2):
        rows_here = pl.ds(part * shape[0], shape[0])

        def advance(position, running):
            chosen = jnp.where(flag == 0, half - 1 - position, position)
            values = samples[chosen, rows_here]
            level = jnp.clip(values, 0.0, 1.0) * (levels - 1.0)
            lower = jnp.minimum(level.astype(jnp.int32), levels - 2)
            fraction = level - lower.astype(F32)
            below = look_up(below_tables, lower, shape)
            above = look_up(above_tables, lower, shape)
            raw = []
            for channel in range(4):
                low = (lax.shift_right_logical(below, 8 * channel) & 255).astype(F32)
                high = (lax.shift_right_logical(above, 8 * channel) & 255).astype(F32)
                raw.append(low + fraction * (high - low))
            alpha = raw[3] * (OPACITY_TOTAL / slice_total / 255.0)
            scaled = alpha * (1.0 / 255.0)
            through = 1.0 - alpha
            return tuple(
                [scaled * raw[c] + through * running[c] for c in range(3)]
                + [alpha + through * running[3]]
            )

        zero = jnp.zeros(shape, F32)
        parts.append(lax.fori_loop(0, half, advance, (zero, zero, zero, zero)))
    for channel in range(4):
        merged = []
        for part in range(2):
            own, own_alpha = parts[part][channel], parts[part][3]
            other, other_alpha = pltpu.roll(own, PIX_C, 1), pltpu.roll(own_alpha, PIX_C, 1)
            merged.append(
                jnp.where(
                    in_front, own + (1.0 - own_alpha) * other, other + (1.0 - other_alpha) * own
                )
            )
        share[channel] = jnp.where(lane < PIX_C, merged[0], merged[1])


def temperature_halo(
    slice_total,
    order,
    part,
    velocity,
    depth_halo,
    row_below,
    row_above,
    column_below,
    column_above,
    halo_weight,
    column_weight,
    row_weight,
    table,
    temperature,
    share,
    toward,
    below,
    above,
    across,
    samples,
):
    halos = (depth_halo, row_below, row_above, column_below, column_above)
    below[...] = jnp.zeros_like(below)
    above[...] = jnp.zeros_like(above)

    def write(d, here, value):
        temperature[d, here] = value

    halo_field(
        part, 3, velocity, halos, halo_weight, below, above, across, 0.5 * TIME_STEP, write
    )
    sample_slices(temperature, column_weight, row_weight, samples)
    toward[...] = jnp.full(toward.shape, order[0, 0], jnp.int32)
    march(samples, table, order[0, 0], slice_total, share)


def fractions_halo(
    part,
    temperature,
    velocity,
    depth_halo,
    row_below,
    row_above,
    column_below,
    column_above,
    halo_weight,
    share,
    new_state,
    below,
    above,
    across,
):
    del share
    halos = (depth_halo, row_below, row_above, column_below, column_above)
    below[...] = jnp.zeros_like(below)
    above[...] = jnp.zeros_like(above)

    def each(field, carry):
        def write(d, here, value):
            new_state[field, d, here] = value

        halo_field(
            part, field, velocity, halos, halo_weight, below, above, across, 0.5 * TIME_STEP, write
        )
        return carry

    lax.fori_loop(0, 3, each, 0)
    new_state[3] = temperature[...]


def merge_kernel(bit, last, toward, own, received, out):
    shape = own.shape[1:]
    mine = lax.axis_index("depth") // 2**bit % 2
    front = jnp.broadcast_to(toward[0:1] == mine, shape)
    own_alpha, received_alpha = own[3], received[3]
    for channel in range(4):
        one, two = own[channel], received[channel]
        front_value = one + (1.0 - own_alpha) * two
        back_value = two + (1.0 - received_alpha) * one
        value = jnp.where(front, front_value, back_value)
        if last:
            out[channel, 0 : shape[0]] = value[:, 0:PIX_C]
            out[channel, shape[0] : 2 * shape[0]] = pltpu.roll(value, PIX_C, 1)[:, 0:PIX_C]
        else:
            out[channel] = value


def shift(value, axis, step):
    count = lax.axis_size(axis)
    return lax.ppermute(value, axis, [(i, (i + step) % count) for i in range(count)])


def exchange(depth_faces, low_rows, high_rows, columns):
    if lax.axis_size("depth") == 2:
        depth_halo = shift(depth_faces, "depth", 1)
    else:
        depth_halo = jnp.concatenate(
            [
                shift(depth_faces[:, :HALO], "depth", 1),
                shift(depth_faces[:, HALO:], "depth", -1),
            ],
            1,
        )
    row_below = shift(high_rows, "row", 1)
    row_above = shift(low_rows, "row", -1)
    column_below = shift(columns, "col", 1)
    column_above = shift(columns, "col", -1)
    return depth_halo, row_below, row_above, column_below, column_above


def call(kernel, outs, scratch, specs, *args):
    vmem = pl.BlockSpec(memory_space=pltpu.VMEM)
    return pl.pallas_call(
        kernel,
        out_shape=outs,
        in_specs=specs + [vmem] * (len(args) - len(specs)),
        out_specs=jax.tree.map(lambda _: vmem, outs),
        scratch_shapes=scratch,
        compiler_params=pltpu.CompilerParams(vmem_limit_bytes=VMEM_LIMIT),
    )(*args)


def in_hbm(value):
    return pltpu.with_memory_space_constraint(value, pltpu.HBM)


def local(state, velocity, view_order, tf_table):
    fields, depth, rows, columns = state.shape
    depth_count = lax.axis_size("depth")

    def array(*shape, dtype=F32):
        return jax.ShapeDtypeStruct(shape, dtype)

    whole = array(*state.shape)
    faces = (
        array(fields, 2 * HALO, rows, columns),
        array(fields, depth // 2, 2 * HALO, columns),
        array(fields, depth // 2, 2 * HALO, columns),
        array(fields, rows, columns),
    )
    across = pltpu.VMEM((depth * rows, 2 * columns), F32)
    inner_work = [
        pltpu.VMEM((depth, rows, columns), F32),
        pltpu.VMEM((depth, rows + 4 * HALO, columns), F32),
        across,
    ]
    halo_work = [
        pltpu.VMEM((depth, 4 * HALO, columns), F32),
        pltpu.VMEM((depth, 4 * HALO, columns), F32),
        across,
    ]
    slice_total = depth * depth_count

    hbm = pl.BlockSpec(memory_space=pltpu.HBM)
    *sent, state, velocity, table = call(
        pack_kernel,
        faces + (whole, array(*velocity.shape), array(*tf_table.shape, dtype=jnp.int32)),
        [pltpu.SemaphoreType.DMA((3,))],
        [hbm, hbm, hbm],
        in_hbm(state),
        in_hbm(velocity),
        in_hbm(tf_table),
    )
    halos = exchange(*sent)
    part, inner_weight, halo_weight, row_weight, column_weight, table = call(
        functools.partial(first_interior, slice_total),
        (
            whole,
            array(2 * columns, 2 * columns, dtype=BF16),
            array(2 * columns, 2 * columns, dtype=BF16),
            array(depth // 2, PIX_R, 4 * rows, dtype=BF16),
            array(2 * columns, 2 * PIX_C, dtype=BF16),
            array(2, tf_table.shape[1], dtype=jnp.int32),
        ),
        inner_work,
        [],
        state,
        velocity,
        table,
        sent[3],
    )
    middle, *sent = call(
        first_halo, (whole,) + faces, halo_work, [], part, velocity, *halos, halo_weight
    )
    halos = exchange(*sent)
    part = call(
        second_interior,
        whole,
        inner_work,
        [],
        middle,
        state,
        velocity,
        inner_weight,
        sent[3],
    )
    temperature, share, toward = call(
        functools.partial(temperature_halo, slice_total),
        (
            array(depth, rows, columns),
            array(4, PIX_R // 2, 2 * PIX_C),
            array(8, 2 * PIX_C, dtype=jnp.int32),
        ),
        halo_work
        + [pltpu.VMEM((depth // 2, PIX_R, 2 * PIX_C), F32)],
        [pl.BlockSpec(memory_space=pltpu.SMEM)],
        view_order,
        part,
        velocity,
        *halos,
        halo_weight,
        column_weight,
        row_weight,
        table,
    )
    new_state = call(
        fractions_halo,
        whole,
        halo_work,
        [],
        part,
        temperature,
        velocity,
        *halos,
        halo_weight,
        share,
    )
    bits = depth_count.bit_length() - 1
    for bit in range(bits):
        pairs = [(i, i ^ 2**bit) for i in range(depth_count)]
        received = lax.ppermute(share, "depth", pairs)
        last = bit == bits - 1
        share = call(
            functools.partial(merge_kernel, bit, last),
            array(4, PIX_R, PIX_C) if last else array(*share.shape),
            [],
            [],
            toward,
            share,
            received,
        )
    return new_state, share


def solution(mesh):
    in_specs = (
        P(None, "depth", "row", "col"),
        P(None, "depth", "row", "col"),
        P("row", "col"),
        P(),
    )
    out_specs = (P(None, "depth", "row", "col"), P(None, "row", "col"))
    return jax.shard_map(local, mesh=mesh, in_specs=in_specs, out_specs=out_specs, check_vma=False)
```

time: 33.7 us -> 30.6 us (0.908)
  waiting for transfers between devices: 6.09 us -> 1.36 us
  Pallas kernels: 7.82 us -> 11.3 us
  local copies, waits for them, and re-layouts: 1.96 us -> 0 us
    pallas_call x4 -> x7, Pallas kernels: 7.82 us -> 11.3 us  [call(): pl.pallas_call(kernel, out_shape=outs, in_specs=specs + [vmem] * (len(arg...]
    ppermute x10, waiting for transfers between devices: 3.3 us -> 0.22 us  [shift(): lax.ppermute(value, axis, [(i, (i + step) % count) for i in range(count)])]
    unnamed x16 -> x0, local copies, waits for them, and re-layouts: 1.96 us -> none
    ppermute x1, waiting for transfers between devices: 2.79 us -> 1.14 us  [local(): received = lax.ppermute(share, 'depth', pairs)]
  transfers between devices with their start and end apart: 11 -> 11, of which waited for: 3 -> 2; matrix products, arithmetic and copies ran while one was open for 0% -> 0% of each run, Pallas kernels for 0% -> 16%
where the time goes in v2:
time: 30.6 us; the launch traced here: 30.4 us
  starting transfers between devices  16.3 us (53%)
  Pallas kernels  11.3 us (37%)
  between operations  1.37 us (4%)
  waiting for transfers between devices  1.36 us (4%)
    ppermute x10, starting transfers between devices, shift(): lax.ppermute(value, axis, [(i, (i + step) % count) for i in range(count)])  14.7 us
    pallas_call x7, Pallas kernels, call(): pl.pallas_call(kernel, out_shape=outs, in_specs=specs + [vmem] * (len(arg...  11.3 us
    ppermute x1, starting transfers between devices, local(): received = lax.ppermute(share, 'depth', pairs)  1.58 us
    ppermute x1, waiting for transfers between devices, local(): received = lax.ppermute(share, 'depth', pairs)  1.14 us
  transfers between devices with their start and end apart: 11, of which 2 were waited for; matrix products, arithmetic and copies ran while one was open for 0% of the time, Pallas kernels for 16%

profile of v2, /device:TPU:0, one launch (start us, length us, event | category | flops | bytes accessed | tf_op | source)
XLA Modules:
  0.0 30.4 jit_solution(6006820110550572425)
XLA Ops:
  0.6 1.5 %shard_map.59 = (f32[4,8,16,128]{3,2,1,0:T(8,128)S(1)}, f32[4,8,8,128]{3,2,1,0:T(8,128)S(1)}, f32[4,8,8,128]{3,2,1,0:T(8,128)S(1)}, f32[4,16,128]{2,1,0:T(8,128)...) custom-call(f32[4,16,16,128]{3,2,1,0:T(8,128)} %state_in.1, ...), custom_call_target="tpu_custom_call" | custom-call | tf_op jit(solution)/shard_map/pallas_call | solution.py:526
  2.1 3.0 %collective-permute-start = (f32[4,8,16,128]{3,2,1,0:T(8,128)S(1)}, f32[4,8,16,128]{3,2,1,0:T(8,128)S(1)}, u32[]{:S(2)}, u32[]{:S(2)}) collective-permute-start(f32[4,8,16,128]{3,2,1,0:T(8,128)S(1)} %get-tuple-element.28), channel_id=1, source_target_pairs={{0,16},{16,0},{1,17},{17,1},{2,18},{18,2},{3,19},{19,3},{4,20},{20... | collective-permute-start | bytes 786440 | tf_op jit(solution)/shard_map/ppermute | solution.py:503
  5.2 0.0 collective-permute-start.1
  5.2 1.7 %collective-permute-start.2 = (f32[4,8,8,128]{3,2,1,0:T(8,128)S(1)}, f32[4,8,8,128]{3,2,1,0:T(8,128)S(1)}, u32[]{:S(2)}, u32[]{:S(2)}) collective-permute-start(f32[4,8,8,128]{3,2,1,0:T(8,128)S(1)} %get-tuple-element.30), channel_id=1, source_target_pairs={{0,12},{4,0},{8,4},{12,8},{1,13},{5,1},{9,5},{13,9},{2,14},{6,2},{... | collective-permute-start | bytes 393224 | tf_op jit(solution)/shard_map/ppermute | solution.py:503
  6.9 1.6 %collective-permute-start.3 = (f32[4,16,128]{2,1,0:T(8,128)S(1)}, f32[4,16,128]{2,1,0:T(8,128)S(1)}, u32[]{:S(2)}, u32[]{:S(2)}) collective-permute-start(f32[4,16,128]{2,1,0:T(8,128)S(1)} %get-tuple-element.26.columns_sent), channel_id=1, source_target_pairs={{0,1},{1,2},{2,3},{3,0},{4,5},{5,6},{6,7},{7,4},{8,9},{9,10},{10,1... | collective-permute-start | bytes 98312 | tf_op jit(solution)/shard_map/ppermute | solution.py:503
  8.5 2.2 %collective-permute-start.4 = (f32[4,16,128]{2,1,0:T(8,128)S(1)}, f32[4,16,128]{2,1,0:T(8,128)S(1)}, u32[]{:S(2)}, u32[]{:S(2)}) collective-permute-start(f32[4,16,128]{2,1,0:T(8,128)S(1)} %get-tuple-element.26.columns_sent), channel_id=1, source_target_pairs={{0,3},{1,0},{2,1},{3,2},{4,7},{5,4},{6,5},{7,6},{8,11},{9,8},{10,9... | collective-permute-start | bytes 98312 | tf_op jit(solution)/shard_map/ppermute | solution.py:503
  10.7 1.8 %shard_map.60 = (f32[4,16,16,128]{3,2,1,0:T(8,128)S(1)}, bf16[256,256]{1,0:T(8,128)(2,1)S(1)}, bf16[256,256]{1,0:T(8,128)(2,1)S(1)}, bf16[8,64,64]{2,1,0:T(8,128...) custom-call(f32[4,16,16,128]{3,2,1,0:T(8,128)S(1)} %get-tuple-element.23.state, ...), custom_call_target="tpu_custom_call" | custom-call | tf_op jit(solution)/shard_map/pallas_call | solution.py:526
  12.6 0.2 collective-permute-done.3.column_below
  12.7 0.0 collective-permute-done.4.column_above
  12.8 0.0 collective-permute-done.1.row_below
  12.8 0.0 collective-permute-done.2.row_above
  12.8 0.0 collective-permute-done.depth_halo
  12.8 1.4 %shard_map.61 = (f32[4,16,16,128]{3,2,1,0:T(8,128)S(1)}, f32[4,8,16,128]{3,2,1,0:T(8,128)S(1)}, f32[4,8,8,128]{3,2,1,0:T(8,128)S(1)}, f32[4,8,8,128]{3,2,1,0:T(8,128)S(1)}, f32[4,16,128]{2,1,0:T(8,128)S(1)}) custom-call(f32[4,16,16,128]{3,2,1,0:T(8,128)S(1)} %get-tuple-element.27.part, f32[3,16,16,128]{3,2,1,0:T(8,128)S(1)} %get-tuple-element.24.velocity, ...), custom_call_target="tpu_custom_call" | custom-call | tf_op jit(solution)/shard_map/pallas_call | solution.py:526
  14.2 0.6 %collective-permute-start.5 = (f32[4,8,16,128]{3,2,1,0:T(8,128)S(1)}, f32[4,8,16,128]{3,2,1,0:T(8,128)S(1)}, u32[]{:S(2)}, u32[]{:S(2)}) collective-permute-start(f32[4,8,16,128]{3,2,1,0:T(8,128)S(1)} %get-tuple-element.35), channel_id=1, source_target_pairs={{0,16},{16,0},{1,17},{17,1},{2,18},{18,2},{3,19},{19,3},{4,20},{20... | collective-permute-start | bytes 786440 | tf_op jit(solution)/shard_map/ppermute | solution.py:503
  14.8 0.0 collective-permute-start.6
  14.8 1.7 %collective-permute-start.7 = (f32[4,8,8,128]{3,2,1,0:T(8,128)S(1)}, f32[4,8,8,128]{3,2,1,0:T(8,128)S(1)}, u32[]{:S(2)}, u32[]{:S(2)}) collective-permute-start(f32[4,8,8,128]{3,2,1,0:T(8,128)S(1)} %get-tuple-element.37), channel_id=1, source_target_pairs={{0,12},{4,0},{8,4},{12,8},{1,13},{5,1},{9,5},{13,9},{2,14},{6,2},{... | collective-permute-start | bytes 393224 | tf_op jit(solution)/shard_map/ppermute | solution.py:503
  16.5 1.5 %collective-permute-start.8 = (f32[4,16,128]{2,1,0:T(8,128)S(1)}, f32[4,16,128]{2,1,0:T(8,128)S(1)}, u32[]{:S(2)}, u32[]{:S(2)}) collective-permute-start(f32[4,16,128]{2,1,0:T(8,128)S(1)} %get-tuple-element.34.columns_sent), channel_id=1, source_target_pairs={{0,1},{1,2},{2,3},{3,0},{4,5},{5,6},{6,7},{7,4},{8,9},{9,10},{10,1... | collective-permute-start | bytes 98312 | tf_op jit(solution)/shard_map/ppermute | solution.py:503
  18.0 2.3 %collective-permute-start.9 = (f32[4,16,128]{2,1,0:T(8,128)S(1)}, f32[4,16,128]{2,1,0:T(8,128)S(1)}, u32[]{:S(2)}, u32[]{:S(2)}) collective-permute-start(f32[4,16,128]{2,1,0:T(8,128)S(1)} %get-tuple-element.34.columns_sent), channel_id=1, source_target_pairs={{0,3},{1,0},{2,1},{3,2},{4,7},{5,4},{6,5},{7,6},{8,11},{9,8},{10,9... | collective-permute-start | bytes 98312 | tf_op jit(solution)/shard_map/ppermute | solution.py:503
  21.0 1.4 %shard_map.62.part = f32[4,16,16,128]{3,2,1,0:T(8,128)S(1)} custom-call(f32[4,16,16,128]{3,2,1,0:T(8,128)S(1)} %get-tuple-element.32.middle, f32[4,16,16,128]{3,2,1,0:T(8,128)S(1)} %get-tuple-element.23.state, f32[3,16,16,128]{3,2,1,0:T(8,128)S(1)} %get-tuple-element.24.velocity, bf16[256,256]{1,0:T(8,128)(2,1)S(1)} %get-tuple-element.33.inner_weight, ...), custom_call_target="tpu_custom_call" | custom-call | tf_op jit(solution)/shard_map/pallas_call | solution.py:526
  22.4 0.0 collective-permute-done.8.column_below
  22.4 0.0 collective-permute-done.9.column_above
  22.4 0.0 collective-permute-done.6.row_below
  22.4 0.0 collective-permute-done.7.row_above
  22.5 0.0 collective-permute-done.5.depth_halo
  22.5 2.8 %shard_map.63 = (f32[16,16,128]{2,1,0:T(8,128)S(1)}, f32[4,32,128]{2,1,0:T(8,128)S(1)}, s32[8,128]{1,0:T(8,128)S(1)}) custom-call(s32[1,1]{1,0:T(1,128)S(6)} %copy.6.order, f32[4,16,16,128]{3,2,1,0:T(8,128)S(1)} %shard_map.62.part, f32[3,16,16,128]{3,2,1,0:T(8,128)S(1)} %get-tuple-element.24.velocity, ...), custom_call_target="tpu_custom_call" | custom-call | tf_op jit(solution)/shard_map/pallas_call | solution.py:526
  25.3 1.6 %collective-permute-start.10 = (f32[4,32,128]{2,1,0:T(8,128)S(1)}, f32[4,32,128]{2,1,0:T(8,128)S(1)}, u32[]{:S(2)}, u32[]{:S(2)}) collective-permute-start(f32[4,32,128]{2,1,0:T(8,128)S(1)} %get-tuple-element.42.share.own), channel_id=1, source_target_pairs={{0,16},{16,0},{1,17},{17,1},{2,18},{18,2},{3,19},{19,3},{4,20},{20... | collective-permute-start | bytes 196616 | tf_op jit(solution)/shard_map/ppermute | solution.py:644
  26.9 1.6 %shard_map.64 = f32[4,16,16,128]{3,2,1,0:T(8,128)} custom-call(f32[4,16,16,128]{3,2,1,0:T(8,128)S(1)} %shard_map.62.part, f32[16,16,128]{2,1,0:T(8,128)S(1)} %get-tuple-element.41.temperature, f32[3,16,16,128]{3,2,1,0:T(8,128)S(1)} %get-tuple-element.24.velocity, f32[4,8,16,128]{3,2,1,0:T(8,128)S(1)} %collective-permute-done.5.depth_halo, ...), custom_call_target="tpu_custom_call" | custom-call | tf_op jit(solution)/shard_map/pallas_call | solution.py:526
  28.5 1.1 %collective-permute-done.10.received = f32[4,32,128]{2,1,0:T(8,128)S(1)} collective-permute-done((f32[4,32,128]{2,1,0:T(8,128)S(1)}, f32[4,32,128]{2,1,0:T(8,128)S(1)}, u32[]{:S(2)}, u32[]{:S(2)}) %collective-permute-start.10) | collective-permute-done | bytes 65568 | tf_op jit(solution)/shard_map/ppermute | solution.py:644
  29.6 0.8 %shard_map.65 = f32[4,64,64]{2,1,0:T(8,128)} custom-call(s32[8,128]{1,0:T(8,128)S(1)} %get-tuple-element.43.toward, f32[4,32,128]{2,1,0:T(8,128)S(1)} %get-tuple-element.42.share.own, f32[4,32,128]{2,1,0:T(8,128)S(1)} %collective-permute-done.10.received), custom_call_target="tpu_custom_call" | custom-call | tf_op jit(solution)/shard_map/pallas_call | solution.py:526
Async XLA Ops:
  2.1 10.6 %collective-permute-start = (f32[4,8,16,128]{3,2,1,0:T(8,128)S(1)}, f32[4,8,16,128]{3,2,1,0:T(8,128)S(1)}, u32[]{:S(2)}, u32[]{:S(2)}) collective-permute-start(f32[4,8,16,128]{3,2,1,0:T(8,128)S(1)} %get-tuple-element.28), channel_id=1, source_target_pairs={{0,16},{16,0},{1,17},{17,1},{2,18},{18,2},{3,19},{19,3},{4,20},{20... | collective-permute-start | bytes 786440 | tf_op jit(solution)/shard_map/ppermute | solution.py:503
  5.2 7.6 %collective-permute-start.1 = (f32[4,8,8,128]{3,2,1,0:T(8,128)S(1)}, f32[4,8,8,128]{3,2,1,0:T(8,128)S(1)}, u32[]{:S(2)}, u32[]{:S(2)}) collective-permute-start(f32[4,8,8,128]{3,2,1,0:T(8,128)S(1)} %get-tuple-element.29), channel_id=1, source_target_pairs={{0,4},{4,8},{8,12},{12,0},{1,5},{5,9},{9,13},{13,1},{2,6},{6,10},{... | collective-permute-start | bytes 393224 | tf_op jit(solution)/shard_map/ppermute | solution.py:503
  5.2 7.6 %collective-permute-start.2 = (f32[4,8,8,128]{3,2,1,0:T(8,128)S(1)}, f32[4,8,8,128]{3,2,1,0:T(8,128)S(1)}, u32[]{:S(2)}, u32[]{:S(2)}) collective-permute-start(f32[4,8,8,128]{3,2,1,0:T(8,128)S(1)} %get-tuple-element.30), channel_id=1, source_target_pairs={{0,12},{4,0},{8,4},{12,8},{1,13},{5,1},{9,5},{13,9},{2,14},{6,2},{... | collective-permute-start | bytes 393224 | tf_op jit(solution)/shard_map/ppermute | solution.py:503
  6.9 5.8 %collective-permute-start.3 = (f32[4,16,128]{2,1,0:T(8,128)S(1)}, f32[4,16,128]{2,1,0:T(8,128)S(1)}, u32[]{:S(2)}, u32[]{:S(2)}) collective-permute-start(f32[4,16,128]{2,1,0:T(8,128)S(1)} %get-tuple-element.26.columns_sent), channel_id=1, source_target_pairs={{0,1},{1,2},{2,3},{3,0},{4,5},{5,6},{6,7},{7,4},{8,9},{9,10},{10,1... | collective-permute-start | bytes 98312 | tf_op jit(solution)/shard_map/ppermute | solution.py:503
  8.5 4.3 %collective-permute-start.4 = (f32[4,16,128]{2,1,0:T(8,128)S(1)}, f32[4,16,128]{2,1,0:T(8,128)S(1)}, u32[]{:S(2)}, u32[]{:S(2)}) collective-permute-start(f32[4,16,128]{2,1,0:T(8,128)S(1)} %get-tuple-element.26.columns_sent), channel_id=1, source_target_pairs={{0,3},{1,0},{2,1},{3,2},{4,7},{5,4},{6,5},{7,6},{8,11},{9,8},{10,9... | collective-permute-start | bytes 98312 | tf_op jit(solution)/shard_map/ppermute | solution.py:503
  14.2 8.3 %collective-permute-start.5 = (f32[4,8,16,128]{3,2,1,0:T(8,128)S(1)}, f32[4,8,16,128]{3,2,1,0:T(8,128)S(1)}, u32[]{:S(2)}, u32[]{:S(2)}) collective-permute-start(f32[4,8,16,128]{3,2,1,0:T(8,128)S(1)} %get-tuple-element.35), channel_id=1, source_target_pairs={{0,16},{16,0},{1,17},{17,1},{2,18},{18,2},{3,19},{19,3},{4,20},{20... | collective-permute-start | bytes 786440 | tf_op jit(solution)/shard_map/ppermute | solution.py:503
  14.8 7.7 %collective-permute-start.6 = (f32[4,8,8,128]{3,2,1,0:T(8,128)S(1)}, f32[4,8,8,128]{3,2,1,0:T(8,128)S(1)}, u32[]{:S(2)}, u32[]{:S(2)}) collective-permute-start(f32[4,8,8,128]{3,2,1,0:T(8,128)S(1)} %get-tuple-element.36), channel_id=1, source_target_pairs={{0,4},{4,8},{8,12},{12,0},{1,5},{5,9},{9,13},{13,1},{2,6},{6,10},{... | collective-permute-start | bytes 393224 | tf_op jit(solution)/shard_map/ppermute | solution.py:503
  14.8 7.7 %collective-permute-start.7 = (f32[4,8,8,128]{3,2,1,0:T(8,128)S(1)}, f32[4,8,8,128]{3,2,1,0:T(8,128)S(1)}, u32[]{:S(2)}, u32[]{:S(2)}) collective-permute-start(f32[4,8,8,128]{3,2,1,0:T(8,128)S(1)} %get-tuple-element.37), channel_id=1, source_target_pairs={{0,12},{4,0},{8,4},{12,8},{1,13},{5,1},{9,5},{13,9},{2,14},{6,2},{... | collective-permute-start | bytes 393224 | tf_op jit(solution)/shard_map/ppermute | solution.py:503
  16.5 5.9 %collective-permute-start.8 = (f32[4,16,128]{2,1,0:T(8,128)S(1)}, f32[4,16,128]{2,1,0:T(8,128)S(1)}, u32[]{:S(2)}, u32[]{:S(2)}) collective-permute-start(f32[4,16,128]{2,1,0:T(8,128)S(1)} %get-tuple-element.34.columns_sent), channel_id=1, source_target_pairs={{0,1},{1,2},{2,3},{3,0},{4,5},{5,6},{6,7},{7,4},{8,9},{9,10},{10,1... | collective-permute-start | bytes 98312 | tf_op jit(solution)/shard_map/ppermute | solution.py:503
  18.0 4.4 %collective-permute-start.9 = (f32[4,16,128]{2,1,0:T(8,128)S(1)}, f32[4,16,128]{2,1,0:T(8,128)S(1)}, u32[]{:S(2)}, u32[]{:S(2)}) collective-permute-start(f32[4,16,128]{2,1,0:T(8,128)S(1)} %get-tuple-element.34.columns_sent), channel_id=1, source_target_pairs={{0,3},{1,0},{2,1},{3,2},{4,7},{5,4},{6,5},{7,6},{8,11},{9,8},{10,9... | collective-permute-start | bytes 98312 | tf_op jit(solution)/shard_map/ppermute | solution.py:503
  25.3 4.3 %collective-permute-start.10 = (f32[4,32,128]{2,1,0:T(8,128)S(1)}, f32[4,32,128]{2,1,0:T(8,128)S(1)}, u32[]{:S(2)}, u32[]{:S(2)}) collective-permute-start(f32[4,32,128]{2,1,0:T(8,128)S(1)} %get-tuple-element.42.share.own), channel_id=1, source_target_pairs={{0,16},{16,0},{1,17},{17,1},{2,18},{18,2},{3,19},{19,3},{4,20},{20... | collective-permute-start | bytes 196616 | tf_op jit(solution)/shard_map/ppermute | solution.py:644

commit v3 on v2

--- a/solution.py
+++ b/solution.py
@@ -44,43 +44,67 @@
     return result
 
 
-def pack_field(source, field, depth_out, low_out, high_out, column_out):
-    _, depth, rows, columns = source.shape
+def pack_rows(layers, low_out, high_out):
+    depth, rows, _ = layers.shape
     half = depth // 2
-    depth_out[field, 0:HALO] = source[field, depth - HALO : depth]
-    depth_out[field, HALO : 2 * HALO] = source[field, 0:HALO]
     for d in range(half):
-        low_out[field, d, 0:HALO] = source[field, d, 0:HALO]
-        low_out[field, d, HALO : 2 * HALO] = source[field, d + half, 0:HALO]
-        high_out[field, d, 0:HALO] = source[field, d, rows - HALO : rows]
-        high_out[field, d, HALO : 2 * HALO] = source[field, d + half, rows - HALO : rows]
+        low_out[d, 0:HALO] = layers[d, 0:HALO]
+        low_out[d, HALO : 2 * HALO] = layers[d + half, 0:HALO]
+        high_out[d, 0:HALO] = layers[d, rows - HALO : rows]
+        high_out[d, HALO : 2 * HALO] = layers[d + half, rows - HALO : rows]
+
+
+def pack_columns(layers, out):
+    depth, rows, columns = layers.shape
     lane = lax.broadcasted_iota(jnp.int32, (rows, columns), 1)
     packed = jnp.zeros((rows, columns), F32)
     for d in range(depth):
-        turned = pltpu.roll(source[field, d], (2 * HALO * d + HALO) % columns, 1)
+        turned = pltpu.roll(layers[d], (2 * HALO * d + HALO) % columns, 1)
         packed = jnp.where(lane // (2 * HALO) == d, turned, packed)
-    column_out[field] = packed
+    out[...] = packed
+
+
+def pack_field(source, field, depth_out, low_out, high_out, column_out):
+    depth = source.shape[1]
+    depth_out[field, 0:HALO] = source[field, depth - HALO : depth]
+    depth_out[field, HALO : 2 * HALO] = source[field, 0:HALO]
+    pack_rows(source.at[field], low_out.at[field], high_out.at[field])
+    pack_columns(source.at[field], column_out.at[field])
 
 
 def pack_kernel(
-    state_in, velocity_in, table_in, depth_out, low_out, high_out, column_out, state, velocity, table, sems
+    state_in,
+    velocity_in,
+    table_in,
+    depth_out,
+    low_out,
+    high_out,
+    column_out,
+    state,
+    velocity,
+    table,
+    sems,
 ):
+    fields, depth = state.shape[:2]
+    outer = depth - HALO
+    pairs = [(state_in.at[field], state.at[field]) for field in range(fields)]
+    pairs += [
+        (state_in.at[:, outer:depth], depth_out.at[:, 0:HALO]),
+        (state_in.at[:, 0:HALO], depth_out.at[:, HALO : 2 * HALO]),
+        (velocity_in, velocity),
+        (table_in, table),
+    ]
     copies = [
         pltpu.make_async_copy(source, target, sems.at[i])
-        for i, (source, target) in enumerate(
-            ((state_in, state), (velocity_in, velocity), (table_in, table))
-        )
+        for i, (source, target) in enumerate(pairs)
     ]
     for copy in copies:
         copy.start()
-    copies[0].wait()
-
-    def each(field, carry):
-        pack_field(state, field, depth_out, low_out, high_out, column_out)
-        return carry
-
-    lax.fori_loop(0, state.shape[0], each, 0)
-    for copy in copies[1:]:
+    for field in range(fields):
+        copies[field].wait()
+        pack_rows(state.at[field], low_out.at[field], high_out.at[field])
+        pack_columns(state.at[field], column_out.at[field])
+    for copy in copies[fields:]:
         copy.wait()
 
 
@@ -93,9 +117,9 @@
     )
 
 
-def band(cells, columns):
+def band(cells, targets, columns):
     lane = lax.broadcasted_iota(jnp.int32, cells.shape, 1)
-    apart = cells - lane % columns
+    apart = cells - targets
     distance = jnp.abs(apart)
     first = jnp.zeros(cells.shape, F32)
     second = jnp.zeros(cells.shape, F32)
@@ -148,69 +172,91 @@
         write(d, diffusivity * laplace - advect + source * rate[d])
 
 
-def halo_field(part, field, velocity, halos, halo_weight, below, above, across, scale, write):
+def halo_fields(part, fields, velocity, edge_velocity, halos, halo_weight, scale, write):
     depth_halo, row_below, row_above, column_below, column_above = halos
+    low_velocity, high_velocity, column_velocity = edge_velocity
     depth, rows, columns = velocity.shape[1:]
     half = depth // 2
+    block = 2 * HALO
     lane = lax.broadcasted_iota(jnp.int32, (rows, columns), 1)
-    edge = jnp.where(lane % (2 * HALO) < HALO, column_below[field], column_above[field])
-    edge_upper, edge_lower = halves(edge)
-    spread = []
-    for d in range(depth):
-        own = lane // (2 * HALO) == d
-        zero = jnp.zeros((rows, columns), BF16)
-        spread.append(
-            jnp.concatenate(
-                [jnp.where(own, edge_upper, zero), jnp.where(own, edge_lower, zero)], 1
+    behind_lane = lane % block < HALO
+    edges = jnp.concatenate(
+        [jnp.where(behind_lane, column_below[f], column_above[f]) for f in fields], 0
+    )
+    upper, lower = halves(edges)
+    along = jnp.dot(
+        jnp.concatenate([upper, lower], 1), halo_weight[...], preferred_element_type=F32
+    )
+    along_columns = []
+    for n, field in enumerate(fields):
+        mine = along[n * rows : (n + 1) * rows]
+        along_columns.append(
+            mine[:, columns:] * (scale * DIFFUSIVITY[field] / SECOND_SCALE)
+            - (column_velocity[...] * (scale / FIRST_SCALE)) * mine[:, :columns]
+        )
+
+    tile = (block, columns)
+    sublane = lax.broadcasted_iota(jnp.int32, tile, 0)
+    lane = lax.broadcasted_iota(jnp.int32, tile, 1)
+    outer_lane = (lane < HALO) | (lane >= columns - HALO)
+    early = sublane < HALO
+    step = sublane % HALO
+    below_first, below_second, above_first, above_second = [], [], [], []
+    for s in range(HALO):
+        first, second = FIRST_COEF[HALO - 1 - s], SECOND_COEF[HALO - 1 - s]
+        below_first.append(jnp.where(step + s < HALO, -scale * first, 0.0))
+        below_second.append(jnp.where(step + s < HALO, scale * second, 0.0))
+        above_first.append(jnp.where(step >= s, scale * first, 0.0))
+        above_second.append(jnp.where(step >= s, scale * second, 0.0))
+
+    def edge_rows(halo, direction, first_weights, second_weights, speed, diffusivity):
+        first = second = None
+        for s in range(HALO):
+            turned = halo if s == 0 else pltpu.roll(halo, (direction * s) % block, 0)
+            one, two = first_weights[s] * turned, second_weights[s] * turned
+            first = one if first is None else first + one
+            second = two if second is None else second + two
+        return diffusivity * second - speed * first
+
+    for n, field in enumerate(fields):
+        diffusivity = DIFFUSIVITY[field]
+        for i in range(half):
+            low = edge_rows(
+                row_below[field, i], -1, below_first, below_second, low_velocity[i], diffusivity
             )
-        )
-    across[...] = jnp.dot(
-        jnp.concatenate(spread, 0), halo_weight[...], preferred_element_type=F32
-    )
-    for d in range(depth):
-        piece = slice(0, HALO) if d < half else slice(HALO, 2 * HALO)
-        below[d, HALO : 2 * HALO] = row_below[field, d % half, piece]
-        above[d, 2 * HALO : 3 * HALO] = row_above[field, d % half, piece]
-    diffusivity = by_field(field, DIFFUSIVITY)
-    block = 2 * HALO
-    for d in range(depth):
-        value = []
-        for first in range(0, rows, block):
-            here = slice(first, first + block)
-            along_column = across[pl.ds(d * rows + first, block), 0:columns] * (1.0 / FIRST_SCALE)
-            laplace = across[pl.ds(d * rows + first, block), columns : 2 * columns] * (
-                1.0 / SECOND_SCALE
+            high = edge_rows(
+                row_above[field, i], 1, above_first, above_second, high_velocity[i], diffusivity
             )
-            advect = velocity[2, d, here] * along_column
-            along_row = None
-            for k in range(HALO):
-                if first == 0:
-                    down = below[d, block - k - 1 : 2 * block - k - 1]
-                    term = -FIRST_COEF[k] * down
-                    along_row = term if along_row is None else along_row + term
-                    laplace = laplace + SECOND_COEF[k] * down
-                if first + block == rows:
-                    up = above[d, k + 1 : k + 1 + block]
-                    term = FIRST_COEF[k] * up
-                    along_row = term if along_row is None else along_row + term
-                    laplace = laplace + SECOND_COEF[k] * up
-            if along_row is not None:
-                advect = advect + velocity[1, d, here] * along_row
-            along_depth = None
-            for k in range(HALO):
-                if d - k - 1 < 0:
-                    behind = depth_halo[field, d - k - 1 + HALO, here]
-                    term = -FIRST_COEF[k] * behind
-                    along_depth = term if along_depth is None else along_depth + term
-                    laplace = laplace + SECOND_COEF[k] * behind
-                if d + k + 1 >= depth:
-                    ahead = depth_halo[field, d + k + 1 - depth + HALO, here]
-                    term = FIRST_COEF[k] * ahead
-                    along_depth = term if along_depth is None else along_depth + term
-                    laplace = laplace + SECOND_COEF[k] * ahead
-            if along_depth is not None:
-                advect = advect + velocity[0, d, here] * along_depth
-            write(d, here, part[field, d, here] + scale * (diffusivity * laplace - advect))
+            for d in (i, i + half):
+                low_here = low if d < half else pltpu.roll(low, HALO, 0)
+                high_here = pltpu.roll(high, HALO, 0) if d < half else high
+                for first_row in range(0, rows, block):
+                    here = slice(first_row, first_row + block)
+                    value = part[field, d, here]
+                    if first_row == 0:
+                        value = value + jnp.where(early, low_here, 0.0)
+                    if first_row + block == rows:
+                        value = value + jnp.where(early, 0.0, high_here)
+                    turned = pltpu.roll(
+                        along_columns[n][here], (-block * d - HALO) % columns, 1
+                    )
+                    value = value + jnp.where(outer_lane, turned, 0.0)
+                    terms = [(-1, d - k - 1 + HALO, k) for k in range(HALO) if d - k - 1 < 0]
+                    terms += [
+                        (1, d + k + 1 - depth + HALO, k)
+                        for k in range(HALO)
+                        if d + k + 1 >= depth
+                    ]
+                    first = second = None
+                    for sign, layer, k in terms:
+                        cells = depth_halo[field, layer, here]
+                        one = (sign * scale * FIRST_COEF[k]) * cells
+                        two = (scale * diffusivity * SECOND_COEF[k]) * cells
+                        first = one if first is None else first + one
+                        second = two if second is None else second + two
+                    if terms:
+                        value = value + (second - velocity[0, d, here] * first)
+                    write(field, d, here, value)
 
 
 def first_interior(
@@ -225,6 +271,9 @@
     row_weight,
     column_weight,
     packed_table,
+    low_velocity,
+    high_velocity,
+    column_velocity,
     rate,
     padded,
     across,
@@ -233,9 +282,18 @@
     _, depth, rows, columns = state.shape
     shape = inner_weight.shape
     index = lax.broadcasted_iota(jnp.int32, shape, 0) % columns
-    inner_weight[...] = band(index, columns)
-    edge = index % (2 * HALO)
-    halo_weight[...] = band(jnp.where(edge < HALO, edge, edge + columns) - HALO, columns)
+    target = lax.broadcasted_iota(jnp.int32, shape, 1) % columns
+    inner_weight[...] = band(index, target, columns)
+    edge, target_edge = index % (2 * HALO), target % (2 * HALO)
+    weight = band(
+        jnp.where(edge < HALO, edge, edge + columns) - HALO,
+        jnp.where(target_edge < HALO, target_edge + columns, target_edge) - HALO,
+        columns,
+    )
+    same_layer = index // (2 * HALO) == target // (2 * HALO)
+    halo_weight[...] = jnp.where(same_layer, weight, jnp.zeros_like(weight))
+    pack_rows(velocity.at[1], low_velocity, high_velocity)
+    pack_columns(velocity.at[2], column_velocity)
     shape = column_weight.shape
     cell = (lax.broadcasted_iota(jnp.int32, shape, 0) % columns).astype(F32)
     pixel = (lax.broadcasted_iota(jnp.int32, shape, 1) % PIX_C).astype(F32)
@@ -271,6 +329,9 @@
 def first_halo(
     part,
     velocity,
+    low_velocity,
+    high_velocity,
+    column_velocity,
     depth_halo,
     row_below,
     row_above,
@@ -282,25 +343,17 @@
     low_out,
     high_out,
     column_out,
-    below,
-    above,
-    across,
 ):
     halos = (depth_halo, row_below, row_above, column_below, column_above)
-    below[...] = jnp.zeros_like(below)
-    above[...] = jnp.zeros_like(above)
-
-    def each(field, carry):
-        def write(d, here, value):
-            middle[field, d, here] = value
-
-        halo_field(
-            part, field, velocity, halos, halo_weight, below, above, across, TIME_STEP, write
-        )
+    edge_velocity = (low_velocity, high_velocity, column_velocity)
+
+    def write(field, d, here, value):
+        middle[field, d, here] = value
+
+    fields = range(part.shape[0])
+    halo_fields(part, fields, velocity, edge_velocity, halos, halo_weight, TIME_STEP, write)
+    for field in fields:
         pack_field(middle, field, depth_out, low_out, high_out, column_out)
-        return carry
-
-    lax.fori_loop(0, part.shape[0], each, 0)
 
 
 def second_interior(
@@ -352,7 +405,7 @@
 
 def look_up(tables, index, shape):
     lanes = tables[0].shape[1]
-    inside = index % lanes
+    inside = index & (lanes - 1)
     result = None
     for part, table in enumerate(tables):
         found = jnp.take_along_axis(
@@ -376,27 +429,31 @@
 
         def advance(position, running):
             chosen = jnp.where(flag == 0, half - 1 - position, position)
-            values = samples[chosen, rows_here]
-            level = jnp.clip(values, 0.0, 1.0) * (levels - 1.0)
-            lower = jnp.minimum(level.astype(jnp.int32), levels - 2)
+            level = jnp.clip(samples[chosen, rows_here] * (levels - 1.0), 0.0, levels - 1.0)
+            lower = level.astype(jnp.int32)
             fraction = level - lower.astype(F32)
             below = look_up(below_tables, lower, shape)
             above = look_up(above_tables, lower, shape)
             raw = []
             for channel in range(4):
-                low = (lax.shift_right_logical(below, 8 * channel) & 255).astype(F32)
-                high = (lax.shift_right_logical(above, 8 * channel) & 255).astype(F32)
+                low, high = below, above
+                if channel > 0:
+                    low = lax.shift_right_logical(low, 8 * channel)
+                    high = lax.shift_right_logical(high, 8 * channel)
+                if channel < 3:
+                    low, high = low & 255, high & 255
+                low, high = low.astype(F32), high.astype(F32)
                 raw.append(low + fraction * (high - low))
             alpha = raw[3] * (OPACITY_TOTAL / slice_total / 255.0)
-            scaled = alpha * (1.0 / 255.0)
             through = 1.0 - alpha
             return tuple(
-                [scaled * raw[c] + through * running[c] for c in range(3)]
+                [alpha * raw[c] + through * running[c] for c in range(3)]
                 + [alpha + through * running[3]]
             )
 
         zero = jnp.zeros(shape, F32)
-        parts.append(lax.fori_loop(0, half, advance, (zero, zero, zero, zero)))
+        running = lax.fori_loop(0, half, advance, (zero, zero, zero, zero), unroll=True)
+        parts.append([value * (1.0 / 255.0) for value in running[:3]] + [running[3]])
     for channel in range(4):
         merged = []
         for part in range(2):
@@ -415,6 +472,9 @@
     order,
     part,
     velocity,
+    low_velocity,
+    high_velocity,
+    column_velocity,
     depth_halo,
     row_below,
     row_above,
@@ -427,21 +487,15 @@
     temperature,
     share,
     toward,
-    below,
-    above,
-    across,
     samples,
 ):
     halos = (depth_halo, row_below, row_above, column_below, column_above)
-    below[...] = jnp.zeros_like(below)
-    above[...] = jnp.zeros_like(above)
-
-    def write(d, here, value):
+    edge_velocity = (low_velocity, high_velocity, column_velocity)
+
+    def write(field, d, here, value):
         temperature[d, here] = value
 
-    halo_field(
-        part, 3, velocity, halos, halo_weight, below, above, across, 0.5 * TIME_STEP, write
-    )
+    halo_fields(part, [3], velocity, edge_velocity, halos, halo_weight, 0.5 * TIME_STEP, write)
     sample_slices(temperature, column_weight, row_weight, samples)
     toward[...] = jnp.full(toward.shape, order[0, 0], jnp.int32)
     march(samples, table, order[0, 0], slice_total, share)
@@ -451,6 +505,9 @@
     part,
     temperature,
     velocity,
+    low_velocity,
+    high_velocity,
+    column_velocity,
     depth_halo,
     row_below,
     row_above,
@@ -459,25 +516,17 @@
     halo_weight,
     share,
     new_state,
-    below,
-    above,
-    across,
 ):
     del share
     halos = (depth_halo, row_below, row_above, column_below, column_above)
-    below[...] = jnp.zeros_like(below)
-    above[...] = jnp.zeros_like(above)
-
-    def each(field, carry):
-        def write(d, here, value):
-            new_state[field, d, here] = value
-
-        halo_field(
-            part, field, velocity, halos, halo_weight, below, above, across, 0.5 * TIME_STEP, write
-        )
-        return carry
-
-    lax.fori_loop(0, 3, each, 0)
+    edge_velocity = (low_velocity, high_velocity, column_velocity)
+
+    def write(field, d, here, value):
+        new_state[field, d, here] = value
+
+    halo_fields(
+        part, range(3), velocity, edge_velocity, halos, halo_weight, 0.5 * TIME_STEP, write
+    )
     new_state[3] = temperature[...]
 
 
@@ -551,31 +600,26 @@
         array(fields, depth // 2, 2 * HALO, columns),
         array(fields, rows, columns),
     )
-    across = pltpu.VMEM((depth * rows, 2 * columns), F32)
     inner_work = [
         pltpu.VMEM((depth, rows, columns), F32),
         pltpu.VMEM((depth, rows + 4 * HALO, columns), F32),
-        across,
+        pltpu.VMEM((depth * rows, 2 * columns), F32),
     ]
-    halo_work = [
-        pltpu.VMEM((depth, 4 * HALO, columns), F32),
-        pltpu.VMEM((depth, 4 * HALO, columns), F32),
-        across,
-    ]
+    edge_rows = array(depth // 2, 2 * HALO, columns)
     slice_total = depth * depth_count
 
     hbm = pl.BlockSpec(memory_space=pltpu.HBM)
     *sent, state, velocity, table = call(
         pack_kernel,
         faces + (whole, array(*velocity.shape), array(*tf_table.shape, dtype=jnp.int32)),
-        [pltpu.SemaphoreType.DMA((3,))],
+        [pltpu.SemaphoreType.DMA((fields + 4,))],
         [hbm, hbm, hbm],
         in_hbm(state),
         in_hbm(velocity),
         in_hbm(tf_table),
     )
     halos = exchange(*sent)
-    part, inner_weight, halo_weight, row_weight, column_weight, table = call(
+    part, inner_weight, halo_weight, row_weight, column_weight, table, *edge_velocity = call(
         functools.partial(first_interior, slice_total),
         (
             whole,
@@ -584,6 +628,9 @@
             array(depth // 2, PIX_R, 4 * rows, dtype=BF16),
             array(2 * columns, 2 * PIX_C, dtype=BF16),
             array(2, tf_table.shape[1], dtype=jnp.int32),
+            edge_rows,
+            edge_rows,
+            array(rows, columns),
         ),
         inner_work,
         [],
@@ -593,7 +640,15 @@
         sent[3],
     )
     middle, *sent = call(
-        first_halo, (whole,) + faces, halo_work, [], part, velocity, *halos, halo_weight
+        first_halo,
+        (whole,) + faces,
+        [],
+        [],
+        part,
+        velocity,
+        *edge_velocity,
+        *halos,
+        halo_weight,
     )
     halos = exchange(*sent)
     part = call(
@@ -614,12 +669,12 @@
             array(4, PIX_R // 2, 2 * PIX_C),
             array(8, 2 * PIX_C, dtype=jnp.int32),
         ),
-        halo_work
-        + [pltpu.VMEM((depth // 2, PIX_R, 2 * PIX_C), F32)],
+        [pltpu.VMEM((depth // 2, PIX_R, 2 * PIX_C), F32)],
         [pl.BlockSpec(memory_space=pltpu.SMEM)],
         view_order,
         part,
         velocity,
+        *edge_velocity,
         *halos,
         halo_weight,
         column_weight,
@@ -629,11 +684,12 @@
     new_state = call(
         fractions_halo,
         whole,
-        halo_work,
+        [],
         [],
         part,
         temperature,
         velocity,
+        *edge_velocity,
         *halos,
         halo_weight,
         share,

time: 30.6 us -> 28.4 us (0.928)
  Pallas kernels: 11.3 us -> 9.01 us
    pallas_call x7, Pallas kernels: 11.3 us -> 9.01 us  [call(): pl.pallas_call(kernel, out_shape=outs, in_specs=specs + [vmem] * (len(arg...]
    ppermute x1, waiting for transfers between devices: 1.14 us -> 1.48 us  [local(): received = lax.ppermute(share, 'depth', pairs)]
  transfers between devices with their start and end apart: 11 -> 11, of which waited for: 2 -> 1; matrix products, arithmetic and copies ran while one was open for 0% -> 0% of each run, Pallas kernels for 16% -> 17%
where the time goes in v3:
time: 28.4 us; the launch traced here: 28.2 us
  starting transfers between devices  16.3 us (57%)
  Pallas kernels  9.01 us (32%)
  waiting for transfers between devices  1.51 us (5%)
  between operations  1.4 us (5%)
    ppermute x10, starting transfers between devices, shift(): lax.ppermute(value, axis, [(i, (i + step) % count) for i in range(count)])  14.7 us
    pallas_call x7, Pallas kernels, call(): pl.pallas_call(kernel, out_shape=outs, in_specs=specs + [vmem] * (len(arg...  9.01 us
    ppermute x1, starting transfers between devices, local(): received = lax.ppermute(share, 'depth', pairs)  1.65 us
    ppermute x1, waiting for transfers between devices, local(): received = lax.ppermute(share, 'depth', pairs)  1.48 us
  transfers between devices with their start and end apart: 11, of which 1 were waited for; matrix products, arithmetic and copies ran while one was open for 0% of the time, Pallas kernels for 17%

profile of v3, /device:TPU:0, one launch (start us, length us, event | category | flops | bytes accessed | tf_op | source)
XLA Modules:
  0.0 28.2 jit_solution(4227330490848788320)
XLA Ops:
  0.6 1.4 %shard_map.59 = (f32[4,8,16,128]{3,2,1,0:T(8,128)S(1)}, f32[4,8,8,128]{3,2,1,0:T(8,128)S(1)}, f32[4,8,8,128]{3,2,1,0:T(8,128)S(1)}, f32[4,16,128]{2,1,0:T(8,128)...) custom-call(f32[4,16,16,128]{3,2,1,0:T(8,128)} %state_in.1, ...), custom_call_target="tpu_custom_call" | custom-call | tf_op jit(solution)/shard_map/pallas_call | solution.py:575
  2.1 3.0 %collective-permute-start = (f32[4,8,16,128]{3,2,1,0:T(8,128)S(1)}, f32[4,8,16,128]{3,2,1,0:T(8,128)S(1)}, u32[]{:S(2)}, u32[]{:S(2)}) collective-permute-start(f32[4,8,16,128]{3,2,1,0:T(8,128)S(1)} %get-tuple-element.34), channel_id=1, source_target_pairs={{0,16},{16,0},{1,17},{17,1},{2,18},{18,2},{3,19},{19,3},{4,20},{20... | collective-permute-start | bytes 786440 | tf_op jit(solution)/shard_map/ppermute | solution.py:552
  5.1 0.0 collective-permute-start.1
  5.1 1.7 %collective-permute-start.2 = (f32[4,8,8,128]{3,2,1,0:T(8,128)S(1)}, f32[4,8,8,128]{3,2,1,0:T(8,128)S(1)}, u32[]{:S(2)}, u32[]{:S(2)}) collective-permute-start(f32[4,8,8,128]{3,2,1,0:T(8,128)S(1)} %get-tuple-element.36), channel_id=1, source_target_pairs={{0,12},{4,0},{8,4},{12,8},{1,13},{5,1},{9,5},{13,9},{2,14},{6,2},{... | collective-permute-start | bytes 393224 | tf_op jit(solution)/shard_map/ppermute | solution.py:552
  6.8 1.6 %collective-permute-start.3 = (f32[4,16,128]{2,1,0:T(8,128)S(1)}, f32[4,16,128]{2,1,0:T(8,128)S(1)}, u32[]{:S(2)}, u32[]{:S(2)}) collective-permute-start(f32[4,16,128]{2,1,0:T(8,128)S(1)} %get-tuple-element.29.columns_sent), channel_id=1, source_target_pairs={{0,1},{1,2},{2,3},{3,0},{4,5},{5,6},{6,7},{7,4},{8,9},{9,10},{10,1... | collective-permute-start | bytes 98312 | tf_op jit(solution)/shard_map/ppermute | solution.py:552
  8.4 2.2 %collective-permute-start.4 = (f32[4,16,128]{2,1,0:T(8,128)S(1)}, f32[4,16,128]{2,1,0:T(8,128)S(1)}, u32[]{:S(2)}, u32[]{:S(2)}) collective-permute-start(f32[4,16,128]{2,1,0:T(8,128)S(1)} %get-tuple-element.29.columns_sent), channel_id=1, source_target_pairs={{0,3},{1,0},{2,1},{3,2},{4,7},{5,4},{6,5},{7,6},{8,11},{9,8},{10,9... | collective-permute-start | bytes 98312 | tf_op jit(solution)/shard_map/ppermute | solution.py:552
  10.7 2.0 %shard_map.60 = (f32[4,16,16,128]{3,2,1,0:T(8,128)S(1)}, bf16[256,256]{1,0:T(8,128)(2,1)S(1)}, bf16[256,256]{1,0:T(8,128)(2,1)S(1)}, bf16[8,64,64]{2,1,0:T(8,128...) custom-call(f32[4,16,16,128]{3,2,1,0:T(8,128)S(1)} %get-tuple-elemen, ...), custom_call_target="tpu_custom_call" | custom-call | tf_op jit(solution)/shard_map/pallas_call | solution.py:575
  12.7 0.0 collective-permute-done.3.column_below
  12.7 0.0 collective-permute-done.4.column_above
  12.7 0.0 collective-permute-done.1.row_below
  12.8 0.0 collective-permute-done.2.row_above
  12.8 0.0 collective-permute-done.depth_halo
  12.8 0.7 %shard_map.61 = (f32[4,16,16,128]{3,2,1,0:T(8,128)S(1)}, f32[4,8,16,128]{3,2,1,0:T(8,128)S(1)}, f32[4,8,8,128]{3,2,1,0:T(8,128)S(1)}, f32[4,8,8,128]{3,2,1,0:T(8,128)S(1)}, f32[4,16,128]{2,1,0:T(8,128)S(1)}) custom-call(f32[4,16,16,128]{3,2,1,0:T(8,128)S(1)} %get-tuple-element.30.part, f32[3,16,16,128]{3,2,1,0:T(8,128)S(1)} %get-tuple-element.27.velocity, ...), custom_call_target="tpu_custom_call" | custom-call | tf_op jit(solution)/shard_map/pallas_call | solution.py:575
  13.5 0.5 %collective-permute-start.5 = (f32[4,8,16,128]{3,2,1,0:T(8,128)S(1)}, f32[4,8,16,128]{3,2,1,0:T(8,128)S(1)}, u32[]{:S(2)}, u32[]{:S(2)}) collective-permute-start(f32[4,8,16,128]{3,2,1,0:T(8,128)S(1)} %get-tuple-element.41), channel_id=1, source_target_pairs={{0,16},{16,0},{1,17},{17,1},{2,18},{18,2},{3,19},{19,3},{4,20},{20... | collective-permute-start | bytes 786440 | tf_op jit(solution)/shard_map/ppermute | solution.py:552
  14.0 0.0 collective-permute-start.6
  14.0 1.7 %collective-permute-start.7 = (f32[4,8,8,128]{3,2,1,0:T(8,128)S(1)}, f32[4,8,8,128]{3,2,1,0:T(8,128)S(1)}, u32[]{:S(2)}, u32[]{:S(2)}) collective-permute-start(f32[4,8,8,128]{3,2,1,0:T(8,128)S(1)} %get-tuple-element.43), channel_id=1, source_target_pairs={{0,12},{4,0},{8,4},{12,8},{1,13},{5,1},{9,5},{13,9},{2,14},{6,2},{... | collective-permute-start | bytes 393224 | tf_op jit(solution)/shard_map/ppermute | solution.py:552
  15.7 1.5 %collective-permute-start.8 = (f32[4,16,128]{2,1,0:T(8,128)S(1)}, f32[4,16,128]{2,1,0:T(8,128)S(1)}, u32[]{:S(2)}, u32[]{:S(2)}) collective-permute-start(f32[4,16,128]{2,1,0:T(8,128)S(1)} %get-tuple-element.40.columns_sent), channel_id=1, source_target_pairs={{0,1},{1,2},{2,3},{3,0},{4,5},{5,6},{6,7},{7,4},{8,9},{9,10},{10,1... | collective-permute-start | bytes 98312 | tf_op jit(solution)/shard_map/ppermute | solution.py:552
  17.2 2.3 %collective-permute-start.9 = (f32[4,16,128]{2,1,0:T(8,128)S(1)}, f32[4,16,128]{2,1,0:T(8,128)S(1)}, u32[]{:S(2)}, u32[]{:S(2)}) collective-permute-start(f32[4,16,128]{2,1,0:T(8,128)S(1)} %get-tuple-element.40.columns_sent), channel_id=1, source_target_pairs={{0,3},{1,0},{2,1},{3,2},{4,7},{5,4},{6,5},{7,6},{8,11},{9,8},{10,9... | collective-permute-start | bytes 98312 | tf_op jit(solution)/shard_map/ppermute | solution.py:552
  20.2 1.6 %shard_map.62.part = f32[4,16,16,128]{3,2,1,0:T(8,128)S(1)} custom-call(f32[4,16,16,128]{3,2,1,0:T(8,128)S(1)} %get-tuple-element.38.middle, f32[4,16,16,128]{3,2,1,0:T(8,128)S(1)} %get-tuple-element.26.state, f32[3,16,16,128]{3,2,1,0:T(8,128)S(1)} %get-tuple-element.27.velocity, bf16[256,256]{1,0:T(8,128)(2,1)S(1)} %get-tuple-element.39.inner_weight, ...), custom_call_target="tpu_custom_call" | custom-call | tf_op jit(solution)/shard_map/pallas_call | solution.py:575
  21.8 0.0 collective-permute-done.8.column_below
  21.8 0.0 collective-permute-done.9.column_above
  21.9 0.0 collective-permute-done.6.row_below
  21.9 0.0 collective-permute-done.7.row_above
  21.9 0.0 collective-permute-done.5.depth_halo
  21.9 1.3 %shard_map.63 = (f32[16,16,128]{2,1,0:T(8,128)S(1)}, f32[4,32,128]{2,1,0:T(8,128)S(1)}, s32[8,128]{1,0:T(8,128)S(1)}) custom-call(s32[1,1]{1,0:T(1,128)S(6)} %copy.6.order, f32[4,16,16,128]{3,2,1,0:T(8,128)S(1)} %shard_map.62.part, f32[3,16,16,128]{3,2,1,0:T(8,128)S(1)} %get-tuple-element.27.velocity, f32[8,8,128]{2,1,0:T(8,128)S(1)} %get-tuple-element.31.low_velocity, ...), custom_call_target="tpu_custom_call" | custom-call | tf_op jit(solution)/shard_map/pallas_call | solution.py:575
  23.2 1.7 %collective-permute-start.10 = (f32[4,32,128]{2,1,0:T(8,128)S(1)}, f32[4,32,128]{2,1,0:T(8,128)S(1)}, u32[]{:S(2)}, u32[]{:S(2)}) collective-permute-start(f32[4,32,128]{2,1,0:T(8,128)S(1)} %get-tuple-element.48.share.own), channel_id=1, source_target_pairs={{0,16},{16,0},{1,17},{17,1},{2,18},{18,2},{3,19},{19,3},{4,20},{20... | collective-permute-start | bytes 196616 | tf_op jit(solution)/shard_map/ppermute | solution.py:700
  24.8 1.2 %shard_map.64 = f32[4,16,16,128]{3,2,1,0:T(8,128)} custom-call(f32[4,16,16,128]{3,2,1,0:T(8,128)S(1)} %shard_map.62.part, f32[16,16,128]{2,1,0:T(8,128)S(1)} %get-tuple-element.47.temperature, f32[3,16,16,128]{3,2,1,0:T(8,128)S(1)} %get-tuple-element.27.velocity, f32[8,8,128]{2,1,0:T(8,128)S(1)} %get-tuple-element.31.low_velocity, ...), custom_call_target="tpu_custom_call" | custom-call | tf_op jit(solution)/shard_map/pallas_call | solution.py:575
  26.0 1.5 %collective-permute-done.10.received = f32[4,32,128]{2,1,0:T(8,128)S(1)} collective-permute-done((f32[4,32,128]{2,1,0:T(8,128)S(1)}, f32[4,32,128]{2,1,0:T(8,128)S(1)}, u32[]{:S(2)}, u32[]{:S(2)}) %collective-permute-start.10) | collective-permute-done | bytes 65568 | tf_op jit(solution)/shard_map/ppermute | solution.py:700
  27.5 0.8 %shard_map.65 = f32[4,64,64]{2,1,0:T(8,128)} custom-call(s32[8,128]{1,0:T(8,128)S(1)} %get-tuple-element.49.toward, f32[4,32,128]{2,1,0:T(8,128)S(1)} %get-tuple-element.48.share.own, f32[4,32,128]{2,1,0:T(8,128)S(1)} %collective-permute-done.10.received), custom_call_target="tpu_custom_call" | custom-call | tf_op jit(solution)/shard_map/pallas_call | solution.py:575
Async XLA Ops:
  2.1 10.7 %collective-permute-start = (f32[4,8,16,128]{3,2,1,0:T(8,128)S(1)}, f32[4,8,16,128]{3,2,1,0:T(8,128)S(1)}, u32[]{:S(2)}, u32[]{:S(2)}) collective-permute-start(f32[4,8,16,128]{3,2,1,0:T(8,128)S(1)} %get-tuple-element.34), channel_id=1, source_target_pairs={{0,16},{16,0},{1,17},{17,1},{2,18},{18,2},{3,19},{19,3},{4,20},{20... | collective-permute-start | bytes 786440 | tf_op jit(solution)/shard_map/ppermute | solution.py:552
  5.1 7.6 %collective-permute-start.1 = (f32[4,8,8,128]{3,2,1,0:T(8,128)S(1)}, f32[4,8,8,128]{3,2,1,0:T(8,128)S(1)}, u32[]{:S(2)}, u32[]{:S(2)}) collective-permute-start(f32[4,8,8,128]{3,2,1,0:T(8,128)S(1)} %get-tuple-element.35), channel_id=1, source_target_pairs={{0,4},{4,8},{8,12},{12,0},{1,5},{5,9},{9,13},{13,1},{2,6},{6,10},{... | collective-permute-start | bytes 393224 | tf_op jit(solution)/shard_map/ppermute | solution.py:552
  5.1 7.6 %collective-permute-start.2 = (f32[4,8,8,128]{3,2,1,0:T(8,128)S(1)}, f32[4,8,8,128]{3,2,1,0:T(8,128)S(1)}, u32[]{:S(2)}, u32[]{:S(2)}) collective-permute-start(f32[4,8,8,128]{3,2,1,0:T(8,128)S(1)} %get-tuple-element.36), channel_id=1, source_target_pairs={{0,12},{4,0},{8,4},{12,8},{1,13},{5,1},{9,5},{13,9},{2,14},{6,2},{... | collective-permute-start | bytes 393224 | tf_op jit(solution)/shard_map/ppermute | solution.py:552
  6.8 5.9 %collective-permute-start.3 = (f32[4,16,128]{2,1,0:T(8,128)S(1)}, f32[4,16,128]{2,1,0:T(8,128)S(1)}, u32[]{:S(2)}, u32[]{:S(2)}) collective-permute-start(f32[4,16,128]{2,1,0:T(8,128)S(1)} %get-tuple-element.29.columns_sent), channel_id=1, source_target_pairs={{0,1},{1,2},{2,3},{3,0},{4,5},{5,6},{6,7},{7,4},{8,9},{9,10},{10,1... | collective-permute-start | bytes 98312 | tf_op jit(solution)/shard_map/ppermute | solution.py:552
  8.4 4.3 %collective-permute-start.4 = (f32[4,16,128]{2,1,0:T(8,128)S(1)}, f32[4,16,128]{2,1,0:T(8,128)S(1)}, u32[]{:S(2)}, u32[]{:S(2)}) collective-permute-start(f32[4,16,128]{2,1,0:T(8,128)S(1)} %get-tuple-element.29.columns_sent), channel_id=1, source_target_pairs={{0,3},{1,0},{2,1},{3,2},{4,7},{5,4},{6,5},{7,6},{8,11},{9,8},{10,9... | collective-permute-start | bytes 98312 | tf_op jit(solution)/shard_map/ppermute | solution.py:552
  13.5 8.4 %collective-permute-start.5 = (f32[4,8,16,128]{3,2,1,0:T(8,128)S(1)}, f32[4,8,16,128]{3,2,1,0:T(8,128)S(1)}, u32[]{:S(2)}, u32[]{:S(2)}) collective-permute-start(f32[4,8,16,128]{3,2,1,0:T(8,128)S(1)} %get-tuple-element.41), channel_id=1, source_target_pairs={{0,16},{16,0},{1,17},{17,1},{2,18},{18,2},{3,19},{19,3},{4,20},{20... | collective-permute-start | bytes 786440 | tf_op jit(solution)/shard_map/ppermute | solution.py:552
  14.0 7.9 %collective-permute-start.6 = (f32[4,8,8,128]{3,2,1,0:T(8,128)S(1)}, f32[4,8,8,128]{3,2,1,0:T(8,128)S(1)}, u32[]{:S(2)}, u32[]{:S(2)}) collective-permute-start(f32[4,8,8,128]{3,2,1,0:T(8,128)S(1)} %get-tuple-element.42), channel_id=1, source_target_pairs={{0,4},{4,8},{8,12},{12,0},{1,5},{5,9},{9,13},{13,1},{2,6},{6,10},{... | collective-permute-start | bytes 393224 | tf_op jit(solution)/shard_map/ppermute | solution.py:552
  14.0 7.9 %collective-permute-start.7 = (f32[4,8,8,128]{3,2,1,0:T(8,128)S(1)}, f32[4,8,8,128]{3,2,1,0:T(8,128)S(1)}, u32[]{:S(2)}, u32[]{:S(2)}) collective-permute-start(f32[4,8,8,128]{3,2,1,0:T(8,128)S(1)} %get-tuple-element.43), channel_id=1, source_target_pairs={{0,12},{4,0},{8,4},{12,8},{1,13},{5,1},{9,5},{13,9},{2,14},{6,2},{... | collective-permute-start | bytes 393224 | tf_op jit(solution)/shard_map/ppermute | solution.py:552
  15.7 6.1 %collective-permute-start.8 = (f32[4,16,128]{2,1,0:T(8,128)S(1)}, f32[4,16,128]{2,1,0:T(8,128)S(1)}, u32[]{:S(2)}, u32[]{:S(2)}) collective-permute-start(f32[4,16,128]{2,1,0:T(8,128)S(1)} %get-tuple-element.40.columns_sent), channel_id=1, source_target_pairs={{0,1},{1,2},{2,3},{3,0},{4,5},{5,6},{6,7},{7,4},{8,9},{9,10},{10,1... | collective-permute-start | bytes 98312 | tf_op jit(solution)/shard_map/ppermute | solution.py:552
  17.2 4.6 %collective-permute-start.9 = (f32[4,16,128]{2,1,0:T(8,128)S(1)}, f32[4,16,128]{2,1,0:T(8,128)S(1)}, u32[]{:S(2)}, u32[]{:S(2)}) collective-permute-start(f32[4,16,128]{2,1,0:T(8,128)S(1)} %get-tuple-element.40.columns_sent), channel_id=1, source_target_pairs={{0,3},{1,0},{2,1},{3,2},{4,7},{5,4},{6,5},{7,6},{8,11},{9,8},{10,9... | collective-permute-start | bytes 98312 | tf_op jit(solution)/shard_map/ppermute | solution.py:552
  23.2 4.3 %collective-permute-start.10 = (f32[4,32,128]{2,1,0:T(8,128)S(1)}, f32[4,32,128]{2,1,0:T(8,128)S(1)}, u32[]{:S(2)}, u32[]{:S(2)}) collective-permute-start(f32[4,32,128]{2,1,0:T(8,128)S(1)} %get-tuple-element.48.share.own), channel_id=1, source_target_pairs={{0,16},{16,0},{1,17},{17,1},{2,18},{18,2},{3,19},{19,3},{4,20},{20... | collective-permute-start | bytes 196616 | tf_op jit(solution)/shard_map/ppermute | solution.py:700

commit v4 on v3

--- a/solution.py
+++ b/solution.py
@@ -37,13 +37,6 @@
     return upper, (value - upper.astype(F32)).astype(BF16)
 
 
-def by_field(field, values):
-    result = jnp.float32(values[-1])
-    for index in range(len(values) - 2, -1, -1):
-        result = jnp.where(field == index, jnp.float32(values[index]), result)
-    return result
-
-
 def pack_rows(layers, low_out, high_out):
     depth, rows, _ = layers.shape
     half = depth // 2
@@ -87,8 +80,8 @@
 ):
     fields, depth = state.shape[:2]
     outer = depth - HALO
-    pairs = [(state_in.at[field], state.at[field]) for field in range(fields)]
-    pairs += [
+    pairs = [
+        (state_in, state),
         (state_in.at[:, outer:depth], depth_out.at[:, 0:HALO]),
         (state_in.at[:, 0:HALO], depth_out.at[:, HALO : 2 * HALO]),
         (velocity_in, velocity),
@@ -100,11 +93,11 @@
     ]
     for copy in copies:
         copy.start()
+    copies[0].wait()
     for field in range(fields):
-        copies[field].wait()
         pack_rows(state.at[field], low_out.at[field], high_out.at[field])
         pack_columns(state.at[field], column_out.at[field])
-    for copy in copies[fields:]:
+    for copy in copies[1:]:
         copy.wait()
 
 
@@ -131,45 +124,50 @@
     return jnp.where(lane < columns, first, second).astype(BF16)
 
 
-def interior_field(fields, field, velocity, inner_weight, rate, padded, across, write):
-    _, depth, rows, columns = fields.shape
+def interior_fields(fields, velocity, inner_weight, rate, padded, across, write):
+    count, depth, rows, columns = fields.shape
     start = 2 * HALO
-    upper, lower = halves(fields[field].reshape(depth * rows, columns))
-    across[...] = jnp.dot(
-        jnp.concatenate([upper, lower], 1), inner_weight[...], preferred_element_type=F32
-    )
-    for d in range(depth):
-        padded[d, start : start + rows] = fields[field, d]
-    diffusivity = by_field(field, DIFFUSIVITY)
-    source = by_field(field, SOURCE_COEF)
-    for d in range(depth):
-        centre = fields[field, d]
-        laplace = 3.0 * CENTER_COEF * centre
-        along_depth = jnp.zeros_like(centre)
-        along_row = jnp.zeros_like(centre)
-        for k in range(HALO):
-            up = padded[d, start + k + 1 : start + k + 1 + rows]
-            down = padded[d, start - k - 1 : start - k - 1 + rows]
-            along_row = along_row + FIRST_COEF[k] * (up - down)
-            both = up + down
-            if d + k + 1 < depth:
-                ahead = fields[field, d + k + 1]
-                along_depth = along_depth + FIRST_COEF[k] * ahead
-                both = both + ahead
-            if d - k - 1 >= 0:
-                behind = fields[field, d - k - 1]
-                along_depth = along_depth - FIRST_COEF[k] * behind
-                both = both + behind
-            laplace = laplace + SECOND_COEF[k] * both
-        here = pl.ds(d * rows, rows)
-        along_column = across[here, 0:columns] * (1.0 / FIRST_SCALE)
-        laplace = laplace + across[here, columns : 2 * columns] * (1.0 / SECOND_SCALE)
-        advect = (
-            velocity[0, d] * along_depth
-            + velocity[1, d] * along_row
-            + velocity[2, d] * along_column
+    for field in range(count):
+        upper, lower = halves(fields[field].reshape(depth * rows, columns))
+        across[field] = jnp.dot(
+            jnp.concatenate([upper, lower], 1), inner_weight[...], preferred_element_type=F32
         )
-        write(d, diffusivity * laplace - advect + source * rate[d])
+        for d in range(depth):
+            padded[field, d, start : start + rows] = fields[field, d]
+    for field in range(count):
+        diffusivity = DIFFUSIVITY[field]
+        for d in range(depth):
+            centre = fields[field, d]
+            laplace = 3.0 * CENTER_COEF * centre
+            along_depth = along_row = None
+            for k in range(HALO):
+                up = padded[field, d, start + k + 1 : start + k + 1 + rows]
+                down = padded[field, d, start - k - 1 : start - k - 1 + rows]
+                term = FIRST_COEF[k] * (up - down)
+                along_row = term if along_row is None else along_row + term
+                both = up + down
+                ahead = fields[field, d + k + 1] if d + k + 1 < depth else None
+                behind = fields[field, d - k - 1] if d - k - 1 >= 0 else None
+                if ahead is not None and behind is not None:
+                    term = FIRST_COEF[k] * (ahead - behind)
+                elif ahead is not None:
+                    term = FIRST_COEF[k] * ahead
+                else:
+                    term = -FIRST_COEF[k] * behind
+                along_depth = term if along_depth is None else along_depth + term
+                for cells in (ahead, behind):
+                    if cells is not None:
+                        both = both + cells
+                laplace = laplace + SECOND_COEF[k] * both
+            here = pl.ds(d * rows, rows)
+            along_column = across[field, here, 0:columns]
+            laplace = laplace + across[field, here, columns : 2 * columns] * (1.0 / SECOND_SCALE)
+            advect = (
+                velocity[0, d] * along_depth
+                + velocity[1, d] * along_row
+                + (velocity[2, d] * (1.0 / FIRST_SCALE)) * along_column
+            )
+            write(field, d, diffusivity * laplace - advect + SOURCE_COEF[field] * rate[d])
 
 
 def halo_fields(part, fields, velocity, edge_velocity, halos, halo_weight, scale, write):
@@ -316,14 +314,10 @@
     padded[...] = jnp.zeros_like(padded)
     reaction(state, rate)
 
-    def each(field, carry):
-        def write(d, value):
-            part[field, d] = state[field, d] + TIME_STEP * value
-
-        interior_field(state, field, velocity, inner_weight, rate, padded, across, write)
-        return carry
-
-    lax.fori_loop(0, state.shape[0], each, 0)
+    def write(field, d, value):
+        part[field, d] = state[field, d] + TIME_STEP * value
+
+    interior_fields(state, velocity, inner_weight, rate, padded, across, write)
 
 
 def first_halo(
@@ -363,16 +357,10 @@
     padded[...] = jnp.zeros_like(padded)
     reaction(middle, rate)
 
-    def each(field, carry):
-        def write(d, value):
-            part[field, d] = 0.5 * (state[field, d] + middle[field, d]) + (
-                0.5 * TIME_STEP
-            ) * value
-
-        interior_field(middle, field, velocity, inner_weight, rate, padded, across, write)
-        return carry
-
-    lax.fori_loop(0, state.shape[0], each, 0)
+    def write(field, d, value):
+        part[field, d] = 0.5 * (state[field, d] + middle[field, d]) + (0.5 * TIME_STEP) * value
+
+    interior_fields(middle, velocity, inner_weight, rate, padded, across, write)
 
 
 def tent(pixel, cell, shift, cells, pixels):
@@ -602,8 +590,8 @@
     )
     inner_work = [
         pltpu.VMEM((depth, rows, columns), F32),
-        pltpu.VMEM((depth, rows + 4 * HALO, columns), F32),
-        pltpu.VMEM((depth * rows, 2 * columns), F32),
+        pltpu.VMEM((fields, depth, rows + 4 * HALO, columns), F32),
+        pltpu.VMEM((fields, depth * rows, 2 * columns), F32),
     ]
     edge_rows = array(depth // 2, 2 * HALO, columns)
     slice_total = depth * depth_count
@@ -612,7 +600,7 @@
     *sent, state, velocity, table = call(
         pack_kernel,
         faces + (whole, array(*velocity.shape), array(*tf_table.shape, dtype=jnp.int32)),
-        [pltpu.SemaphoreType.DMA((fields + 4,))],
+        [pltpu.SemaphoreType.DMA((5,))],
         [hbm, hbm, hbm],
         in_hbm(state),
         in_hbm(velocity),

time: 28.4 us -> 28.1 us (0.989)
  Pallas kernels: 9.01 us -> 8.38 us
  waiting for transfers between devices: 1.51 us -> 1.86 us
    pallas_call x7, Pallas kernels: 9.01 us -> 8.38 us  [call(): pl.pallas_call(kernel, out_shape=outs, in_specs=specs + [vmem] * (len(arg...]
    ppermute x10, waiting for transfers between devices: 0.03 us -> 0.32 us  [shift(): lax.ppermute(value, axis, [(i, (i + step) % count) for i in range(count)])]
  transfers between devices with their start and end apart: 11 -> 11, of which waited for: 1 -> 2; matrix products, arithmetic and copies ran while one was open for 0% -> 0% of each run, Pallas kernels for 17% -> 15%
where the time goes in v4:
time: 28.1 us; the launch traced here: 27.9 us
  starting transfers between devices  16.3 us (58%)
  Pallas kernels  8.38 us (30%)
  waiting for transfers between devices  1.86 us (7%)
  between operations  1.37 us (5%)
    ppermute x10, starting transfers between devices, shift(): lax.ppermute(value, axis, [(i, (i + step) % count) for i in range(count)])  14.7 us
    pallas_call x7, Pallas kernels, call(): pl.pallas_call(kernel, out_shape=outs, in_specs=specs + [vmem] * (len(arg...  8.38 us
    ppermute x1, starting transfers between devices, local(): received = lax.ppermute(share, 'depth', pairs)  1.58 us
    ppermute x1, waiting for transfers between devices, local(): received = lax.ppermute(share, 'depth', pairs)  1.55 us
  transfers between devices with their start and end apart: 11, of which 2 were waited for; matrix products, arithmetic and copies ran while one was open for 0% of the time, Pallas kernels for 15%

profile of v4, /device:TPU:0, one launch (start us, length us, event | category | flops | bytes accessed | tf_op | source)
XLA Modules:
  0.0 27.9 jit_solution(2888191549084369445)
XLA Ops:
  0.6 1.3 %shard_map.59 = (f32[4,8,16,128]{3,2,1,0:T(8,128)S(1)}, f32[4,8,8,128]{3,2,1,0:T(8,128)S(1)}, f32[4,8,8,128]{3,2,1,0:T(8,128)S(1)}, f32[4,16,128]{2,1,0:T(8,128)...) custom-call(f32[4,16,16,128]{3,2,1,0:T(8,128)} %state_in.1, ...), custom_call_target="tpu_custom_call" | custom-call | tf_op jit(solution)/shard_map/pallas_call | solution.py:563
  2.0 3.0 %collective-permute-start = (f32[4,8,16,128]{3,2,1,0:T(8,128)S(1)}, f32[4,8,16,128]{3,2,1,0:T(8,128)S(1)}, u32[]{:S(2)}, u32[]{:S(2)}) collective-permute-start(f32[4,8,16,128]{3,2,1,0:T(8,128)S(1)} %get-tuple-element.34), channel_id=1, source_target_pairs={{0,16},{16,0},{1,17},{17,1},{2,18},{18,2},{3,19},{19,3},{4,20},{20... | collective-permute-start | bytes 786440 | tf_op jit(solution)/shard_map/ppermute | solution.py:540
  5.0 0.0 collective-permute-start.1
  5.0 1.7 %collective-permute-start.2 = (f32[4,8,8,128]{3,2,1,0:T(8,128)S(1)}, f32[4,8,8,128]{3,2,1,0:T(8,128)S(1)}, u32[]{:S(2)}, u32[]{:S(2)}) collective-permute-start(f32[4,8,8,128]{3,2,1,0:T(8,128)S(1)} %get-tuple-element.36), channel_id=1, source_target_pairs={{0,12},{4,0},{8,4},{12,8},{1,13},{5,1},{9,5},{13,9},{2,14},{6,2},{... | collective-permute-start | bytes 393224 | tf_op jit(solution)/shard_map/ppermute | solution.py:540
  6.8 1.6 %collective-permute-start.3 = (f32[4,16,128]{2,1,0:T(8,128)S(1)}, f32[4,16,128]{2,1,0:T(8,128)S(1)}, u32[]{:S(2)}, u32[]{:S(2)}) collective-permute-start(f32[4,16,128]{2,1,0:T(8,128)S(1)} %get-tuple-element.29.columns_sent), channel_id=1, source_target_pairs={{0,1},{1,2},{2,3},{3,0},{4,5},{5,6},{6,7},{7,4},{8,9},{9,10},{10,1... | collective-permute-start | bytes 98312 | tf_op jit(solution)/shard_map/ppermute | solution.py:540
  8.3 2.2 %collective-permute-start.4 = (f32[4,16,128]{2,1,0:T(8,128)S(1)}, f32[4,16,128]{2,1,0:T(8,128)S(1)}, u32[]{:S(2)}, u32[]{:S(2)}) collective-permute-start(f32[4,16,128]{2,1,0:T(8,128)S(1)} %get-tuple-element.29.columns_sent), channel_id=1, source_target_pairs={{0,3},{1,0},{2,1},{3,2},{4,7},{5,4},{6,5},{7,6},{8,11},{9,8},{10,9... | collective-permute-start | bytes 98312 | tf_op jit(solution)/shard_map/ppermute | solution.py:540
  10.6 1.7 %shard_map.60 = (f32[4,16,16,128]{3,2,1,0:T(8,128)S(1)}, bf16[256,256]{1,0:T(8,128)(2,1)S(1)}, bf16[256,256]{1,0:T(8,128)(2,1)S(1)}, bf16[8,64,64]{2,1,0:T(8,128...) custom-call(f32[4,16,16,128]{3,2,1,0:T(8,128)S(1)} %get-tuple-elemen, ...), custom_call_target="tpu_custom_call" | custom-call | tf_op jit(solution)/shard_map/pallas_call | solution.py:563
  12.3 0.3 collective-permute-done.3.column_below
  12.6 0.0 collective-permute-done.4.column_above
  12.6 0.0 collective-permute-done.1.row_below
  12.6 0.0 collective-permute-done.2.row_above
  12.6 0.0 collective-permute-done.depth_halo
  12.6 0.7 %shard_map.61 = (f32[4,16,16,128]{3,2,1,0:T(8,128)S(1)}, f32[4,8,16,128]{3,2,1,0:T(8,128)S(1)}, f32[4,8,8,128]{3,2,1,0:T(8,128)S(1)}, f32[4,8,8,128]{3,2,1,0:T(8,128)S(1)}, f32[4,16,128]{2,1,0:T(8,128)S(1)}) custom-call(f32[4,16,16,128]{3,2,1,0:T(8,128)S(1)} %get-tuple-element.30.part, f32[3,16,16,128]{3,2,1,0:T(8,128)S(1)} %get-tuple-element.27.velocity, ...), custom_call_target="tpu_custom_call" | custom-call | tf_op jit(solution)/shard_map/pallas_call | solution.py:563
  13.3 0.6 %collective-permute-start.5 = (f32[4,8,16,128]{3,2,1,0:T(8,128)S(1)}, f32[4,8,16,128]{3,2,1,0:T(8,128)S(1)}, u32[]{:S(2)}, u32[]{:S(2)}) collective-permute-start(f32[4,8,16,128]{3,2,1,0:T(8,128)S(1)} %get-tuple-element.41), channel_id=1, source_target_pairs={{0,16},{16,0},{1,17},{17,1},{2,18},{18,2},{3,19},{19,3},{4,20},{20... | collective-permute-start | bytes 786440 | tf_op jit(solution)/shard_map/ppermute | solution.py:540
  13.9 0.0 collective-permute-start.6
  13.9 1.7 %collective-permute-start.7 = (f32[4,8,8,128]{3,2,1,0:T(8,128)S(1)}, f32[4,8,8,128]{3,2,1,0:T(8,128)S(1)}, u32[]{:S(2)}, u32[]{:S(2)}) collective-permute-start(f32[4,8,8,128]{3,2,1,0:T(8,128)S(1)} %get-tuple-element.43), channel_id=1, source_target_pairs={{0,12},{4,0},{8,4},{12,8},{1,13},{5,1},{9,5},{13,9},{2,14},{6,2},{... | collective-permute-start | bytes 393224 | tf_op jit(solution)/shard_map/ppermute | solution.py:540
  15.6 1.5 %collective-permute-start.8 = (f32[4,16,128]{2,1,0:T(8,128)S(1)}, f32[4,16,128]{2,1,0:T(8,128)S(1)}, u32[]{:S(2)}, u32[]{:S(2)}) collective-permute-start(f32[4,16,128]{2,1,0:T(8,128)S(1)} %get-tuple-element.40.columns_sent), channel_id=1, source_target_pairs={{0,1},{1,2},{2,3},{3,0},{4,5},{5,6},{6,7},{7,4},{8,9},{9,10},{10,1... | collective-permute-start | bytes 98312 | tf_op jit(solution)/shard_map/ppermute | solution.py:540
  17.2 2.3 %collective-permute-start.9 = (f32[4,16,128]{2,1,0:T(8,128)S(1)}, f32[4,16,128]{2,1,0:T(8,128)S(1)}, u32[]{:S(2)}, u32[]{:S(2)}) collective-permute-start(f32[4,16,128]{2,1,0:T(8,128)S(1)} %get-tuple-element.40.columns_sent), channel_id=1, source_target_pairs={{0,3},{1,0},{2,1},{3,2},{4,7},{5,4},{6,5},{7,6},{8,11},{9,8},{10,9... | collective-permute-start | bytes 98312 | tf_op jit(solution)/shard_map/ppermute | solution.py:540
  20.1 1.4 %shard_map.62.part = f32[4,16,16,128]{3,2,1,0:T(8,128)S(1)} custom-call(f32[4,16,16,128]{3,2,1,0:T(8,128)S(1)} %get-tuple-element.38.middle, f32[4,16,16,128]{3,2,1,0:T(8,128)S(1)} %get-tuple-element.26.state, f32[3,16,16,128]{3,2,1,0:T(8,128)S(1)} %get-tuple-element.27.velocity, bf16[256,256]{1,0:T(8,128)(2,1)S(1)} %get-tuple-element.39.inner_weight, ...), custom_call_target="tpu_custom_call" | custom-call | tf_op jit(solution)/shard_map/pallas_call | solution.py:563
  21.5 0.0 collective-permute-done.8.column_below
  21.5 0.0 collective-permute-done.9.column_above
  21.5 0.0 collective-permute-done.6.row_below
  21.5 0.0 collective-permute-done.7.row_above
  21.6 0.0 collective-permute-done.5.depth_halo
  21.6 1.3 %shard_map.63 = (f32[16,16,128]{2,1,0:T(8,128)S(1)}, f32[4,32,128]{2,1,0:T(8,128)S(1)}, s32[8,128]{1,0:T(8,128)S(1)}) custom-call(s32[1,1]{1,0:T(1,128)S(6)} %copy.6.order, f32[4,16,16,128]{3,2,1,0:T(8,128)S(1)} %shard_map.62.part, f32[3,16,16,128]{3,2,1,0:T(8,128)S(1)} %get-tuple-element.27.velocity, f32[8,8,128]{2,1,0:T(8,128)S(1)} %get-tuple-element.31.low_velocity, ...), custom_call_target="tpu_custom_call" | custom-call | tf_op jit(solution)/shard_map/pallas_call | solution.py:563
  22.9 1.6 %collective-permute-start.10 = (f32[4,32,128]{2,1,0:T(8,128)S(1)}, f32[4,32,128]{2,1,0:T(8,128)S(1)}, u32[]{:S(2)}, u32[]{:S(2)}) collective-permute-start(f32[4,32,128]{2,1,0:T(8,128)S(1)} %get-tuple-element.48.share.own), channel_id=1, source_target_pairs={{0,16},{16,0},{1,17},{17,1},{2,18},{18,2},{3,19},{19,3},{4,20},{20... | collective-permute-start | bytes 196616 | tf_op jit(solution)/shard_map/ppermute | solution.py:688
  24.4 1.2 %shard_map.64 = f32[4,16,16,128]{3,2,1,0:T(8,128)} custom-call(f32[4,16,16,128]{3,2,1,0:T(8,128)S(1)} %shard_map.62.part, f32[16,16,128]{2,1,0:T(8,128)S(1)} %get-tuple-element.47.temperature, f32[3,16,16,128]{3,2,1,0:T(8,128)S(1)} %get-tuple-element.27.velocity, f32[8,8,128]{2,1,0:T(8,128)S(1)} %get-tuple-element.31.low_velocity, ...), custom_call_target="tpu_custom_call" | custom-call | tf_op jit(solution)/shard_map/pallas_call | solution.py:563
  25.6 1.5 %collective-permute-done.10.received = f32[4,32,128]{2,1,0:T(8,128)S(1)} collective-permute-done((f32[4,32,128]{2,1,0:T(8,128)S(1)}, f32[4,32,128]{2,1,0:T(8,128)S(1)}, u32[]{:S(2)}, u32[]{:S(2)}) %collective-permute-start.10) | collective-permute-done | bytes 65568 | tf_op jit(solution)/shard_map/ppermute | solution.py:688
  27.2 0.8 %shard_map.65 = f32[4,64,64]{2,1,0:T(8,128)} custom-call(s32[8,128]{1,0:T(8,128)S(1)} %get-tuple-element.49.toward, f32[4,32,128]{2,1,0:T(8,128)S(1)} %get-tuple-element.48.share.own, f32[4,32,128]{2,1,0:T(8,128)S(1)} %collective-permute-done.10.received), custom_call_target="tpu_custom_call" | custom-call | tf_op jit(solution)/shard_map/pallas_call | solution.py:563
Async XLA Ops:
  2.0 10.6 %collective-permute-start = (f32[4,8,16,128]{3,2,1,0:T(8,128)S(1)}, f32[4,8,16,128]{3,2,1,0:T(8,128)S(1)}, u32[]{:S(2)}, u32[]{:S(2)}) collective-permute-start(f32[4,8,16,128]{3,2,1,0:T(8,128)S(1)} %get-tuple-element.34), channel_id=1, source_target_pairs={{0,16},{16,0},{1,17},{17,1},{2,18},{18,2},{3,19},{19,3},{4,20},{20... | collective-permute-start | bytes 786440 | tf_op jit(solution)/shard_map/ppermute | solution.py:540
  5.0 7.6 %collective-permute-start.1 = (f32[4,8,8,128]{3,2,1,0:T(8,128)S(1)}, f32[4,8,8,128]{3,2,1,0:T(8,128)S(1)}, u32[]{:S(2)}, u32[]{:S(2)}) collective-permute-start(f32[4,8,8,128]{3,2,1,0:T(8,128)S(1)} %get-tuple-element.35), channel_id=1, source_target_pairs={{0,4},{4,8},{8,12},{12,0},{1,5},{5,9},{9,13},{13,1},{2,6},{6,10},{... | collective-permute-start | bytes 393224 | tf_op jit(solution)/shard_map/ppermute | solution.py:540
  5.0 7.6 %collective-permute-start.2 = (f32[4,8,8,128]{3,2,1,0:T(8,128)S(1)}, f32[4,8,8,128]{3,2,1,0:T(8,128)S(1)}, u32[]{:S(2)}, u32[]{:S(2)}) collective-permute-start(f32[4,8,8,128]{3,2,1,0:T(8,128)S(1)} %get-tuple-element.36), channel_id=1, source_target_pairs={{0,12},{4,0},{8,4},{12,8},{1,13},{5,1},{9,5},{13,9},{2,14},{6,2},{... | collective-permute-start | bytes 393224 | tf_op jit(solution)/shard_map/ppermute | solution.py:540
  6.8 5.8 %collective-permute-start.3 = (f32[4,16,128]{2,1,0:T(8,128)S(1)}, f32[4,16,128]{2,1,0:T(8,128)S(1)}, u32[]{:S(2)}, u32[]{:S(2)}) collective-permute-start(f32[4,16,128]{2,1,0:T(8,128)S(1)} %get-tuple-element.29.columns_sent), channel_id=1, source_target_pairs={{0,1},{1,2},{2,3},{3,0},{4,5},{5,6},{6,7},{7,4},{8,9},{9,10},{10,1... | collective-permute-start | bytes 98312 | tf_op jit(solution)/shard_map/ppermute | solution.py:540
  8.3 4.3 %collective-permute-start.4 = (f32[4,16,128]{2,1,0:T(8,128)S(1)}, f32[4,16,128]{2,1,0:T(8,128)S(1)}, u32[]{:S(2)}, u32[]{:S(2)}) collective-permute-start(f32[4,16,128]{2,1,0:T(8,128)S(1)} %get-tuple-element.29.columns_sent), channel_id=1, source_target_pairs={{0,3},{1,0},{2,1},{3,2},{4,7},{5,4},{6,5},{7,6},{8,11},{9,8},{10,9... | collective-permute-start | bytes 98312 | tf_op jit(solution)/shard_map/ppermute | solution.py:540
  13.3 8.2 %collective-permute-start.5 = (f32[4,8,16,128]{3,2,1,0:T(8,128)S(1)}, f32[4,8,16,128]{3,2,1,0:T(8,128)S(1)}, u32[]{:S(2)}, u32[]{:S(2)}) collective-permute-start(f32[4,8,16,128]{3,2,1,0:T(8,128)S(1)} %get-tuple-element.41), channel_id=1, source_target_pairs={{0,16},{16,0},{1,17},{17,1},{2,18},{18,2},{3,19},{19,3},{4,20},{20... | collective-permute-start | bytes 786440 | tf_op jit(solution)/shard_map/ppermute | solution.py:540
  13.9 7.6 %collective-permute-start.6 = (f32[4,8,8,128]{3,2,1,0:T(8,128)S(1)}, f32[4,8,8,128]{3,2,1,0:T(8,128)S(1)}, u32[]{:S(2)}, u32[]{:S(2)}) collective-permute-start(f32[4,8,8,128]{3,2,1,0:T(8,128)S(1)} %get-tuple-element.42), channel_id=1, source_target_pairs={{0,4},{4,8},{8,12},{12,0},{1,5},{5,9},{9,13},{13,1},{2,6},{6,10},{... | collective-permute-start | bytes 393224 | tf_op jit(solution)/shard_map/ppermute | solution.py:540
  13.9 7.7 %collective-permute-start.7 = (f32[4,8,8,128]{3,2,1,0:T(8,128)S(1)}, f32[4,8,8,128]{3,2,1,0:T(8,128)S(1)}, u32[]{:S(2)}, u32[]{:S(2)}) collective-permute-start(f32[4,8,8,128]{3,2,1,0:T(8,128)S(1)} %get-tuple-element.43), channel_id=1, source_target_pairs={{0,12},{4,0},{8,4},{12,8},{1,13},{5,1},{9,5},{13,9},{2,14},{6,2},{... | collective-permute-start | bytes 393224 | tf_op jit(solution)/shard_map/ppermute | solution.py:540
  15.6 5.9 %collective-permute-start.8 = (f32[4,16,128]{2,1,0:T(8,128)S(1)}, f32[4,16,128]{2,1,0:T(8,128)S(1)}, u32[]{:S(2)}, u32[]{:S(2)}) collective-permute-start(f32[4,16,128]{2,1,0:T(8,128)S(1)} %get-tuple-element.40.columns_sent), channel_id=1, source_target_pairs={{0,1},{1,2},{2,3},{3,0},{4,5},{5,6},{6,7},{7,4},{8,9},{9,10},{10,1... | collective-permute-start | bytes 98312 | tf_op jit(solution)/shard_map/ppermute | solution.py:540
  17.2 4.4 %collective-permute-start.9 = (f32[4,16,128]{2,1,0:T(8,128)S(1)}, f32[4,16,128]{2,1,0:T(8,128)S(1)}, u32[]{:S(2)}, u32[]{:S(2)}) collective-permute-start(f32[4,16,128]{2,1,0:T(8,128)S(1)} %get-tuple-element.40.columns_sent), channel_id=1, source_target_pairs={{0,3},{1,0},{2,1},{3,2},{4,7},{5,4},{6,5},{7,6},{8,11},{9,8},{10,9... | collective-permute-start | bytes 98312 | tf_op jit(solution)/shard_map/ppermute | solution.py:540
  22.9 4.3 %collective-permute-start.10 = (f32[4,32,128]{2,1,0:T(8,128)S(1)}, f32[4,32,128]{2,1,0:T(8,128)S(1)}, u32[]{:S(2)}, u32[]{:S(2)}) collective-permute-start(f32[4,32,128]{2,1,0:T(8,128)S(1)} %get-tuple-element.48.share.own), channel_id=1, source_target_pairs={{0,16},{16,0},{1,17},{17,1},{2,18},{18,2},{3,19},{19,3},{4,20},{20... | collective-permute-start | bytes 196616 | tf_op jit(solution)/shard_map/ppermute | solution.py:688

commit v5 on v4

--- a/solution.py
+++ b/solution.py
@@ -171,7 +171,7 @@
 
 
 def halo_fields(part, fields, velocity, edge_velocity, halos, halo_weight, scale, write):
-    depth_halo, row_below, row_above, column_below, column_above = halos
+    depth_halo, row_above, row_below, column_below, column_above = halos
     low_velocity, high_velocity, column_velocity = edge_velocity
     depth, rows, columns = velocity.shape[1:]
     half = depth // 2
@@ -327,8 +327,8 @@
     high_velocity,
     column_velocity,
     depth_halo,
+    row_above,
     row_below,
-    row_above,
     column_below,
     column_above,
     halo_weight,
@@ -338,7 +338,7 @@
     high_out,
     column_out,
 ):
-    halos = (depth_halo, row_below, row_above, column_below, column_above)
+    halos = (depth_halo, row_above, row_below, column_below, column_above)
     edge_velocity = (low_velocity, high_velocity, column_velocity)
 
     def write(field, d, here, value):
@@ -464,8 +464,8 @@
     high_velocity,
     column_velocity,
     depth_halo,
+    row_above,
     row_below,
-    row_above,
     column_below,
     column_above,
     halo_weight,
@@ -477,7 +477,7 @@
     toward,
     samples,
 ):
-    halos = (depth_halo, row_below, row_above, column_below, column_above)
+    halos = (depth_halo, row_above, row_below, column_below, column_above)
     edge_velocity = (low_velocity, high_velocity, column_velocity)
 
     def write(field, d, here, value):
@@ -497,8 +497,8 @@
     high_velocity,
     column_velocity,
     depth_halo,
+    row_above,
     row_below,
-    row_above,
     column_below,
     column_above,
     halo_weight,
@@ -506,7 +506,7 @@
     new_state,
 ):
     del share
-    halos = (depth_halo, row_below, row_above, column_below, column_above)
+    halos = (depth_halo, row_above, row_below, column_below, column_above)
     edge_velocity = (low_velocity, high_velocity, column_velocity)
 
     def write(field, d, here, value):
@@ -555,7 +555,7 @@
     row_above = shift(low_rows, "row", -1)
     column_below = shift(columns, "col", 1)
     column_above = shift(columns, "col", -1)
-    return depth_halo, row_below, row_above, column_below, column_above
+    return depth_halo, row_above, row_below, column_below, column_above
 
 
 def call(kernel, outs, scratch, specs, *args):

time: 28.1 us -> 27.3 us (0.972)
  starting transfers between devices: 16.3 us -> 13.6 us
  waiting for transfers between devices: 1.86 us -> 3.86 us
    ppermute x10, starting transfers between devices: 14.7 us -> 13 us  [shift(): lax.ppermute(value, axis, [(i, (i + step) % count) for i in range(count)])]
    ppermute x1, starting transfers between devices: 1.58 us -> 0.57 us  [local(): received = lax.ppermute(share, 'depth', pairs)]
    ppermute x1, waiting for transfers between devices: 1.55 us -> 2.56 us  [local(): received = lax.ppermute(share, 'depth', pairs)]
    ppermute x10, waiting for transfers between devices: 0.32 us -> 1.3 us  [shift(): lax.ppermute(value, axis, [(i, (i + step) % count) for i in range(count)])]
  transfers between devices with their start and end apart: 11 -> 11, of which waited for: 2 -> 6; matrix products, arithmetic and copies ran while one was open for 0% -> 0% of each run, Pallas kernels for 15% -> 16%
where the time goes in v5:
time: 27.3 us; the launch traced here: 27.2 us
  starting transfers between devices  13.6 us (50%)
  Pallas kernels  8.37 us (31%)
  waiting for transfers between devices  3.86 us (14%)
  between operations  1.33 us (5%)
    ppermute x10, starting transfers between devices, shift(): lax.ppermute(value, axis, [(i, (i + step) % count) for i in range(count)])  13 us
    pallas_call x7, Pallas kernels, call(): pl.pallas_call(kernel, out_shape=outs, in_specs=specs + [vmem] * (len(arg...  8.37 us
    ppermute x1, waiting for transfers between devices, local(): received = lax.ppermute(share, 'depth', pairs)  2.56 us
    ppermute x10, waiting for transfers between devices, shift(): lax.ppermute(value, axis, [(i, (i + step) % count) for i in range(count)])  1.3 us
    ppermute x1, starting transfers between devices, local(): received = lax.ppermute(share, 'depth', pairs)  0.57 us
  transfers between devices with their start and end apart: 11, of which 6 were waited for; matrix products, arithmetic and copies ran while one was open for 0% of the time, Pallas kernels for 16%

profile of v5, /device:TPU:0, one launch (start us, length us, event | category | flops | bytes accessed | tf_op | source)
XLA Modules:
  0.0 27.2 jit_solution(12243992145352508538)
XLA Ops:
  0.6 1.3 %shard_map.59 = (f32[4,8,16,128]{3,2,1,0:T(8,128)S(1)}, f32[4,8,8,128]{3,2,1,0:T(8,128)S(1)}, f32[4,8,8,128]{3,2,1,0:T(8,128)S(1)}, f32[4,16,128]{2,1,0:T(8,128)...) custom-call(f32[4,16,16,128]{3,2,1,0:T(8,128)} %state_in.1, ...), custom_call_target="tpu_custom_call" | custom-call | tf_op jit(solution)/shard_map/pallas_call | solution.py:563
  2.0 3.0 %collective-permute-start = (f32[4,8,16,128]{3,2,1,0:T(8,128)S(1)}, f32[4,8,16,128]{3,2,1,0:T(8,128)S(1)}, u32[]{:S(2)}, u32[]{:S(2)}) collective-permute-start(f32[4,8,16,128]{3,2,1,0:T(8,128)S(1)} %get-tuple-element.34), channel_id=1, source_target_pairs={{0,16},{16,0},{1,17},{17,1},{2,18},{18,2},{3,19},{19,3},{4,20},{20... | collective-permute-start | bytes 786440 | tf_op jit(solution)/shard_map/ppermute | solution.py:540
  5.0 0.7 %collective-permute-start.1 = (f32[4,8,8,128]{3,2,1,0:T(8,128)S(1)}, f32[4,8,8,128]{3,2,1,0:T(8,128)S(1)}, u32[]{:S(2)}, u32[]{:S(2)}) collective-permute-start(f32[4,8,8,128]{3,2,1,0:T(8,128)S(1)} %get-tuple-element.35), channel_id=1, source_target_pairs={{0,12},{4,0},{8,4},{12,8},{1,13},{5,1},{9,5},{13,9},{2,14},{6,2},{... | collective-permute-start | bytes 393224 | tf_op jit(solution)/shard_map/ppermute | solution.py:540
  5.7 0.0 collective-permute-start.2
  5.7 1.6 %collective-permute-start.3 = (f32[4,16,128]{2,1,0:T(8,128)S(1)}, f32[4,16,128]{2,1,0:T(8,128)S(1)}, u32[]{:S(2)}, u32[]{:S(2)}) collective-permute-start(f32[4,16,128]{2,1,0:T(8,128)S(1)} %get-tuple-element.29.columns_sent), channel_id=1, source_target_pairs={{0,1},{1,2},{2,3},{3,0},{4,5},{5,6},{6,7},{7,4},{8,9},{9,10},{10,1... | collective-permute-start | bytes 98312 | tf_op jit(solution)/shard_map/ppermute | solution.py:540
  7.2 2.2 %collective-permute-start.4 = (f32[4,16,128]{2,1,0:T(8,128)S(1)}, f32[4,16,128]{2,1,0:T(8,128)S(1)}, u32[]{:S(2)}, u32[]{:S(2)}) collective-permute-start(f32[4,16,128]{2,1,0:T(8,128)S(1)} %get-tuple-element.29.columns_sent), channel_id=1, source_target_pairs={{0,3},{1,0},{2,1},{3,2},{4,7},{5,4},{6,5},{7,6},{8,11},{9,8},{10,9... | collective-permute-start | bytes 98312 | tf_op jit(solution)/shard_map/ppermute | solution.py:540
  9.5 1.7 %shard_map.60 = (f32[4,16,16,128]{3,2,1,0:T(8,128)S(1)}, bf16[256,256]{1,0:T(8,128)(2,1)S(1)}, bf16[256,256]{1,0:T(8,128)(2,1)S(1)}, bf16[8,64,64]{2,1,0:T(8,128...) custom-call(f32[4,16,16,128]{3,2,1,0:T(8,128)S(1)} %get-tuple-elemen, ...), custom_call_target="tpu_custom_call" | custom-call | tf_op jit(solution)/shard_map/pallas_call | solution.py:563
  11.2 0.6 %collective-permute-done.3.column_below = f32[4,16,128]{2,1,0:T(8,128)S(1)} collective-permute-done((f32[4,16,128]{2,1,0:T(8,128)S(1)}, f32[4,16,128]{2,1,0:T(8,128)S(1)}, u32[]{:S(2)}, u32[]{:S(2)}) %collective-permute-start.3) | collective-permute-done | bytes 32800 | tf_op jit(solution)/shard_map/ppermute | solution.py:540
  11.8 0.1 collective-permute-done.4.column_above
  11.9 0.0 collective-permute-done.1.row_above
  11.9 0.0 collective-permute-done.2.row_below
  11.9 0.0 collective-permute-done.depth_halo
  11.9 0.7 %shard_map.61 = (f32[4,16,16,128]{3,2,1,0:T(8,128)S(1)}, f32[4,8,16,128]{3,2,1,0:T(8,128)S(1)}, f32[4,8,8,128]{3,2,1,0:T(8,128)S(1)}, f32[4,8,8,128]{3,2,1,0:T(8,128)S(1)}, f32[4,16,128]{2,1,0:T(8,128)S(1)}) custom-call(f32[4,16,16,128]{3,2,1,0:T(8,128)S(1)} %get-tuple-element.30.part, f32[3,16,16,128]{3,2,1,0:T(8,128)S(1)} %get-tuple-element.27.velocity, ...), custom_call_target="tpu_custom_call" | custom-call | tf_op jit(solution)/shard_map/pallas_call | solution.py:563
  12.6 1.2 %collective-permute-start.5 = (f32[4,8,16,128]{3,2,1,0:T(8,128)S(1)}, f32[4,8,16,128]{3,2,1,0:T(8,128)S(1)}, u32[]{:S(2)}, u32[]{:S(2)}) collective-permute-start(f32[4,8,16,128]{3,2,1,0:T(8,128)S(1)} %get-tuple-element.41), channel_id=1, source_target_pairs={{0,16},{16,0},{1,17},{17,1},{2,18},{18,2},{3,19},{19,3},{4,20},{20... | collective-permute-start | bytes 786440 | tf_op jit(solution)/shard_map/ppermute | solution.py:540
  13.8 0.0 collective-permute-start.6
  13.8 0.5 %collective-permute-start.7 = (f32[4,8,8,128]{3,2,1,0:T(8,128)S(1)}, f32[4,8,8,128]{3,2,1,0:T(8,128)S(1)}, u32[]{:S(2)}, u32[]{:S(2)}) collective-permute-start(f32[4,8,8,128]{3,2,1,0:T(8,128)S(1)} %get-tuple-element.43), channel_id=1, source_target_pairs={{0,4},{4,8},{8,12},{12,0},{1,5},{5,9},{9,13},{13,1},{2,6},{6,10},{... | collective-permute-start | bytes 393224 | tf_op jit(solution)/shard_map/ppermute | solution.py:540
  14.3 1.6 %collective-permute-start.8 = (f32[4,16,128]{2,1,0:T(8,128)S(1)}, f32[4,16,128]{2,1,0:T(8,128)S(1)}, u32[]{:S(2)}, u32[]{:S(2)}) collective-permute-start(f32[4,16,128]{2,1,0:T(8,128)S(1)} %get-tuple-element.40.columns_sent), channel_id=1, source_target_pairs={{0,1},{1,2},{2,3},{3,0},{4,5},{5,6},{6,7},{7,4},{8,9},{9,10},{10,1... | collective-permute-start | bytes 98312 | tf_op jit(solution)/shard_map/ppermute | solution.py:540
  15.9 2.2 %collective-permute-start.9 = (f32[4,16,128]{2,1,0:T(8,128)S(1)}, f32[4,16,128]{2,1,0:T(8,128)S(1)}, u32[]{:S(2)}, u32[]{:S(2)}) collective-permute-start(f32[4,16,128]{2,1,0:T(8,128)S(1)} %get-tuple-element.40.columns_sent), channel_id=1, source_target_pairs={{0,3},{1,0},{2,1},{3,2},{4,7},{5,4},{6,5},{7,6},{8,11},{9,8},{10,9... | collective-permute-start | bytes 98312 | tf_op jit(solution)/shard_map/ppermute | solution.py:540
  18.8 1.4 %shard_map.62.part = f32[4,16,16,128]{3,2,1,0:T(8,128)S(1)} custom-call(f32[4,16,16,128]{3,2,1,0:T(8,128)S(1)} %get-tuple-element.38.middle, f32[4,16,16,128]{3,2,1,0:T(8,128)S(1)} %get-tuple-element.26.state, f32[3,16,16,128]{3,2,1,0:T(8,128)S(1)} %get-tuple-element.27.velocity, bf16[256,256]{1,0:T(8,128)(2,1)S(1)} %get-tuple-element.39.inner_weight, ...), custom_call_target="tpu_custom_call" | custom-call | tf_op jit(solution)/shard_map/pallas_call | solution.py:563
  20.2 0.1 collective-permute-done.8.column_below
  20.3 0.4 %collective-permute-done.9.column_above = f32[4,16,128]{2,1,0:T(8,128)S(1)} collective-permute-done((f32[4,16,128]{2,1,0:T(8,128)S(1)}, f32[4,16,128]{2,1,0:T(8,128)S(1)}, u32[]{:S(2)}, u32[]{:S(2)}) %collective-permute-start.9) | collective-permute-done | bytes 32800 | tf_op jit(solution)/shard_map/ppermute | solution.py:540
  20.7 0.0 collective-permute-done.6.row_above
  20.7 0.0 collective-permute-done.7.row_below
  20.7 0.1 collective-permute-done.5.depth_halo
  20.8 1.3 %shard_map.63 = (f32[16,16,128]{2,1,0:T(8,128)S(1)}, f32[4,32,128]{2,1,0:T(8,128)S(1)}, s32[8,128]{1,0:T(8,128)S(1)}) custom-call(s32[1,1]{1,0:T(1,128)S(6)} %copy.6.order, f32[4,16,16,128]{3,2,1,0:T(8,128)S(1)} %shard_map.62.part, f32[3,16,16,128]{3,2,1,0:T(8,128)S(1)} %get-tuple-element.27.velocity, f32[8,8,128]{2,1,0:T(8,128)S(1)} %get-tuple-element.31.low_velocity, ...), custom_call_target="tpu_custom_call" | custom-call | tf_op jit(solution)/shard_map/pallas_call | solution.py:563
  22.1 0.6 %collective-permute-start.10 = (f32[4,32,128]{2,1,0:T(8,128)S(1)}, f32[4,32,128]{2,1,0:T(8,128)S(1)}, u32[]{:S(2)}, u32[]{:S(2)}) collective-permute-start(f32[4,32,128]{2,1,0:T(8,128)S(1)} %get-tuple-element.48.share.own), channel_id=1, source_target_pairs={{0,16},{16,0},{1,17},{17,1},{2,18},{18,2},{3,19},{19,3},{4,20},{20... | collective-permute-start | bytes 196616 | tf_op jit(solution)/shard_map/ppermute | solution.py:688
  22.7 1.2 %shard_map.64 = f32[4,16,16,128]{3,2,1,0:T(8,128)} custom-call(f32[4,16,16,128]{3,2,1,0:T(8,128)S(1)} %shard_map.62.part, f32[16,16,128]{2,1,0:T(8,128)S(1)} %get-tuple-element.47.temperature, f32[3,16,16,128]{3,2,1,0:T(8,128)S(1)} %get-tuple-element.27.velocity, f32[8,8,128]{2,1,0:T(8,128)S(1)} %get-tuple-element.31.low_velocity, ...), custom_call_target="tpu_custom_call" | custom-call | tf_op jit(solution)/shard_map/pallas_call | solution.py:563
  23.9 2.6 %collective-permute-done.10.received = f32[4,32,128]{2,1,0:T(8,128)S(1)} collective-permute-done((f32[4,32,128]{2,1,0:T(8,128)S(1)}, f32[4,32,128]{2,1,0:T(8,128)S(1)}, u32[]{:S(2)}, u32[]{:S(2)}) %collective-permute-start.10) | collective-permute-done | bytes 65568 | tf_op jit(solution)/shard_map/ppermute | solution.py:688
  26.4 0.8 %shard_map.65 = f32[4,64,64]{2,1,0:T(8,128)} custom-call(s32[8,128]{1,0:T(8,128)S(1)} %get-tuple-element.49.toward, f32[4,32,128]{2,1,0:T(8,128)S(1)} %get-tuple-element.48.share.own, f32[4,32,128]{2,1,0:T(8,128)S(1)} %collective-permute-done.10.received), custom_call_target="tpu_custom_call" | custom-call | tf_op jit(solution)/shard_map/pallas_call | solution.py:563
Async XLA Ops:
  2.0 9.9 %collective-permute-start = (f32[4,8,16,128]{3,2,1,0:T(8,128)S(1)}, f32[4,8,16,128]{3,2,1,0:T(8,128)S(1)}, u32[]{:S(2)}, u32[]{:S(2)}) collective-permute-start(f32[4,8,16,128]{3,2,1,0:T(8,128)S(1)} %get-tuple-element.34), channel_id=1, source_target_pairs={{0,16},{16,0},{1,17},{17,1},{2,18},{18,2},{3,19},{19,3},{4,20},{20... | collective-permute-start | bytes 786440 | tf_op jit(solution)/shard_map/ppermute | solution.py:540
  5.0 6.9 %collective-permute-start.1 = (f32[4,8,8,128]{3,2,1,0:T(8,128)S(1)}, f32[4,8,8,128]{3,2,1,0:T(8,128)S(1)}, u32[]{:S(2)}, u32[]{:S(2)}) collective-permute-start(f32[4,8,8,128]{3,2,1,0:T(8,128)S(1)} %get-tuple-element.35), channel_id=1, source_target_pairs={{0,12},{4,0},{8,4},{12,8},{1,13},{5,1},{9,5},{13,9},{2,14},{6,2},{... | collective-permute-start | bytes 393224 | tf_op jit(solution)/shard_map/ppermute | solution.py:540
  5.7 6.3 %collective-permute-start.2 = (f32[4,8,8,128]{3,2,1,0:T(8,128)S(1)}, f32[4,8,8,128]{3,2,1,0:T(8,128)S(1)}, u32[]{:S(2)}, u32[]{:S(2)}) collective-permute-start(f32[4,8,8,128]{3,2,1,0:T(8,128)S(1)} %get-tuple-element.36), channel_id=1, source_target_pairs={{0,4},{4,8},{8,12},{12,0},{1,5},{5,9},{9,13},{13,1},{2,6},{6,10},{... | collective-permute-start | bytes 393224 | tf_op jit(solution)/shard_map/ppermute | solution.py:540
  5.7 6.1 %collective-permute-start.3 = (f32[4,16,128]{2,1,0:T(8,128)S(1)}, f32[4,16,128]{2,1,0:T(8,128)S(1)}, u32[]{:S(2)}, u32[]{:S(2)}) collective-permute-start(f32[4,16,128]{2,1,0:T(8,128)S(1)} %get-tuple-element.29.columns_sent), channel_id=1, source_target_pairs={{0,1},{1,2},{2,3},{3,0},{4,5},{5,6},{6,7},{7,4},{8,9},{9,10},{10,1... | collective-permute-start | bytes 98312 | tf_op jit(solution)/shard_map/ppermute | solution.py:540
  7.2 4.7 %collective-permute-start.4 = (f32[4,16,128]{2,1,0:T(8,128)S(1)}, f32[4,16,128]{2,1,0:T(8,128)S(1)}, u32[]{:S(2)}, u32[]{:S(2)}) collective-permute-start(f32[4,16,128]{2,1,0:T(8,128)S(1)} %get-tuple-element.29.columns_sent), channel_id=1, source_target_pairs={{0,3},{1,0},{2,1},{3,2},{4,7},{5,4},{6,5},{7,6},{8,11},{9,8},{10,9... | collective-permute-start | bytes 98312 | tf_op jit(solution)/shard_map/ppermute | solution.py:540
  12.6 8.2 %collective-permute-start.5 = (f32[4,8,16,128]{3,2,1,0:T(8,128)S(1)}, f32[4,8,16,128]{3,2,1,0:T(8,128)S(1)}, u32[]{:S(2)}, u32[]{:S(2)}) collective-permute-start(f32[4,8,16,128]{3,2,1,0:T(8,128)S(1)} %get-tuple-element.41), channel_id=1, source_target_pairs={{0,16},{16,0},{1,17},{17,1},{2,18},{18,2},{3,19},{19,3},{4,20},{20... | collective-permute-start | bytes 786440 | tf_op jit(solution)/shard_map/ppermute | solution.py:540
  13.8 6.9 %collective-permute-start.6 = (f32[4,8,8,128]{3,2,1,0:T(8,128)S(1)}, f32[4,8,8,128]{3,2,1,0:T(8,128)S(1)}, u32[]{:S(2)}, u32[]{:S(2)}) collective-permute-start(f32[4,8,8,128]{3,2,1,0:T(8,128)S(1)} %get-tuple-element.42), channel_id=1, source_target_pairs={{0,12},{4,0},{8,4},{12,8},{1,13},{5,1},{9,5},{13,9},{2,14},{6,2},{... | collective-permute-start | bytes 393224 | tf_op jit(solution)/shard_map/ppermute | solution.py:540
  13.8 6.9 %collective-permute-start.7 = (f32[4,8,8,128]{3,2,1,0:T(8,128)S(1)}, f32[4,8,8,128]{3,2,1,0:T(8,128)S(1)}, u32[]{:S(2)}, u32[]{:S(2)}) collective-permute-start(f32[4,8,8,128]{3,2,1,0:T(8,128)S(1)} %get-tuple-element.43), channel_id=1, source_target_pairs={{0,4},{4,8},{8,12},{12,0},{1,5},{5,9},{9,13},{13,1},{2,6},{6,10},{... | collective-permute-start | bytes 393224 | tf_op jit(solution)/shard_map/ppermute | solution.py:540
  14.3 6.0 %collective-permute-start.8 = (f32[4,16,128]{2,1,0:T(8,128)S(1)}, f32[4,16,128]{2,1,0:T(8,128)S(1)}, u32[]{:S(2)}, u32[]{:S(2)}) collective-permute-start(f32[4,16,128]{2,1,0:T(8,128)S(1)} %get-tuple-element.40.columns_sent), channel_id=1, source_target_pairs={{0,1},{1,2},{2,3},{3,0},{4,5},{5,6},{6,7},{7,4},{8,9},{9,10},{10,1... | collective-permute-start | bytes 98312 | tf_op jit(solution)/shard_map/ppermute | solution.py:540
  15.9 4.8 %collective-permute-start.9 = (f32[4,16,128]{2,1,0:T(8,128)S(1)}, f32[4,16,128]{2,1,0:T(8,128)S(1)}, u32[]{:S(2)}, u32[]{:S(2)}) collective-permute-start(f32[4,16,128]{2,1,0:T(8,128)S(1)} %get-tuple-element.40.columns_sent), channel_id=1, source_target_pairs={{0,3},{1,0},{2,1},{3,2},{4,7},{5,4},{6,5},{7,6},{8,11},{9,8},{10,9... | collective-permute-start | bytes 98312 | tf_op jit(solution)/shard_map/ppermute | solution.py:540
  22.1 4.3 %collective-permute-start.10 = (f32[4,32,128]{2,1,0:T(8,128)S(1)}, f32[4,32,128]{2,1,0:T(8,128)S(1)}, u32[]{:S(2)}, u32[]{:S(2)}) collective-permute-start(f32[4,32,128]{2,1,0:T(8,128)S(1)} %get-tuple-element.48.share.own), channel_id=1, source_target_pairs={{0,16},{16,0},{1,17},{17,1},{2,18},{18,2},{3,19},{19,3},{4,20},{20... | collective-permute-start | bytes 196616 | tf_op jit(solution)/shard_map/ppermute | solution.py:688

commit v6 on v5

--- a/solution.py
+++ b/solution.py
@@ -370,10 +370,10 @@
     return jnp.maximum(0.0, 1.0 - jnp.abs(at - cell) / reach) / reach
 
 
-def sample_slices(temperature, column_weight, row_weight, samples):
+def sample_slices(temperature, scale, column_weight, row_weight, samples):
     depth, rows, columns = temperature.shape
     half = depth // 2
-    upper, lower = halves(temperature[...].reshape(depth * rows, columns))
+    upper, lower = halves(temperature[...].reshape(depth * rows, columns) * scale)
     wide = jnp.dot(
         jnp.concatenate([upper, lower], 1), column_weight[...], preferred_element_type=F32
     )
@@ -417,31 +417,33 @@
 
         def advance(position, running):
             chosen = jnp.where(flag == 0, half - 1 - position, position)
-            level = jnp.clip(samples[chosen, rows_here] * (levels - 1.0), 0.0, levels - 1.0)
+            level = jnp.clip(samples[chosen, rows_here], 0.0, levels - 1.0)
             lower = level.astype(jnp.int32)
             fraction = level - lower.astype(F32)
             below = look_up(below_tables, lower, shape)
             above = look_up(above_tables, lower, shape)
-            raw = []
-            for channel in range(4):
-                low, high = below, above
-                if channel > 0:
-                    low = lax.shift_right_logical(low, 8 * channel)
-                    high = lax.shift_right_logical(high, 8 * channel)
-                if channel < 3:
-                    low, high = low & 255, high & 255
-                low, high = low.astype(F32), high.astype(F32)
-                raw.append(low + fraction * (high - low))
-            alpha = raw[3] * (OPACITY_TOTAL / slice_total / 255.0)
+            low_alpha = lax.shift_right_logical(below, 24).astype(F32)
+            high_alpha = lax.shift_right_logical(above, 24).astype(F32)
+            alpha = (low_alpha + fraction * (high_alpha - low_alpha)) * (
+                OPACITY_TOTAL / slice_total / 255.0
+            )
             through = 1.0 - alpha
-            return tuple(
-                [alpha * raw[c] + through * running[c] for c in range(3)]
-                + [alpha + through * running[3]]
-            )
+            high_share = alpha * fraction
+            low_share = alpha - high_share
+            result = []
+            for channel in range(3):
+                low = (below & (255 << 8 * channel)).astype(F32)
+                high = (above & (255 << 8 * channel)).astype(F32)
+                result.append(
+                    through * running[channel] + (low_share * low + high_share * high)
+                )
+            return tuple(result + [alpha + through * running[3]])
 
         zero = jnp.zeros(shape, F32)
         running = lax.fori_loop(0, half, advance, (zero, zero, zero, zero), unroll=True)
-        parts.append([value * (1.0 / 255.0) for value in running[:3]] + [running[3]])
+        parts.append(
+            [running[c] * (1.0 / 255.0 / 256.0**c) for c in range(3)] + [running[3]]
+        )
     for channel in range(4):
         merged = []
         for part in range(2):
@@ -484,7 +486,7 @@
         temperature[d, here] = value
 
     halo_fields(part, [3], velocity, edge_velocity, halos, halo_weight, 0.5 * TIME_STEP, write)
-    sample_slices(temperature, column_weight, row_weight, samples)
+    sample_slices(temperature, table.shape[1] - 1.0, column_weight, row_weight, samples)
     toward[...] = jnp.full(toward.shape, order[0, 0], jnp.int32)
     march(samples, table, order[0, 0], slice_total, share)
 

time: 27.3 us -> 27.3 us (level)
  no operation moved by 1% of the time
where the time goes in v6:
time: 27.3 us; the launch traced here: 27.2 us
  starting transfers between devices  13.6 us (50%)
  Pallas kernels  8.36 us (31%)
  waiting for transfers between devices  3.86 us (14%)
  between operations  1.33 us (5%)
    ppermute x10, starting transfers between devices, shift(): lax.ppermute(value, axis, [(i, (i + step) % count) for i in range(count)])  13 us
    pallas_call x7, Pallas kernels, call(): pl.pallas_call(kernel, out_shape=outs, in_specs=specs + [vmem] * (len(arg...  8.36 us
    ppermute x1, waiting for transfers between devices, local(): received = lax.ppermute(share, 'depth', pairs)  2.56 us
    ppermute x10, waiting for transfers between devices, shift(): lax.ppermute(value, axis, [(i, (i + step) % count) for i in range(count)])  1.3 us
    ppermute x1, starting transfers between devices, local(): received = lax.ppermute(share, 'depth', pairs)  0.57 us
  transfers between devices with their start and end apart: 11, of which 6 were waited for; matrix products, arithmetic and copies ran while one was open for 0% of the time, Pallas kernels for 16%

profile of v6, /device:TPU:0, one launch (start us, length us, event | category | flops | bytes accessed | tf_op | source)
XLA Modules:
  0.0 27.2 jit_solution(6967877724078714786)
XLA Ops:
  0.6 1.3 %shard_map.59 = (f32[4,8,16,128]{3,2,1,0:T(8,128)S(1)}, f32[4,8,8,128]{3,2,1,0:T(8,128)S(1)}, f32[4,8,8,128]{3,2,1,0:T(8,128)S(1)}, f32[4,16,128]{2,1,0:T(8,128)...) custom-call(f32[4,16,16,128]{3,2,1,0:T(8,128)} %state_in.1, ...), custom_call_target="tpu_custom_call" | custom-call | tf_op jit(solution)/shard_map/pallas_call | solution.py:565
  2.0 3.0 %collective-permute-start = (f32[4,8,16,128]{3,2,1,0:T(8,128)S(1)}, f32[4,8,16,128]{3,2,1,0:T(8,128)S(1)}, u32[]{:S(2)}, u32[]{:S(2)}) collective-permute-start(f32[4,8,16,128]{3,2,1,0:T(8,128)S(1)} %get-tuple-element.34), channel_id=1, source_target_pairs={{0,16},{16,0},{1,17},{17,1},{2,18},{18,2},{3,19},{19,3},{4,20},{20... | collective-permute-start | bytes 786440 | tf_op jit(solution)/shard_map/ppermute | solution.py:542
  5.0 0.7 %collective-permute-start.1 = (f32[4,8,8,128]{3,2,1,0:T(8,128)S(1)}, f32[4,8,8,128]{3,2,1,0:T(8,128)S(1)}, u32[]{:S(2)}, u32[]{:S(2)}) collective-permute-start(f32[4,8,8,128]{3,2,1,0:T(8,128)S(1)} %get-tuple-element.35), channel_id=1, source_target_pairs={{0,12},{4,0},{8,4},{12,8},{1,13},{5,1},{9,5},{13,9},{2,14},{6,2},{... | collective-permute-start | bytes 393224 | tf_op jit(solution)/shard_map/ppermute | solution.py:542
  5.7 0.0 collective-permute-start.2
  5.7 1.6 %collective-permute-start.3 = (f32[4,16,128]{2,1,0:T(8,128)S(1)}, f32[4,16,128]{2,1,0:T(8,128)S(1)}, u32[]{:S(2)}, u32[]{:S(2)}) collective-permute-start(f32[4,16,128]{2,1,0:T(8,128)S(1)} %get-tuple-element.29.columns_sent), channel_id=1, source_target_pairs={{0,1},{1,2},{2,3},{3,0},{4,5},{5,6},{6,7},{7,4},{8,9},{9,10},{10,1... | collective-permute-start | bytes 98312 | tf_op jit(solution)/shard_map/ppermute | solution.py:542
  7.2 2.2 %collective-permute-start.4 = (f32[4,16,128]{2,1,0:T(8,128)S(1)}, f32[4,16,128]{2,1,0:T(8,128)S(1)}, u32[]{:S(2)}, u32[]{:S(2)}) collective-permute-start(f32[4,16,128]{2,1,0:T(8,128)S(1)} %get-tuple-element.29.columns_sent), channel_id=1, source_target_pairs={{0,3},{1,0},{2,1},{3,2},{4,7},{5,4},{6,5},{7,6},{8,11},{9,8},{10,9... | collective-permute-start | bytes 98312 | tf_op jit(solution)/shard_map/ppermute | solution.py:542
  9.5 1.7 %shard_map.60 = (f32[4,16,16,128]{3,2,1,0:T(8,128)S(1)}, bf16[256,256]{1,0:T(8,128)(2,1)S(1)}, bf16[256,256]{1,0:T(8,128)(2,1)S(1)}, bf16[8,64,64]{2,1,0:T(8,128...) custom-call(f32[4,16,16,128]{3,2,1,0:T(8,128)S(1)} %get-tuple-elemen, ...), custom_call_target="tpu_custom_call" | custom-call | tf_op jit(solution)/shard_map/pallas_call | solution.py:565
  11.2 0.6 %collective-permute-done.3.column_below = f32[4,16,128]{2,1,0:T(8,128)S(1)} collective-permute-done((f32[4,16,128]{2,1,0:T(8,128)S(1)}, f32[4,16,128]{2,1,0:T(8,128)S(1)}, u32[]{:S(2)}, u32[]{:S(2)}) %collective-permute-start.3) | collective-permute-done | bytes 32800 | tf_op jit(solution)/shard_map/ppermute | solution.py:542
  11.8 0.1 collective-permute-done.4.column_above
  11.9 0.0 collective-permute-done.1.row_above
  11.9 0.0 collective-permute-done.2.row_below
  11.9 0.0 collective-permute-done.depth_halo
  11.9 0.7 %shard_map.61 = (f32[4,16,16,128]{3,2,1,0:T(8,128)S(1)}, f32[4,8,16,128]{3,2,1,0:T(8,128)S(1)}, f32[4,8,8,128]{3,2,1,0:T(8,128)S(1)}, f32[4,8,8,128]{3,2,1,0:T(8,128)S(1)}, f32[4,16,128]{2,1,0:T(8,128)S(1)}) custom-call(f32[4,16,16,128]{3,2,1,0:T(8,128)S(1)} %get-tuple-element.30.part, f32[3,16,16,128]{3,2,1,0:T(8,128)S(1)} %get-tuple-element.27.velocity, ...), custom_call_target="tpu_custom_call" | custom-call | tf_op jit(solution)/shard_map/pallas_call | solution.py:565
  12.6 1.2 %collective-permute-start.5 = (f32[4,8,16,128]{3,2,1,0:T(8,128)S(1)}, f32[4,8,16,128]{3,2,1,0:T(8,128)S(1)}, u32[]{:S(2)}, u32[]{:S(2)}) collective-permute-start(f32[4,8,16,128]{3,2,1,0:T(8,128)S(1)} %get-tuple-element.41), channel_id=1, source_target_pairs={{0,16},{16,0},{1,17},{17,1},{2,18},{18,2},{3,19},{19,3},{4,20},{20... | collective-permute-start | bytes 786440 | tf_op jit(solution)/shard_map/ppermute | solution.py:542
  13.8 0.0 collective-permute-start.6
  13.8 0.5 %collective-permute-start.7 = (f32[4,8,8,128]{3,2,1,0:T(8,128)S(1)}, f32[4,8,8,128]{3,2,1,0:T(8,128)S(1)}, u32[]{:S(2)}, u32[]{:S(2)}) collective-permute-start(f32[4,8,8,128]{3,2,1,0:T(8,128)S(1)} %get-tuple-element.43), channel_id=1, source_target_pairs={{0,4},{4,8},{8,12},{12,0},{1,5},{5,9},{9,13},{13,1},{2,6},{6,10},{... | collective-permute-start | bytes 393224 | tf_op jit(solution)/shard_map/ppermute | solution.py:542
  14.3 1.6 %collective-permute-start.8 = (f32[4,16,128]{2,1,0:T(8,128)S(1)}, f32[4,16,128]{2,1,0:T(8,128)S(1)}, u32[]{:S(2)}, u32[]{:S(2)}) collective-permute-start(f32[4,16,128]{2,1,0:T(8,128)S(1)} %get-tuple-element.40.columns_sent), channel_id=1, source_target_pairs={{0,1},{1,2},{2,3},{3,0},{4,5},{5,6},{6,7},{7,4},{8,9},{9,10},{10,1... | collective-permute-start | bytes 98312 | tf_op jit(solution)/shard_map/ppermute | solution.py:542
  15.9 2.2 %collective-permute-start.9 = (f32[4,16,128]{2,1,0:T(8,128)S(1)}, f32[4,16,128]{2,1,0:T(8,128)S(1)}, u32[]{:S(2)}, u32[]{:S(2)}) collective-permute-start(f32[4,16,128]{2,1,0:T(8,128)S(1)} %get-tuple-element.40.columns_sent), channel_id=1, source_target_pairs={{0,3},{1,0},{2,1},{3,2},{4,7},{5,4},{6,5},{7,6},{8,11},{9,8},{10,9... | collective-permute-start | bytes 98312 | tf_op jit(solution)/shard_map/ppermute | solution.py:542
  18.8 1.4 %shard_map.62.part = f32[4,16,16,128]{3,2,1,0:T(8,128)S(1)} custom-call(f32[4,16,16,128]{3,2,1,0:T(8,128)S(1)} %get-tuple-element.38.middle, f32[4,16,16,128]{3,2,1,0:T(8,128)S(1)} %get-tuple-element.26.state, f32[3,16,16,128]{3,2,1,0:T(8,128)S(1)} %get-tuple-element.27.velocity, bf16[256,256]{1,0:T(8,128)(2,1)S(1)} %get-tuple-element.39.inner_weight, ...), custom_call_target="tpu_custom_call" | custom-call | tf_op jit(solution)/shard_map/pallas_call | solution.py:565
  20.2 0.1 collective-permute-done.8.column_below
  20.3 0.4 %collective-permute-done.9.column_above = f32[4,16,128]{2,1,0:T(8,128)S(1)} collective-permute-done((f32[4,16,128]{2,1,0:T(8,128)S(1)}, f32[4,16,128]{2,1,0:T(8,128)S(1)}, u32[]{:S(2)}, u32[]{:S(2)}) %collective-permute-start.9) | collective-permute-done | bytes 32800 | tf_op jit(solution)/shard_map/ppermute | solution.py:542
  20.7 0.0 collective-permute-done.6.row_above
  20.7 0.0 collective-permute-done.7.row_below
  20.7 0.1 collective-permute-done.5.depth_halo
  20.8 1.3 %shard_map.63 = (f32[16,16,128]{2,1,0:T(8,128)S(1)}, f32[4,32,128]{2,1,0:T(8,128)S(1)}, s32[8,128]{1,0:T(8,128)S(1)}) custom-call(s32[1,1]{1,0:T(1,128)S(6)} %copy.6.order, f32[4,16,16,128]{3,2,1,0:T(8,128)S(1)} %shard_map.62.part, f32[3,16,16,128]{3,2,1,0:T(8,128)S(1)} %get-tuple-element.27.velocity, f32[8,8,128]{2,1,0:T(8,128)S(1)} %get-tuple-element.31.low_velocity, ...), custom_call_target="tpu_custom_call" | custom-call | tf_op jit(solution)/shard_map/pallas_call | solution.py:565
  22.1 0.6 %collective-permute-start.10 = (f32[4,32,128]{2,1,0:T(8,128)S(1)}, f32[4,32,128]{2,1,0:T(8,128)S(1)}, u32[]{:S(2)}, u32[]{:S(2)}) collective-permute-start(f32[4,32,128]{2,1,0:T(8,128)S(1)} %get-tuple-element.48.share.own), channel_id=1, source_target_pairs={{0,16},{16,0},{1,17},{17,1},{2,18},{18,2},{3,19},{19,3},{4,20},{20... | collective-permute-start | bytes 196616 | tf_op jit(solution)/shard_map/ppermute | solution.py:690
  22.6 1.2 %shard_map.64 = f32[4,16,16,128]{3,2,1,0:T(8,128)} custom-call(f32[4,16,16,128]{3,2,1,0:T(8,128)S(1)} %shard_map.62.part, f32[16,16,128]{2,1,0:T(8,128)S(1)} %get-tuple-element.47.temperature, f32[3,16,16,128]{3,2,1,0:T(8,128)S(1)} %get-tuple-element.27.velocity, f32[8,8,128]{2,1,0:T(8,128)S(1)} %get-tuple-element.31.low_velocity, ...), custom_call_target="tpu_custom_call" | custom-call | tf_op jit(solution)/shard_map/pallas_call | solution.py:565
  23.8 2.6 %collective-permute-done.10.received = f32[4,32,128]{2,1,0:T(8,128)S(1)} collective-permute-done((f32[4,32,128]{2,1,0:T(8,128)S(1)}, f32[4,32,128]{2,1,0:T(8,128)S(1)}, u32[]{:S(2)}, u32[]{:S(2)}) %collective-permute-start.10) | collective-permute-done | bytes 65568 | tf_op jit(solution)/shard_map/ppermute | solution.py:690
  26.4 0.8 %shard_map.65 = f32[4,64,64]{2,1,0:T(8,128)} custom-call(s32[8,128]{1,0:T(8,128)S(1)} %get-tuple-element.49.toward, f32[4,32,128]{2,1,0:T(8,128)S(1)} %get-tuple-element.48.share.own, f32[4,32,128]{2,1,0:T(8,128)S(1)} %collective-permute-done.10.received), custom_call_target="tpu_custom_call" | custom-call | tf_op jit(solution)/shard_map/pallas_call | solution.py:565
Async XLA Ops:
  2.0 9.9 %collective-permute-start = (f32[4,8,16,128]{3,2,1,0:T(8,128)S(1)}, f32[4,8,16,128]{3,2,1,0:T(8,128)S(1)}, u32[]{:S(2)}, u32[]{:S(2)}) collective-permute-start(f32[4,8,16,128]{3,2,1,0:T(8,128)S(1)} %get-tuple-element.34), channel_id=1, source_target_pairs={{0,16},{16,0},{1,17},{17,1},{2,18},{18,2},{3,19},{19,3},{4,20},{20... | collective-permute-start | bytes 786440 | tf_op jit(solution)/shard_map/ppermute | solution.py:542
  5.0 6.9 %collective-permute-start.1 = (f32[4,8,8,128]{3,2,1,0:T(8,128)S(1)}, f32[4,8,8,128]{3,2,1,0:T(8,128)S(1)}, u32[]{:S(2)}, u32[]{:S(2)}) collective-permute-start(f32[4,8,8,128]{3,2,1,0:T(8,128)S(1)} %get-tuple-element.35), channel_id=1, source_target_pairs={{0,12},{4,0},{8,4},{12,8},{1,13},{5,1},{9,5},{13,9},{2,14},{6,2},{... | collective-permute-start | bytes 393224 | tf_op jit(solution)/shard_map/ppermute | solution.py:542
  5.7 6.3 %collective-permute-start.2 = (f32[4,8,8,128]{3,2,1,0:T(8,128)S(1)}, f32[4,8,8,128]{3,2,1,0:T(8,128)S(1)}, u32[]{:S(2)}, u32[]{:S(2)}) collective-permute-start(f32[4,8,8,128]{3,2,1,0:T(8,128)S(1)} %get-tuple-element.36), channel_id=1, source_target_pairs={{0,4},{4,8},{8,12},{12,0},{1,5},{5,9},{9,13},{13,1},{2,6},{6,10},{... | collective-permute-start | bytes 393224 | tf_op jit(solution)/shard_map/ppermute | solution.py:542
  5.7 6.1 %collective-permute-start.3 = (f32[4,16,128]{2,1,0:T(8,128)S(1)}, f32[4,16,128]{2,1,0:T(8,128)S(1)}, u32[]{:S(2)}, u32[]{:S(2)}) collective-permute-start(f32[4,16,128]{2,1,0:T(8,128)S(1)} %get-tuple-element.29.columns_sent), channel_id=1, source_target_pairs={{0,1},{1,2},{2,3},{3,0},{4,5},{5,6},{6,7},{7,4},{8,9},{9,10},{10,1... | collective-permute-start | bytes 98312 | tf_op jit(solution)/shard_map/ppermute | solution.py:542
  7.2 4.7 %collective-permute-start.4 = (f32[4,16,128]{2,1,0:T(8,128)S(1)}, f32[4,16,128]{2,1,0:T(8,128)S(1)}, u32[]{:S(2)}, u32[]{:S(2)}) collective-permute-start(f32[4,16,128]{2,1,0:T(8,128)S(1)} %get-tuple-element.29.columns_sent), channel_id=1, source_target_pairs={{0,3},{1,0},{2,1},{3,2},{4,7},{5,4},{6,5},{7,6},{8,11},{9,8},{10,9... | collective-permute-start | bytes 98312 | tf_op jit(solution)/shard_map/ppermute | solution.py:542
  12.6 8.2 %collective-permute-start.5 = (f32[4,8,16,128]{3,2,1,0:T(8,128)S(1)}, f32[4,8,16,128]{3,2,1,0:T(8,128)S(1)}, u32[]{:S(2)}, u32[]{:S(2)}) collective-permute-start(f32[4,8,16,128]{3,2,1,0:T(8,128)S(1)} %get-tuple-element.41), channel_id=1, source_target_pairs={{0,16},{16,0},{1,17},{17,1},{2,18},{18,2},{3,19},{19,3},{4,20},{20... | collective-permute-start | bytes 786440 | tf_op jit(solution)/shard_map/ppermute | solution.py:542
  13.8 6.9 %collective-permute-start.6 = (f32[4,8,8,128]{3,2,1,0:T(8,128)S(1)}, f32[4,8,8,128]{3,2,1,0:T(8,128)S(1)}, u32[]{:S(2)}, u32[]{:S(2)}) collective-permute-start(f32[4,8,8,128]{3,2,1,0:T(8,128)S(1)} %get-tuple-element.42), channel_id=1, source_target_pairs={{0,12},{4,0},{8,4},{12,8},{1,13},{5,1},{9,5},{13,9},{2,14},{6,2},{... | collective-permute-start | bytes 393224 | tf_op jit(solution)/shard_map/ppermute | solution.py:542
  13.8 6.9 %collective-permute-start.7 = (f32[4,8,8,128]{3,2,1,0:T(8,128)S(1)}, f32[4,8,8,128]{3,2,1,0:T(8,128)S(1)}, u32[]{:S(2)}, u32[]{:S(2)}) collective-permute-start(f32[4,8,8,128]{3,2,1,0:T(8,128)S(1)} %get-tuple-element.43), channel_id=1, source_target_pairs={{0,4},{4,8},{8,12},{12,0},{1,5},{5,9},{9,13},{13,1},{2,6},{6,10},{... | collective-permute-start | bytes 393224 | tf_op jit(solution)/shard_map/ppermute | solution.py:542
  14.3 6.0 %collective-permute-start.8 = (f32[4,16,128]{2,1,0:T(8,128)S(1)}, f32[4,16,128]{2,1,0:T(8,128)S(1)}, u32[]{:S(2)}, u32[]{:S(2)}) collective-permute-start(f32[4,16,128]{2,1,0:T(8,128)S(1)} %get-tuple-element.40.columns_sent), channel_id=1, source_target_pairs={{0,1},{1,2},{2,3},{3,0},{4,5},{5,6},{6,7},{7,4},{8,9},{9,10},{10,1... | collective-permute-start | bytes 98312 | tf_op jit(solution)/shard_map/ppermute | solution.py:542
  15.9 4.8 %collective-permute-start.9 = (f32[4,16,128]{2,1,0:T(8,128)S(1)}, f32[4,16,128]{2,1,0:T(8,128)S(1)}, u32[]{:S(2)}, u32[]{:S(2)}) collective-permute-start(f32[4,16,128]{2,1,0:T(8,128)S(1)} %get-tuple-element.40.columns_sent), channel_id=1, source_target_pairs={{0,3},{1,0},{2,1},{3,2},{4,7},{5,4},{6,5},{7,6},{8,11},{9,8},{10,9... | collective-permute-start | bytes 98312 | tf_op jit(solution)/shard_map/ppermute | solution.py:542
  22.1 4.3 %collective-permute-start.10 = (f32[4,32,128]{2,1,0:T(8,128)S(1)}, f32[4,32,128]{2,1,0:T(8,128)S(1)}, u32[]{:S(2)}, u32[]{:S(2)}) collective-permute-start(f32[4,32,128]{2,1,0:T(8,128)S(1)} %get-tuple-element.48.share.own), channel_id=1, source_target_pairs={{0,16},{16,0},{1,17},{17,1},{2,18},{18,2},{3,19},{19,3},{4,20},{20... | collective-permute-start | bytes 196616 | tf_op jit(solution)/shard_map/ppermute | solution.py:690
